TPU v7x, 32 devices: a whole 2x2x4 slice. The times are simulated.
32 devices in a mesh: dp: 16 (over z, y, core), section: 2 (over x).
Axes of the slice: x: 2, y: 2, z: 4, core: 2. Of those that a mesh axis runs over, the one named last changes fastest.
Arguments:
- tokens: bfloat16 [16, 1024, 768], P('dp'), may hold values from -6 to 6
- cotangent: bfloat16 [16, 1024, 768], P('dp'), may hold values from -6 to 6
- norm_gains: bfloat16 [2, 2, 768], P('section'), may hold values from 0.5 to 1.5
- norm_shifts: bfloat16 [2, 2, 768], P('section'), may hold values from -1.75 to 1.75
- in_weight: bfloat16 [2, 768, 2304], P('section'), may hold values from -0.21875 to 0.21875
- in_bias: bfloat16 [2, 3, 768], P('section'), may hold values from -1.75 to 1.75
- short_taps: bfloat16 [2, 3, 3, 768], P('section'), may hold values from -3.5 to 3.5
- long_filter: bfloat16 [2, 2, 1024, 768], P('section'), may hold values from -1.1 to 1.1
- skip_gains: bfloat16 [2, 2, 768], P('section'), may hold values from -3 to 3
- out_weight: bfloat16 [2, 768, 768], P('section'), may hold values from -0.21875 to 0.21875
- out_bias: bfloat16 [2, 768], P('section'), may hold values from -1.75 to 1.75
- up_weight: bfloat16 [2, 768, 3072], P('section'), may hold values from -0.21875 to 0.21875
- up_bias: bfloat16 [2, 3072], P('section'), may hold values from -1.75 to 1.75
- down_weight: bfloat16 [2, 3072, 768], P('section'), may hold values from -0.109375 to 0.109375
- down_bias: bfloat16 [2, 768], P('section'), may hold values from -1.75 to 1.75
Outputs:
- stream_out: bfloat16 [16, 1024, 768], P('dp', 'section')
- grad_tokens: float32 [16, 1024, 768], P('dp', 'section')
- grad_norm_gains: float32 [2, 2, 768], P('section', None, 'dp')
- grad_norm_shifts: float32 [2, 2, 768], P('section', None, 'dp')
- grad_in_weight: float32 [2, 768, 2304], P('section', 'dp')
- grad_in_bias: float32 [2, 3, 768], P('section', None, 'dp')
- grad_short_taps: float32 [2, 3, 3, 768], P('section', None, None, 'dp')
- grad_long_filter: float32 [2, 2, 1024, 768], P('section', None, 'dp')
- grad_skip_gains: float32 [2, 2, 768], P('section', None, 'dp')
- grad_out_weight: float32 [2, 768, 768], P('section', 'dp')
- grad_out_bias: float32 [2, 768], P('section', 'dp')
- grad_up_weight: float32 [2, 768, 3072], P('section', 'dp')
- grad_up_bias: float32 [2, 3072], P('section', 'dp')
- grad_down_weight: float32 [2, 3072, 768], P('section', None, 'dp')
- grad_down_bias: float32 [2, 768], P('section', 'dp')
All inputs are finite; a program needn't handle non-finite values.
Results may differ from a plain program's by a relative error of at most 0.025.
Values may be sent and summed in bfloat16 or wider, within the bound.
A program may use at most 576 MiB of HBM per device.

v0:
```python
import math

import jax
import jax.numpy as jnp
from jax import lax
from jax.sharding import PartitionSpec as P

BLOCK = 256


eps = 1e-05
highest = lax.Precision.HIGHEST


def shifted(block, axis, distance):
    devices = range(lax.axis_size(axis))
    route = [(i - distance, i) for i in devices if i - distance in devices]
    return lax.ppermute(block, axis, route)


def norm_affine(rows, gain_row, shift_row):
    average = jnp.mean(rows, axis=-1, keepdims=True)
    centered = rows - average
    variance = jnp.mean(centered * centered, axis=-1, keepdims=True)
    return centered * lax.rsqrt(variance + eps) * gain_row + shift_row


def gelu_exact(rows):
    return jax.nn.gelu(rows, approximate=False)


def dot_rows(first_op, second_op):
    return lax.dot_general(
        first_op, second_op, (((0,), (0,)), ((), ())), preferred_element_type=jnp.float32
    )


def dot_cols(first_op, second_op):
    return lax.dot_general(
        first_op, second_op, (((1,), (1,)), ((), ())), preferred_element_type=jnp.float32
    )


def precise(table, data):
    return jnp.dot(table, data, precision=highest, preferred_element_type=jnp.float32)


def precise_back(table, data):
    return lax.dot_general(
        table, data, (((0,), (0,)), ((), ())), precision=highest, preferred_element_type=jnp.float32
    )


def wave_tables(piece_rows):
    points = 2 * piece_rows
    freq_index = lax.broadcasted_iota(jnp.int32, (points, points), 0)
    place_index = lax.broadcasted_iota(jnp.int32, (points, points), 1)
    angle = (freq_index * place_index % points).astype(jnp.float32) * (2.0 * math.pi / points)
    return (jnp.cos(angle), jnp.sin(angle))


def place_rows(buffer, rows, offset, active):
    previous = lax.dynamic_slice_in_dim(buffer, offset, rows.shape[0], 0)
    return lax.dynamic_update_slice_in_dim(buffer, jnp.where(active, rows, previous), offset, 0)


def filter_spectrum(response, cosine, sine, piece_rows):
    features = response.shape[1]
    pieces = response.shape[0] // piece_rows
    padded = jnp.concatenate([jnp.zeros((piece_rows, features), jnp.float32), response], axis=0)
    padded = padded.reshape(pieces + 1, piece_rows, features)
    windows = jnp.concatenate([padded[:-1], padded[1:]], axis=1)
    real_part = jnp.einsum("fn,knd->kfd", cosine, windows, precision=highest)
    imag_part = -jnp.einsum("fn,knd->kfd", sine, windows, precision=highest)
    leading = jnp.zeros((pieces - 1,) + real_part.shape[1:], jnp.float32)
    return (jnp.concatenate([leading, real_part], 0), jnp.concatenate([leading, imag_part], 0))


def body(
    tokens,
    cotangent,
    norm_gains,
    norm_shifts,
    in_weight,
    in_bias,
    short_taps,
    long_filter,
    skip_gains,
    out_weight,
    out_bias,
    up_weight,
    up_bias,
    down_weight,
    down_bias,
):
    section_count = lax.axis_size("section")
    section_rank = lax.axis_index("section")
    total_rows = tokens.shape[1]
    features = tokens.shape[2]
    piece_rows = BLOCK
    pieces = total_rows // piece_rows
    steps_total = pieces + section_count - 1
    points = 2 * piece_rows
    cosine, sine = wave_tables(piece_rows)
    cosine_head, sine_head = (cosine[:, :piece_rows], sine[:, :piece_rows])
    cosine_tail, sine_tail = (cosine[:, piece_rows:], sine[:, piece_rows:])
    gain_rows = norm_gains[0].astype(jnp.float32)
    shift_rows = norm_shifts[0].astype(jnp.float32)
    weight_in = in_weight[0]
    bias_in = in_bias[0].astype(jnp.float32).reshape(-1)
    taps_flat = short_taps[0].astype(jnp.float32).reshape(3, -1)
    skip_rows = skip_gains[0].astype(jnp.float32)
    weight_out = out_weight[0]
    bias_out = out_bias[0].astype(jnp.float32)
    weight_up = up_weight[0]
    bias_up = up_bias[0].astype(jnp.float32)
    weight_down = down_weight[0]
    bias_down = down_bias[0].astype(jnp.float32)
    hidden_units = weight_up.shape[1]
    responses = long_filter[0].astype(jnp.float32)
    kernel_one = filter_spectrum(responses[0], cosine, sine, piece_rows)
    kernel_two = filter_spectrum(responses[1], cosine, sine, piece_rows)
    token_rows = tokens[0]
    cot_rows = cotangent[0]

    def inverse_tail(sum_real, sum_imag):
        return (precise_back(cosine_tail, sum_real) - precise_back(sine_tail, sum_imag)) / points

    def inverse_head(sum_real, sum_imag):
        return (precise_back(cosine_head, sum_real) - precise_back(sine_head, sum_imag)) / points

    def store_input(spectra, rows, segment, active):
        real_part = precise(cosine_head, rows)
        imag_part = -precise(sine_head, rows)
        slot = pieces - 1 - segment
        return (
            place_rows(spectra[0], real_part[None], slot, active),
            place_rows(spectra[1], imag_part[None], slot, active),
        )

    def tail_spectrum(rows):
        return (precise(cosine_tail, rows), -precise(sine_tail, rows))

    def store_grad(spectra, tail_pair, segment, active):
        return (
            place_rows(spectra[0], tail_pair[0][None], segment, active),
            place_rows(spectra[1], tail_pair[1][None], segment, active),
        )

    def conv_forward(kernel, spectra, segment):
        kernel_real = lax.dynamic_slice_in_dim(kernel[0], segment, pieces, 0)
        kernel_imag = lax.dynamic_slice_in_dim(kernel[1], segment, pieces, 0)
        sum_real = jnp.sum(kernel_real * spectra[0] - kernel_imag * spectra[1], axis=0)
        sum_imag = jnp.sum(kernel_real * spectra[1] + kernel_imag * spectra[0], axis=0)
        return inverse_tail(sum_real, sum_imag)

    def conv_back(kernel, spectra, segment):
        offset = pieces - 1 - segment
        kernel_real = lax.dynamic_slice_in_dim(kernel[0], offset, pieces, 0)
        kernel_imag = lax.dynamic_slice_in_dim(kernel[1], offset, pieces, 0)
        sum_real = jnp.sum(kernel_real * spectra[0] + kernel_imag * spectra[1], axis=0)
        sum_imag = jnp.sum(kernel_real * spectra[1] - kernel_imag * spectra[0], axis=0)
        return inverse_head(sum_real, sum_imag)

    def add_filter(totals, tail_pair, input_spectra, segment, weight_on):
        prod_real = (tail_pair[0] * input_spectra[0] + tail_pair[1] * input_spectra[1]) * weight_on
        prod_imag = (tail_pair[1] * input_spectra[0] - tail_pair[0] * input_spectra[1]) * weight_on
        real_now = lax.dynamic_slice_in_dim(totals[0], segment, pieces, 0) + prod_real
        imag_now = lax.dynamic_slice_in_dim(totals[1], segment, pieces, 0) + prod_imag
        return (
            lax.dynamic_update_slice_in_dim(totals[0], real_now, segment, 0),
            lax.dynamic_update_slice_in_dim(totals[1], imag_now, segment, 0),
        )

    def filter_grad(totals):
        tail_real = totals[0][pieces - 1 :]
        tail_imag = totals[1][pieces - 1 :]
        rows_all = (
            jnp.einsum("fn,kfd->knd", cosine, tail_real, precision=highest)
            - jnp.einsum("fn,kfd->knd", sine, tail_imag, precision=highest)
        ) / points
        upper = rows_all[:, piece_rows:]
        lower = jnp.concatenate(
            [rows_all[1:, :piece_rows], jnp.zeros((1, piece_rows, features), jnp.float32)], 0
        )
        return (upper + lower).reshape(pieces * piece_rows, features)

    def mixer(window, spec_one, spec_two, segment, active, store):
        short_filter_apply = (
            taps_flat[0] * window[2:] + taps_flat[1] * window[1:-1] + taps_flat[2] * window[:-2]
        )
        relay_state, gate_leading, gate_trailing = jnp.split(short_filter_apply, 3, axis=1)
        input_leading = relay_state * gate_leading
        if store:
            spec_one = store_input(spec_one, input_leading, segment, active)
        leading_section = conv_forward(kernel_one, spec_one, segment) + skip_rows[0] * input_leading
        input_trailing = leading_section * gate_trailing
        if store:
            spec_two = store_input(spec_two, input_trailing, segment, active)
        trailing_section = (
            conv_forward(kernel_two, spec_two, segment) + skip_rows[1] * input_trailing
        )
        values = (
            relay_state,
            gate_leading,
            gate_trailing,
            input_leading,
            leading_section,
            input_trailing,
            trailing_section,
        )
        return (values, spec_one, spec_two)

    spectrum_zero = jnp.zeros((pieces, points, features), jnp.float32)
    padded_zero = jnp.zeros((2 * pieces - 1, points, features), jnp.float32)

    def forward_step(moment, loop_state):
        arrived, proj_rows, input_rows, spec_one, spec_two, output_rows = loop_state
        segment_raw = moment - section_rank
        active = (segment_raw >= 0) & (segment_raw < pieces)
        segment = jnp.clip(segment_raw, 0, pieces - 1)
        offset = segment * piece_rows
        fresh = lax.dynamic_slice_in_dim(token_rows, offset, piece_rows, 0)
        incoming = jnp.where(section_rank == 0, fresh, arrived)
        input_rows = place_rows(input_rows, incoming, offset, active)
        residual_in = incoming.astype(jnp.float32)
        normed = norm_affine(residual_in, gain_rows[0], shift_rows[0]).astype(jnp.bfloat16)
        projected = jnp.dot(normed, weight_in, preferred_element_type=jnp.float32) + bias_in
        proj_rows = place_rows(proj_rows, projected, offset + 2, active)
        window = lax.dynamic_slice_in_dim(proj_rows, offset, piece_rows + 2, 0)
        values, spec_one, spec_two = mixer(window, spec_one, spec_two, segment, active, True)
        branch = (
            jnp.dot(values[6].astype(jnp.bfloat16), weight_out, preferred_element_type=jnp.float32)
            + bias_out
        )
        residual_mid = residual_in + branch
        normed_two = norm_affine(residual_mid, gain_rows[1], shift_rows[1]).astype(jnp.bfloat16)
        hidden = jnp.dot(normed_two, weight_up, preferred_element_type=jnp.float32) + bias_up
        activation = gelu_exact(hidden).astype(jnp.bfloat16)
        result = (
            residual_mid
            + jnp.dot(activation, weight_down, preferred_element_type=jnp.float32)
            + bias_down
        )
        outgoing = result.astype(jnp.bfloat16)
        output_rows = place_rows(output_rows, outgoing, offset, active)
        arrived = shifted(outgoing, "section", 1)
        return (arrived, proj_rows, input_rows, spec_one, spec_two, output_rows)

    forward_start = (
        jnp.zeros((piece_rows, features), jnp.bfloat16),
        jnp.zeros((total_rows + 2, 3 * features), jnp.float32),
        jnp.zeros((total_rows, features), jnp.bfloat16),
        (spectrum_zero, spectrum_zero),
        (spectrum_zero, spectrum_zero),
        jnp.zeros((total_rows, features), jnp.bfloat16),
    )
    arrived_end, proj_rows, input_rows, spec_one, spec_two, output_rows = lax.fori_loop(
        0, steps_total, forward_step, forward_start
    )
    terms_start = jnp.zeros((features, 4 * features + 2 * hidden_units), jnp.float32)
    small_start = (
        jnp.zeros((2, features), jnp.float32),
        jnp.zeros((2, features), jnp.float32),
        jnp.zeros((3 * features,), jnp.float32),
        jnp.zeros((3, 3 * features), jnp.float32),
        jnp.zeros((2, features), jnp.float32),
        jnp.zeros((features,), jnp.float32),
        jnp.zeros((hidden_units,), jnp.float32),
        jnp.zeros((features,), jnp.float32),
    )

    def backward_step(moment, loop_state):
        (
            arrived,
            grad_mixed_rows,
            grads_one,
            grads_two,
            filter_one,
            filter_two,
            small,
            terms,
            grad_rows,
        ) = loop_state
        segment_raw = pieces - 1 - moment + (section_count - 1 - section_rank)
        active = (segment_raw >= 0) & (segment_raw < pieces)
        weight_on = active.astype(jnp.float32)
        segment = jnp.clip(segment_raw, 0, pieces - 1)
        offset = segment * piece_rows
        fresh = lax.dynamic_slice_in_dim(cot_rows, offset, piece_rows, 0)
        grad_out = jnp.where(section_rank == section_count - 1, fresh, arrived).astype(jnp.float32)
        residual_in = lax.dynamic_slice_in_dim(input_rows, offset, piece_rows, 0).astype(
            jnp.float32
        )
        normed_full, norm_pull = jax.vjp(norm_affine, residual_in, gain_rows[0], shift_rows[0])
        normed = normed_full.astype(jnp.bfloat16)
        window = lax.dynamic_slice_in_dim(proj_rows, offset, piece_rows + 2, 0)
        values = mixer(window, spec_one, spec_two, segment, active, False)[0]
        (
            relay_state,
            gate_leading,
            gate_trailing,
            input_leading,
            leading_section,
            input_trailing,
            trailing_section,
        ) = values
        low_two = trailing_section.astype(jnp.bfloat16)
        residual_mid = (
            residual_in
            + jnp.dot(low_two, weight_out, preferred_element_type=jnp.float32)
            + bias_out
        )
        normed_two_full, second_pull = jax.vjp(
            norm_affine, residual_mid, gain_rows[1], shift_rows[1]
        )
        normed_two = normed_two_full.astype(jnp.bfloat16)
        hidden = jnp.dot(normed_two, weight_up, preferred_element_type=jnp.float32) + bias_up
        activation_full, gelu_pull = jax.vjp(gelu_exact, hidden)
        activation = activation_full.astype(jnp.bfloat16)
        down_grad = grad_out.astype(jnp.bfloat16)
        grad_hidden = gelu_pull(dot_cols(down_grad, weight_down))[0]
        up_grad = grad_hidden.astype(jnp.bfloat16)
        grad_mid_norm, grad_gain_two, grad_shift_two = second_pull(dot_cols(up_grad, weight_up))
        grad_mid = grad_out + grad_mid_norm
        out_grad = grad_mid.astype(jnp.bfloat16)
        grad_section_two = dot_cols(out_grad, weight_out)
        tail_two = tail_spectrum(grad_section_two)
        grads_two = store_grad(grads_two, tail_two, segment, active)
        filter_two = add_filter(filter_two, tail_two, spec_two, segment, weight_on)
        grad_second_input = (
            conv_back(kernel_two, grads_two, segment) + skip_rows[1] * grad_section_two
        )
        grad_section_one = grad_second_input * gate_trailing
        gate_trailing_gradient = grad_second_input * leading_section
        tail_one = tail_spectrum(grad_section_one)
        grads_one = store_grad(grads_one, tail_one, segment, active)
        filter_one = add_filter(filter_one, tail_one, spec_one, segment, weight_on)
        input_leading_gradient = (
            conv_back(kernel_one, grads_one, segment) + skip_rows[0] * grad_section_one
        )
        relay_state_gradient = input_leading_gradient * gate_leading
        gate_leading_gradient = input_leading_gradient * relay_state
        short_filter_gradient = jnp.concatenate(
            [relay_state_gradient, gate_leading_gradient, gate_trailing_gradient], axis=1
        )
        grad_mixed_rows = place_rows(grad_mixed_rows, short_filter_gradient, offset, active)
        grad_window = lax.dynamic_slice_in_dim(grad_mixed_rows, offset, piece_rows + 2, 0)
        grad_proj = (
            taps_flat[0] * grad_window[:-2]
            + taps_flat[1] * grad_window[1:-1]
            + taps_flat[2] * grad_window[2:]
        )
        proj_grad = grad_proj.astype(jnp.bfloat16)
        grad_in_norm, grad_gain_one, grad_shift_one = norm_pull(dot_cols(proj_grad, weight_in))
        grad_input = grad_mid + grad_in_norm
        grad_rows = place_rows(grad_rows, grad_input, offset, active)
        arrived = shifted(grad_input.astype(jnp.bfloat16), "section", -1)
        updates = (
            jnp.stack([grad_gain_one, grad_gain_two]),
            jnp.stack([grad_shift_one, grad_shift_two]),
            jnp.sum(proj_grad.astype(jnp.float32), axis=0),
            jnp.stack(
                [
                    jnp.sum(short_filter_gradient * window[2:], axis=0),
                    jnp.sum(short_filter_gradient * window[1:-1], axis=0),
                    jnp.sum(short_filter_gradient * window[:-2], axis=0),
                ]
            ),
            jnp.stack(
                [
                    jnp.sum(grad_section_one * input_leading, axis=0),
                    jnp.sum(grad_section_two * input_trailing, axis=0),
                ]
            ),
            jnp.sum(out_grad.astype(jnp.float32), axis=0),
            jnp.sum(up_grad.astype(jnp.float32), axis=0),
            jnp.sum(down_grad.astype(jnp.float32), axis=0),
        )
        small = tuple(
            (running + weight_on * fresh_term for running, fresh_term in zip(small, updates))
        )
        products = jnp.concatenate(
            [
                dot_rows(normed, proj_grad),
                dot_rows(low_two, out_grad),
                dot_rows(normed_two, up_grad),
                dot_rows(down_grad, activation),
            ],
            axis=1,
        )
        terms = terms + weight_on * products
        return (
            arrived,
            grad_mixed_rows,
            grads_one,
            grads_two,
            filter_one,
            filter_two,
            small,
            terms,
            grad_rows,
        )

    backward_start = (
        jnp.zeros((piece_rows, features), jnp.bfloat16),
        jnp.zeros((total_rows + 2, 3 * features), jnp.float32),
        (spectrum_zero, spectrum_zero),
        (spectrum_zero, spectrum_zero),
        (padded_zero, padded_zero),
        (padded_zero, padded_zero),
        small_start,
        terms_start,
        jnp.zeros((total_rows, features), jnp.float32),
    )
    (
        arrived_last,
        grad_mixed_rows,
        grads_one,
        grads_two,
        filter_one,
        filter_two,
        small,
        terms,
        grad_rows,
    ) = lax.fori_loop(0, steps_total, backward_step, backward_start)
    filter_term = jnp.stack([filter_grad(filter_one), filter_grad(filter_two)], axis=1)
    (
        gain_grad,
        shift_grad,
        bias_in_grad,
        taps_grad,
        skip_grad,
        bias_out_grad,
        bias_up_grad,
        bias_down_grad,
    ) = small
    small_term = jnp.concatenate(
        [
            gain_grad,
            shift_grad,
            bias_in_grad.reshape(3, features),
            taps_grad.reshape(9, features),
            skip_grad,
            bias_out_grad[None],
            bias_down_grad[None],
        ],
        axis=0,
    ).T
    up_term = bias_up_grad[:, None]
    slab_part, filter_part, small_part, up_part = (
        lax.psum_scatter(terms.astype(jnp.bfloat16), "dp", scatter_dimension=0, tiled=True).astype(
            jnp.float32
        ),
        lax.psum_scatter(
            filter_term.astype(jnp.bfloat16), "dp", scatter_dimension=0, tiled=True
        ).astype(jnp.float32),
        lax.psum_scatter(
            small_term.astype(jnp.bfloat16), "dp", scatter_dimension=0, tiled=True
        ).astype(jnp.float32),
        lax.psum_scatter(
            up_term.astype(jnp.bfloat16), "dp", scatter_dimension=0, tiled=True
        ).astype(jnp.float32),
    )
    grad_in_weight = slab_part[:, : 3 * features][None]
    grad_out_weight = slab_part[:, 3 * features : 4 * features][None]
    grad_up_weight = slab_part[:, 4 * features : 4 * features + hidden_units][None]
    grad_down_weight = slab_part[:, 4 * features + hidden_units :].T[None]
    grad_long_filter = filter_part.transpose(1, 0, 2)[None]
    small_rows = small_part.T
    grad_gains = small_rows[0:2][None]
    grad_shifts = small_rows[2:4][None]
    grad_in_bias = small_rows[4:7][None]
    grad_taps = small_rows[7:16].reshape(3, 3, -1)[None]
    grad_skips = small_rows[16:18][None]
    grad_out_bias = small_rows[18][None]
    grad_down_bias = small_rows[19][None]
    grad_up_bias = up_part[:, 0][None]
    out_full = jnp.where(section_rank == section_count - 1, output_rows.astype(jnp.float32), 0.0)
    grad_full = jnp.where(section_rank == 0, grad_rows, 0.0)
    out_part, grad_part = (
        lax.psum_scatter(
            out_full.astype(jnp.bfloat16), "section", scatter_dimension=0, tiled=True
        ).astype(jnp.float32),
        lax.psum_scatter(
            grad_full.astype(jnp.bfloat16), "section", scatter_dimension=0, tiled=True
        ).astype(jnp.float32),
    )
    return (
        out_part.astype(jnp.bfloat16)[None],
        grad_part[None],
        grad_gains,
        grad_shifts,
        grad_in_weight,
        grad_in_bias,
        grad_taps,
        grad_long_filter,
        grad_skips,
        grad_out_weight,
        grad_out_bias,
        grad_up_weight,
        grad_up_bias,
        grad_down_weight,
        grad_down_bias,
    )


def solution(mesh):
    placed = (
        P("dp", None, None),
        P("dp", None, None),
        P("section", None, None),
        P("section", None, None),
        P("section", None, None),
        P("section", None, None),
        P("section", None, None, None),
        P("section", None, None, None),
        P("section", None, None),
        P("section", None, None),
        P("section", None),
        P("section", None, None),
        P("section", None),
        P("section", None, None),
        P("section", None),
    )
    return jax.shard_map(
        body,
        mesh=mesh,
        in_specs=placed,
        out_specs=(
            P("dp", "section", None),
            P("dp", "section", None),
            P("section", None, "dp"),
            P("section", None, "dp"),
            P("section", "dp", None),
            P("section", None, "dp"),
            P("section", None, None, "dp"),
            P("section", None, "dp", None),
            P("section", None, "dp"),
            P("section", "dp", None),
            P("section", "dp"),
            P("section", "dp", None),
            P("section", "dp"),
            P("section", None, "dp"),
            P("section", "dp"),
        ),
        check_vma=False,
    )
```

profile of v0, /device:TPU:0, one launch (start us, length us, event | category | flops | bytes accessed | tf_op | source)
XLA Modules:
  0.0 2854.7 jit_solution(3434627207193865753)
XLA Ops:
  32.3 18.8 negate_bitcast_fusion
  51.1 16.2 fusion.151
  73.1 19.5 negate_bitcast_fusion.1
  92.7 16.4 fusion.152
  160.1 576.5 %while.87 = (s32[]{:T(128)}, bf16[256,768]{1,0:T(8,128)(2,1)S(1)}, f32[1026,2304]{1,0:T(8,128)}, bf16[1024,768]{1,0:T(8,128)(2,1)S(1)}, f32[4,512,768]{1,2,0:T(8...) while((s32[]{:T(128)}, bf16[256,768]{1,0:T(8,128)(2,1)S(1)}, ...), condition=%wide.wide.region_9.10_spmd.clone, body=%wide.wide.region_0.9_spmd.clone.sunk | while | flops 13377994752 | bytes 347234816 | solution.py:258
  183.4 12.4 copy.178
  204.9 13.9 dynamic_update_slice.252
  262.4 13.7 select_dynamic-update-slice_fusion.10
  281.2 12.2 copy.180
  296.4 12.4 copy.178
  317.9 13.9 dynamic_update_slice.252
  375.7 13.7 select_dynamic-update-slice_fusion.10
  391.0 12.2 copy.180
  406.2 12.4 copy.178
  427.7 13.9 dynamic_update_slice.252
  485.6 13.8 select_dynamic-update-slice_fusion.10
  500.8 12.2 copy.180
  516.0 12.4 copy.178
  537.5 13.7 dynamic_update_slice.252
  595.0 13.7 select_dynamic-update-slice_fusion.10
  610.2 12.2 copy.180
  625.4 12.4 copy.178
  646.9 13.7 dynamic_update_slice.252
  704.4 13.7 select_dynamic-update-slice_fusion.10
  719.6 12.2 copy.180
  777.1 1674.2 %while.86 = (s32[]{:T(128)}, bf16[256,768]{1,0:T(8,128)(2,1)}, f32[1026,2304]{0,1:T(8,128)}, f32[4,512,768]{1,2,0:T(8,128)}, f32[4,512,768]{1,2,0:T(8,128)}, /*i...) while((s32[]{:T(128)}, bf16[256,768]{1,0:T(8,128)(2,1)}, ...), condition=%wide.region_41.42_spmd.clone.clone, body=%wide.region_11.41_spmd.clone.clone.sunk | while | flops 23472889856 | bytes 1068125248 | solution.py:426
  1003.8 29.0 %multiply_add_fusion.10 = (f32[4,512,768]{1,2,0:T(8,128)}, f32[4,512,768]{1,2,0:T(8,128)}, f32[4,512,768]{1,2,0:T(8,128)}, f32[4,512,768]{1,2,0:T(8,128)}) fusion(f32[4,512,768]{1,2,0:T(8,128)} %copy.170, f32[4,512,768]{1,2,0:T(8,128)} %get-tuple-element.4058, f32[4,512,768]{1,2,0:T(8,128)} %get-tuple-element.4056, f32[512,768]{0,1:T(8,128)} %bitcast.440, ...), kind=kLoop, calls=%fused_computation.122.clone.1 | loop fusion | flops 31457280 | bytes 81788928 | tf_op jit(solution)/shard_map/while/body/eval_jaxpr/add | solution.py:169
  1080.3 19.7 fusion.489
  1189.4 12.1 subtract_reduce_fusion.8
  1330.0 29.0 %multiply_add_fusion.10 = (f32[4,512,768]{1,2,0:T(8,128)}, f32[4,512,768]{1,2,0:T(8,128)}, f32[4,512,768]{1,2,0:T(8,128)}, f32[4,512,768]{1,2,0:T(8,128)}) fusion(f32[4,512,768]{1,2,0:T(8,128)} %copy.170, f32[4,512,768]{1,2,0:T(8,128)} %get-tuple-element.4058, f32[4,512,768]{1,2,0:T(8,128)} %get-tuple-element.4056, f32[512,768]{0,1:T(8,128)} %bitcast.440, ...), kind=kLoop, calls=%fused_computation.122.clone.1 | loop fusion | flops 31457280 | bytes 81788928 | tf_op jit(solution)/shard_map/while/body/eval_jaxpr/add | solution.py:169
  1406.5 27.4 fusion.489
  1523.4 11.9 subtract_reduce_fusion.8
  1664.6 29.0 %multiply_add_fusion.10 = (f32[4,512,768]{1,2,0:T(8,128)}, f32[4,512,768]{1,2,0:T(8,128)}, f32[4,512,768]{1,2,0:T(8,128)}, f32[4,512,768]{1,2,0:T(8,128)}) fusion(f32[4,512,768]{1,2,0:T(8,128)} %copy.170, f32[4,512,768]{1,2,0:T(8,128)} %get-tuple-element.4058, f32[4,512,768]{1,2,0:T(8,128)} %get-tuple-element.4056, f32[512,768]{0,1:T(8,128)} %bitcast.440, ...), kind=kLoop, calls=%fused_computation.122.clone.1 | loop fusion | flops 31457280 | bytes 81788928 | tf_op jit(solution)/shard_map/while/body/eval_jaxpr/add | solution.py:169
  1741.1 27.4 fusion.489
  1858.4 11.8 subtract_reduce_fusion.8
  1999.4 29.0 %multiply_add_fusion.10 = (f32[4,512,768]{1,2,0:T(8,128)}, f32[4,512,768]{1,2,0:T(8,128)}, f32[4,512,768]{1,2,0:T(8,128)}, f32[4,512,768]{1,2,0:T(8,128)}) fusion(f32[4,512,768]{1,2,0:T(8,128)} %copy.170, f32[4,512,768]{1,2,0:T(8,128)} %get-tuple-element.4058, f32[4,512,768]{1,2,0:T(8,128)} %get-tuple-element.4056, f32[512,768]{0,1:T(8,128)} %bitcast.440, ...), kind=kLoop, calls=%fused_computation.122.clone.1 | loop fusion | flops 31457280 | bytes 81788928 | tf_op jit(solution)/shard_map/while/body/eval_jaxpr/add | solution.py:169
  2076.0 27.4 fusion.489
  2334.2 29.0 %multiply_add_fusion.10 = (f32[4,512,768]{1,2,0:T(8,128)}, f32[4,512,768]{1,2,0:T(8,128)}, f32[4,512,768]{1,2,0:T(8,128)}, f32[4,512,768]{1,2,0:T(8,128)}) fusion(f32[4,512,768]{1,2,0:T(8,128)} %copy.170, f32[4,512,768]{1,2,0:T(8,128)} %get-tuple-element.4058, f32[4,512,768]{1,2,0:T(8,128)} %get-tuple-element.4056, f32[512,768]{0,1:T(8,128)} %bitcast.440, ...), kind=kLoop, calls=%fused_computation.122.clone.1 | loop fusion | flops 31457280 | bytes 81788928 | tf_op jit(solution)/shard_map/while/body/eval_jaxpr/add | solution.py:169
  2410.9 27.4 fusion.489
  2461.3 18.5 fusion.162
  2479.9 20.7 multiply_bitcast_fusion.1
  2503.9 15.8 fusion.160
  2519.8 15.9 multiply_bitcast_fusion
  2542.0 15.9 convert_element_type.373
  2576.9 24.4 reduce-scatter.13.cloned.1.call-done
  2603.7 67.5 %reduce-scatter.17.cloned.1.call-done = bf16[64,2,768]{2,0,1:T(8,128)(2,1)} async-done(((bf16[1024,2,768]{2,0,1:T(8,128)(2,1)}), bf16[64,2,768]{2,0,1:T(8,128)(2,1)}) %reduce-scatter.17.cloned.1.call-update) | async-done | bytes 196624 | tf_op jit(solution)/shard_map/reduce_scatter | solution.py:455
  2672.9 146.9 %reduce-scatter.15.cloned.1.call-done = bf16[48,9216]{1,0:T(8,128)(2,1)} async-done(((bf16[768,9216]{1,0:T(8,128)(2,1)}), bf16[48,9216]{1,0:T(8,128)(2,1)}) %reduce-scatter.15.cloned.1.call-update) | async-done | bytes 884752 | tf_op jit(solution)/shard_map/reduce_scatter | solution.py:452
  2823.7 24.0 reduce-scatter.11.cloned.1.call-done
  (2128 shorter events, 1802.8 us)
Async XLA Ops:
  7.2 2553.5 %reduce-scatter.21.cloned.1.call-start = ((), (), s32[]{:S(2)}) async-start(), calls=%async_computation.11 | async-start | bytes 835584
  276.2 17.2 collective-permute-start.1
  389.5 13.7 collective-permute-start.1
  499.4 13.7 collective-permute-start.1
  608.8 13.7 collective-permute-start.1
  718.2 13.7 collective-permute-start.1
  779.7 45.4 %copy-start.70 = (f32[768]{0:T(1024)}, f32[768]{0:T(1024)S(1)}, u32[]{:S(2)}) copy-start(f32[768]{0:T(1024)S(1)} %get-tuple-element.3663) | copy-start | bytes 9220 | tf_op jit(solution)/shard_map/while
  863.1 29.3 %slice-start.13 = ((s8[11010048]{0:T(1024)(128)(4,1)}), s8[4194304]{0:T(1024)(128)(4,1)S(1)}, s32[]{:S(2)}) async-start(s8[11010048]{0:T(1024)(128)(4,1)} %bitcast.429), calls=%async_computation.25 | async-start | bytes 8388608 | tf_op jit(solution)/shard_map/while
  863.1 29.3 %slice-start.14 = ((s8[11010048]{0:T(1024)(128)(4,1)}), s8[4194304]{0:T(1024)(128)(4,1)S(1)}, s32[]{:S(2)}) async-start(s8[11010048]{0:T(1024)(128)(4,1)} %bitcast.429), calls=%async_computation.26 | async-start | bytes 8388608 | tf_op jit(solution)/shard_map/while
  863.1 29.3 %slice-start.16 = ((s8[11010048]{0:T(1024)(128)(4,1)}), s8[4194304]{0:T(1024)(128)(4,1)S(1)}, s32[]{:S(2)}) async-start(s8[11010048]{0:T(1024)(128)(4,1)} %bitcast.431), calls=%async_computation.28 | async-start | bytes 8388608 | tf_op jit(solution)/shard_map/while
  863.2 29.4 %slice-start.17 = ((s8[11010048]{0:T(1024)(128)(4,1)}), s8[4194304]{0:T(1024)(128)(4,1)S(1)}, s32[]{:S(2)}) async-start(s8[11010048]{0:T(1024)(128)(4,1)} %bitcast.431), calls=%async_computation.29 | async-start | bytes 8388608 | tf_op jit(solution)/shard_map/while
  935.8 167.7 %collective-permute-start = (bf16[256,768]{1,0:T(8,128)(2,1)}, bf16[256,768]{1,0:T(8,128)(2,1)}, u32[]{:S(2)}, u32[]{:S(2)}) collective-permute-start(bf16[256,768]{1,0:T(8,128)(2,1)} %get-tuple-element.3698), channel_id=1, source_target_pairs={{1,0},{3,2},{5,4},{7,6},{9,8},{11,10},{13,12},{15,14},{17,16},{19,... | collective-permute-start | bytes 1179656 | tf_op jit(solution)/shard_map/while/body/eval_jaxpr/ppermute | solution.py:18
  1106.2 45.3 %copy-start.70 = (f32[768]{0:T(1024)}, f32[768]{0:T(1024)S(1)}, u32[]{:S(2)}) copy-start(f32[768]{0:T(1024)S(1)} %get-tuple-element.3663) | copy-start | bytes 9220 | tf_op jit(solution)/shard_map/while
  1189.4 29.6 %slice-start.13 = ((s8[11010048]{0:T(1024)(128)(4,1)}), s8[4194304]{0:T(1024)(128)(4,1)S(1)}, s32[]{:S(2)}) async-start(s8[11010048]{0:T(1024)(128)(4,1)} %bitcast.429), calls=%async_computation.25 | async-start | bytes 8388608 | tf_op jit(solution)/shard_map/while
  1189.4 29.6 %slice-start.14 = ((s8[11010048]{0:T(1024)(128)(4,1)}), s8[4194304]{0:T(1024)(128)(4,1)S(1)}, s32[]{:S(2)}) async-start(s8[11010048]{0:T(1024)(128)(4,1)} %bitcast.429), calls=%async_computation.26 | async-start | bytes 8388608 | tf_op jit(solution)/shard_map/while
  1189.4 29.6 %slice-start.16 = ((s8[11010048]{0:T(1024)(128)(4,1)}), s8[4194304]{0:T(1024)(128)(4,1)S(1)}, s32[]{:S(2)}) async-start(s8[11010048]{0:T(1024)(128)(4,1)} %bitcast.431), calls=%async_computation.28 | async-start | bytes 8388608 | tf_op jit(solution)/shard_map/while
  1189.4 29.6 %slice-start.17 = ((s8[11010048]{0:T(1024)(128)(4,1)}), s8[4194304]{0:T(1024)(128)(4,1)S(1)}, s32[]{:S(2)}) async-start(s8[11010048]{0:T(1024)(128)(4,1)} %bitcast.431), calls=%async_computation.29 | async-start | bytes 8388608 | tf_op jit(solution)/shard_map/while
  1262.2 175.2 %collective-permute-start = (bf16[256,768]{1,0:T(8,128)(2,1)}, bf16[256,768]{1,0:T(8,128)(2,1)}, u32[]{:S(2)}, u32[]{:S(2)}) collective-permute-start(bf16[256,768]{1,0:T(8,128)(2,1)} %get-tuple-element.3698), channel_id=1, source_target_pairs={{1,0},{3,2},{5,4},{7,6},{9,8},{11,10},{13,12},{15,14},{17,16},{19,... | collective-permute-start | bytes 1179656 | tf_op jit(solution)/shard_map/while/body/eval_jaxpr/ppermute | solution.py:18
  1406.3 27.7 copy-start.90
  1440.3 45.3 %copy-start.70 = (f32[768]{0:T(1024)}, f32[768]{0:T(1024)S(1)}, u32[]{:S(2)}) copy-start(f32[768]{0:T(1024)S(1)} %get-tuple-element.3663) | copy-start | bytes 9220 | tf_op jit(solution)/shard_map/while
  1523.4 29.4 %slice-start.13 = ((s8[11010048]{0:T(1024)(128)(4,1)}), s8[4194304]{0:T(1024)(128)(4,1)S(1)}, s32[]{:S(2)}) async-start(s8[11010048]{0:T(1024)(128)(4,1)} %bitcast.429), calls=%async_computation.25 | async-start | bytes 8388608 | tf_op jit(solution)/shard_map/while
  1523.4 29.4 %slice-start.14 = ((s8[11010048]{0:T(1024)(128)(4,1)}), s8[4194304]{0:T(1024)(128)(4,1)S(1)}, s32[]{:S(2)}) async-start(s8[11010048]{0:T(1024)(128)(4,1)} %bitcast.429), calls=%async_computation.26 | async-start | bytes 8388608 | tf_op jit(solution)/shard_map/while
  1523.4 29.4 %slice-start.16 = ((s8[11010048]{0:T(1024)(128)(4,1)}), s8[4194304]{0:T(1024)(128)(4,1)S(1)}, s32[]{:S(2)}) async-start(s8[11010048]{0:T(1024)(128)(4,1)} %bitcast.431), calls=%async_computation.28 | async-start | bytes 8388608 | tf_op jit(solution)/shard_map/while
  1523.4 29.4 %slice-start.17 = ((s8[11010048]{0:T(1024)(128)(4,1)}), s8[4194304]{0:T(1024)(128)(4,1)S(1)}, s32[]{:S(2)}) async-start(s8[11010048]{0:T(1024)(128)(4,1)} %bitcast.431), calls=%async_computation.29 | async-start | bytes 8388608 | tf_op jit(solution)/shard_map/while
  1596.7 175.4 %collective-permute-start = (bf16[256,768]{1,0:T(8,128)(2,1)}, bf16[256,768]{1,0:T(8,128)(2,1)}, u32[]{:S(2)}, u32[]{:S(2)}) collective-permute-start(bf16[256,768]{1,0:T(8,128)(2,1)} %get-tuple-element.3698), channel_id=1, source_target_pairs={{1,0},{3,2},{5,4},{7,6},{9,8},{11,10},{13,12},{15,14},{17,16},{19,... | collective-permute-start | bytes 1179656 | tf_op jit(solution)/shard_map/while/body/eval_jaxpr/ppermute | solution.py:18
  1740.9 27.7 copy-start.90
  1774.8 45.5 %copy-start.70 = (f32[768]{0:T(1024)}, f32[768]{0:T(1024)S(1)}, u32[]{:S(2)}) copy-start(f32[768]{0:T(1024)S(1)} %get-tuple-element.3663) | copy-start | bytes 9220 | tf_op jit(solution)/shard_map/while
  1858.4 29.4 %slice-start.13 = ((s8[11010048]{0:T(1024)(128)(4,1)}), s8[4194304]{0:T(1024)(128)(4,1)S(1)}, s32[]{:S(2)}) async-start(s8[11010048]{0:T(1024)(128)(4,1)} %bitcast.429), calls=%async_computation.25 | async-start | bytes 8388608 | tf_op jit(solution)/shard_map/while
  1858.4 29.4 %slice-start.14 = ((s8[11010048]{0:T(1024)(128)(4,1)}), s8[4194304]{0:T(1024)(128)(4,1)S(1)}, s32[]{:S(2)}) async-start(s8[11010048]{0:T(1024)(128)(4,1)} %bitcast.429), calls=%async_computation.26 | async-start | bytes 8388608 | tf_op jit(solution)/shard_map/while
  1858.4 29.4 %slice-start.16 = ((s8[11010048]{0:T(1024)(128)(4,1)}), s8[4194304]{0:T(1024)(128)(4,1)S(1)}, s32[]{:S(2)}) async-start(s8[11010048]{0:T(1024)(128)(4,1)} %bitcast.431), calls=%async_computation.28 | async-start | bytes 8388608 | tf_op jit(solution)/shard_map/while
  1858.4 29.4 %slice-start.17 = ((s8[11010048]{0:T(1024)(128)(4,1)}), s8[4194304]{0:T(1024)(128)(4,1)S(1)}, s32[]{:S(2)}) async-start(s8[11010048]{0:T(1024)(128)(4,1)} %bitcast.431), calls=%async_computation.29 | async-start | bytes 8388608 | tf_op jit(solution)/shard_map/while
  1931.6 175.4 %collective-permute-start = (bf16[256,768]{1,0:T(8,128)(2,1)}, bf16[256,768]{1,0:T(8,128)(2,1)}, u32[]{:S(2)}, u32[]{:S(2)}) collective-permute-start(bf16[256,768]{1,0:T(8,128)(2,1)} %get-tuple-element.3698), channel_id=1, source_target_pairs={{1,0},{3,2},{5,4},{7,6},{9,8},{11,10},{13,12},{15,14},{17,16},{19,... | collective-permute-start | bytes 1179656 | tf_op jit(solution)/shard_map/while/body/eval_jaxpr/ppermute | solution.py:18
  2109.7 45.5 %copy-start.70 = (f32[768]{0:T(1024)}, f32[768]{0:T(1024)S(1)}, u32[]{:S(2)}) copy-start(f32[768]{0:T(1024)S(1)} %get-tuple-element.3663) | copy-start | bytes 9220 | tf_op jit(solution)/shard_map/while
  2193.1 29.5 %slice-start.13 = ((s8[11010048]{0:T(1024)(128)(4,1)}), s8[4194304]{0:T(1024)(128)(4,1)S(1)}, s32[]{:S(2)}) async-start(s8[11010048]{0:T(1024)(128)(4,1)} %bitcast.429), calls=%async_computation.25 | async-start | bytes 8388608 | tf_op jit(solution)/shard_map/while
  2193.1 29.5 %slice-start.14 = ((s8[11010048]{0:T(1024)(128)(4,1)}), s8[4194304]{0:T(1024)(128)(4,1)S(1)}, s32[]{:S(2)}) async-start(s8[11010048]{0:T(1024)(128)(4,1)} %bitcast.429), calls=%async_computation.26 | async-start | bytes 8388608 | tf_op jit(solution)/shard_map/while
  2193.1 29.5 %slice-start.16 = ((s8[11010048]{0:T(1024)(128)(4,1)}), s8[4194304]{0:T(1024)(128)(4,1)S(1)}, s32[]{:S(2)}) async-start(s8[11010048]{0:T(1024)(128)(4,1)} %bitcast.431), calls=%async_computation.28 | async-start | bytes 8388608 | tf_op jit(solution)/shard_map/while
  2193.1 29.5 %slice-start.17 = ((s8[11010048]{0:T(1024)(128)(4,1)}), s8[4194304]{0:T(1024)(128)(4,1)S(1)}, s32[]{:S(2)}) async-start(s8[11010048]{0:T(1024)(128)(4,1)} %bitcast.431), calls=%async_computation.29 | async-start | bytes 8388608 | tf_op jit(solution)/shard_map/while
  2266.4 175.3 %collective-permute-start = (bf16[256,768]{1,0:T(8,128)(2,1)}, bf16[256,768]{1,0:T(8,128)(2,1)}, u32[]{:S(2)}, u32[]{:S(2)}) collective-permute-start(bf16[256,768]{1,0:T(8,128)(2,1)} %get-tuple-element.3698), channel_id=1, source_target_pairs={{1,0},{3,2},{5,4},{7,6},{9,8},{11,10},{13,12},{15,14},{17,16},{19,... | collective-permute-start | bytes 1179656 | tf_op jit(solution)/shard_map/while/body/eval_jaxpr/ppermute | solution.py:18
  2410.6 27.7 copy-start.90
  2453.6 120.3 %reduce-scatter.19.cloned.1.call-start = ((), (), s32[]{:S(2)}) async-start(), calls=%async_computation.10 | async-start | bytes 208896
  2459.7 141.6 %reduce-scatter.13.cloned.1.call-start = ((), (), s32[]{:S(2)}) async-start(), calls=%async_computation.7 | async-start | bytes 2359296 | tf_op jit(solution)/shard_map/reduce_scatter | solution.py:485
  2461.3 209.9 %reduce-scatter.17.cloned.1.call-start = ((), (), s32[]{:S(2)}) async-start(), calls=%async_computation.9 | async-start | bytes 3342336 | tf_op jit(solution)/shard_map/reduce_scatter | solution.py:455
  2461.3 42.6 %slice-start.24 = ((s8[11010048]{0:T(1024)(128)(4,1)}), s8[4194304]{0:T(1024)(128)(4,1)S(1)}, s32[]{:S(2)}) async-start(s8[11010048]{0:T(1024)(128)(4,1)} %bitcast.438), calls=%async_computation.36 | async-start | bytes 8388608
  2461.3 42.6 %slice-start.25 = ((s8[11010048]{0:T(1024)(128)(4,1)}), s8[4194304]{0:T(1024)(128)(4,1)S(1)}, s32[]{:S(2)}) async-start(s8[11010048]{0:T(1024)(128)(4,1)} %bitcast.438), calls=%async_computation.37 | async-start | bytes 8388608
  2479.9 39.9 %slice-start.21 = ((s8[11010048]{0:T(1024)(128)(4,1)}), s8[4194304]{0:T(1024)(128)(4,1)S(1)}, s32[]{:S(2)}) async-start(s8[11010048]{0:T(1024)(128)(4,1)} %bitcast.436), calls=%async_computation.33 | async-start | bytes 8388608
  2479.9 39.9 %slice-start.22 = ((s8[11010048]{0:T(1024)(128)(4,1)}), s8[4194304]{0:T(1024)(128)(4,1)S(1)}, s32[]{:S(2)}) async-start(s8[11010048]{0:T(1024)(128)(4,1)} %bitcast.436), calls=%async_computation.34 | async-start | bytes 8388608
  2541.9 277.9 %reduce-scatter.15.cloned.1.call-start = ((), (), s32[]{:S(2)}) async-start(), calls=%async_computation.8 | async-start | bytes 15040512 | tf_op jit(solution)/shard_map/reduce_scatter | solution.py:452
  2557.9 289.8 %reduce-scatter.11.cloned.1.call-start = ((), (), s32[]{:S(2)}) async-start(), calls=%async_computation.6 | async-start | bytes 2359296 | tf_op jit(solution)/shard_map/reduce_scatter | solution.py:482
  (670 other events, 5843.7 us)
Sparse Core Ops, SparseCore 0:
  2453.7 62.8 reduce-scatter.20
  2521.0 52.7 reduce-scatter.18
  2576.2 25.0 reduce-scatter.12
  2605.0 66.1 reduce-scatter.16
  2675.2 144.5 reduce-scatter.14
  2822.5 25.1 reduce-scatter.10
where the time goes:
time: 2880 us; the launch traced here: 2850 us
  local copies, waits for them, and re-layouts  976 us (34%)
  other arithmetic  774 us (27%)
  matrix products  752 us (26%)
  waiting for transfers between devices  275 us (10%)
  loops' own time  45.5 us (2%)
    reduce_sum x20, other arithmetic, conv_forward(): jnp.sum(kernel_real * spectra[1] + kernel_imag * spectra[0], axis=0)  194 us
    while x1365, local copies, waits for them, and re-layouts  181 us
    dot_general x60, matrix products, precise_back(): lax.dot_general(table, data, (((0,), (0,)), ((), ())), precision=highest,...  158 us
    dot_general x40, matrix products, precise(): jnp.dot(table, data, precision=highest, preferred_element_type=jnp.float32)  156 us
    reduce_scatter x1, waiting for transfers between devices, body(): lax.psum_scatter(terms.astype(jnp.bfloat16), 'dp', scatter_dimension=0, t...  147 us
    add x5, other arithmetic, add_filter(): lax.dynamic_slice_in_dim(totals[1], segment, pieces, 0) + prod_imag  145 us
    add x5, other arithmetic, backward_step(): terms = terms + weight_on * products  129 us
    dynamic_update_slice x10, local copies, waits for them, and re-layouts, place_rows(): lax.dynamic_update_slice_in_dim(buffer, jnp.where(active, rows, previous)...  127 us
  transfers between devices with their start and end apart: 16, of which 5 were waited for; matrix products, arithmetic and copies ran while one was open for 36% of the time, Pallas kernels for 0%

commit v1 on v0

v1 whole, which is shorter than its diff:
```python
import functools
import math

import jax
import jax.numpy as jnp
import ml_dtypes
import numpy as np
from jax import lax
from jax.experimental import pallas as pl
from jax.experimental.pallas import tpu as pltpu
from jax.sharding import PartitionSpec as P

CH = 256
FT = 512
CARRY = 8
f32, bf16 = jnp.float32, jnp.bfloat16
VMEM_LIMIT = 60 * 1024 * 1024
ANY = pl.BlockSpec(memory_space=pl.ANY)
SMEM = pl.BlockSpec(memory_space=pltpu.SMEM)
VM = pl.BlockSpec(memory_space=pltpu.VMEM)

GAIN, SHIFT, INB, TAP, SKIP, OUTB, DOWNB, UPB = 0, 2, 4, 7, 16, 18, 19, 20


def tables():
    order = np.concatenate([np.arange(0, CH, 2), np.arange(1, CH, 2)])
    angle = np.pi * ((2 * order[:, None] + 1) * np.arange(CH)[None] % (4 * CH)) / (2 * CH)
    cos, sin = np.cos(angle), np.sin(angle)
    sign = np.where(order % 2 == 0, 1.0, -1.0)[:, None]
    spread = np.concatenate([cos, -sin], 0)
    turned = np.concatenate([sign * sin, sign * cos], 0)
    as_low = lambda t: jnp.asarray(t.astype(ml_dtypes.bfloat16))
    return as_low(spread), as_low(spread.T / CH), as_low(np.concatenate([turned, spread], 1))


def dot(x, y):
    return jnp.dot(x, y, preferred_element_type=f32)


def dot_nt(x, y):
    return lax.dot_general(x, y, (((1,), (1,)), ((), ())), preferred_element_type=f32)


def rows_at(index, size):
    return pl.ds(pl.multiple_of(index * size, size), size)


def for_rows(total, size, step):
    def run(i, carry):
        step(pl.multiple_of(i * size, size))
        return carry

    lax.fori_loop(0, total // size, run, 0)


def normalize(rows):
    average = jnp.mean(rows, axis=-1, keepdims=True)
    centered = rows - average
    scale = lax.rsqrt(jnp.mean(centered * centered, axis=-1, keepdims=True) + 1e-05)
    return centered * scale, scale


def norm_back(z, gain, unit, scale):
    w = z * gain
    return (
        w - jnp.mean(w, axis=-1, keepdims=True) - unit * jnp.mean(w * unit, axis=-1, keepdims=True)
    ) * scale


def gelu_pair(u):
    t = 1.0 / (1.0 + (0.3275911 * math.sqrt(0.5)) * jnp.abs(u))
    series = t * (
        0.5 * 0.254829592
        + t * (0.5 * -0.284496736 + t * (0.5 * 1.421413741 + t * (0.5 * -1.453152027 + t * (0.5 * 1.061405429))))
    )
    bell = jnp.exp(-0.5 * (u * u))
    tail = series * bell
    phi_sum = jnp.where(u >= 0, 1.0 - tail, tail)
    return u * phi_sum, phi_sum + u * (bell * (1.0 / math.sqrt(2.0 * math.pi)))


def mix_spectra(left, right, out, low, high, left_of, conj):
    width = out.shape[1] // 2

    def tile(i, carry):
        r = pl.multiple_of(i * 16, 16)
        for half in range(2):
            cols = slice(half * width, (half + 1) * width)

            def term(j, acc):
                k = left_of(j)
                ar = left[k, pl.ds(r, 16), cols].astype(f32)
                ai = left[k, pl.ds(CH + r, 16), cols].astype(f32)
                br = right[j, pl.ds(r, 16), cols].astype(f32)
                bi = right[j, pl.ds(CH + r, 16), cols].astype(f32)
                if conj:
                    return acc[0] + (ar * br + ai * bi), acc[1] + (ar * bi - ai * br)
                return acc[0] + (ar * br - ai * bi), acc[1] + (ar * bi + ai * br)

            zero = jnp.zeros((16, width), f32)
            real, imag = lax.fori_loop(low, high, term, (zero, zero))
            out[pl.ds(r, 16), cols] = real.astype(out.dtype)
            out[pl.ds(CH + r, 16), cols] = imag.astype(out.dtype)
        return carry

    lax.fori_loop(0, CH // 16, tile, 0)


def forward_kernel(pieces, n_state, info, par, *refs):
    (tokens, arrived, filt, win, wout, wup, wdown, spread_h, back_h, pair_h) = refs[:10]
    refs = refs[10 + n_state :]
    out_h, aS, hS, pS, y1S, ybS, mS, nS, eS, dS, s1S, s2S, k1S, k2S, tailS = refs[:15]
    (
        hb, ab, winb, woutb, wupb, wdownb, spread, back, pair, wn1, wn2, k1, k2, s1, s2,
        pb, plow, g2b, sf, sb, yspec, y1b, y1low, yb, mb, nb, ub, eb, db, ob, outb, sem, osem,
    ) = refs[15:]
    seg, active, first = info[0], info[1], info[2]
    D = hb.shape[1]
    FF = wupb.shape[1]
    here = rows_at(seg, CH)

    def cp(src, dst, k):
        return pltpu.make_async_copy(src, dst, sem.at[k])

    def put(src, dst, k):
        c = pltpu.make_async_copy(src, dst, osem.at[k])
        c.start()
        return c

    @pl.when(active == 1)
    def _():
        @pl.when(first == 1)
        def _():
            cp(tokens.at[here], hb, 0).start()

        @pl.when(first == 0)
        def _():
            cp(arrived, hb, 0).start()

        cp(win, winb, 1).start()
        cp(pair_h, pair, 2).start()

        @pl.when(seg == 0)
        def _():
            cp(filt.at[0, pl.ds(0, CH)], wn1.at[pl.ds(CH, CH)], 3).start()
            cp(filt.at[1, pl.ds(0, CH)], wn2.at[pl.ds(CH, CH)], 4).start()
            wn1[pl.ds(0, CH), :] = jnp.zeros((CH, D), bf16)
            wn2[pl.ds(0, CH), :] = jnp.zeros((CH, D), bf16)
            pb[pl.ds(0, CARRY), :] = jnp.zeros((CARRY, 3 * D), f32)

        @pl.when(seg > 0)
        def _():
            before = pl.ds(pl.multiple_of((seg - 1) * CH, CH), 2 * CH)
            cp(filt.at[0, before], wn1, 3).start()
            cp(filt.at[1, before], wn2, 4).start()
            cp(tailS, pb.at[pl.ds(0, CARRY)], 5).start()

        cp(spread_h, spread, 6).start()
        cp(back_h, back, 7).start()
        cp(arrived, hb, 0).wait()
        back_h_put = put(hb, hS.at[here], 0)

        def ln1(r):
            unit, _ = normalize(hb[pl.ds(r, 64), :].astype(f32))
            ab[pl.ds(r, 64), :] = (unit * par[GAIN : GAIN + 1, :] + par[SHIFT : SHIFT + 1, :]).astype(bf16)

        for_rows(CH, 64, ln1)
        a_put = put(ab, aS.at[here], 1)
        cp(win, winb, 1).wait()
        for j in range(pieces - 1):

            @pl.when(j < seg)
            def _(j=j):
                for k, (src, dst) in enumerate(((k1S, k1), (s1S, s1), (k2S, k2), (s2S, s2))):
                    cp(src.at[j], dst.at[j], 8 + 4 * j + k).start()

        base = 8 + 4 * pieces
        cp(wout, woutb, base).start()
        cp(wup, wupb, base + 1).start()
        for b in range(3):
            cols = slice(b * D, (b + 1) * D)
            pb[pl.ds(CARRY, CH), cols] = dot(ab[...], winb[:, cols]) + par[INB + b : INB + b + 1, :]
        cp(wdown, wdownb, base + 2).start()

        @pl.when(seg > 0)
        def _():
            cp(tailS, pb.at[pl.ds(0, CARRY)], 5).wait()

        def short(r):
            got = []
            for b in range(3):
                cols = slice(b * D, (b + 1) * D)
                rows = pb[pl.ds(r, 32 + CARRY), cols]
                now = rows[CARRY:]
                plow[pl.ds(r, 32), cols] = now.astype(bf16)
                t = [par[TAP + 3 * i + b : TAP + 3 * i + b + 1, :] for i in range(3)]
                got.append(t[0] * now + t[1] * rows[CARRY - 1 : -1] + t[2] * rows[CARRY - 2 : -2])
            g2b[pl.ds(r, 32), :] = got[2]
            lead = got[0] * got[1]
            sf[pl.ds(r, 32), :] = lead
            sb[pl.ds(r, 32), :] = lead.astype(bf16)

        for_rows(CH, 32, short)
        p_put = put(plow, pS.at[here], 2)
        tail_put = put(pb.at[pl.ds(CH, CARRY)], tailS, 3)
        cp(pair_h, pair, 2).wait()
        cp(spread_h, spread, 6).wait()
        cp(back_h, back, 7).wait()
        cp(filt.at[0, pl.ds(0, CH)], wn1.at[pl.ds(CH, CH)], 3).wait()
        cp(filt.at[1, pl.ds(0, CH)], wn2.at[pl.ds(CH, CH)], 4).wait()

        @pl.when(seg > 0)
        def _():
            cp(filt.at[0, pl.ds(0, CH)], wn1.at[pl.ds(CH, CH)], 3).wait()
            cp(filt.at[1, pl.ds(0, CH)], wn2.at[pl.ds(CH, CH)], 4).wait()

        for j in range(pieces - 1):

            @pl.when(j < seg)
            def _(j=j):
                for k, (src, dst) in enumerate(((k1S, k1), (s1S, s1), (k2S, k2), (s2S, s2))):
                    cp(src.at[j], dst.at[j], 8 + 4 * j + k).wait()

        k1[seg] = dot(pair[...], wn1[...]).astype(bf16)
        k2[seg] = dot(pair[...], wn2[...]).astype(bf16)
        puts = [put(k1.at[seg], k1S.at[seg], 4), put(k2.at[seg], k2S.at[seg], 5)]
        s1[seg] = dot(spread[...], sb[...]).astype(bf16)
        puts.append(put(s1.at[seg], s1S.at[seg], 6))
        mix_spectra(k1, s1, yspec, 0, seg + 1, lambda j: seg - j, False)
        y1b[...] = dot(back[...], yspec[...])

        def second(r):
            rows = pl.ds(r, 64)
            y = y1b[rows, :] + par[SKIP : SKIP + 1, :] * sf[rows, :]
            y1low[rows, :] = y.astype(bf16)
            trail = y * g2b[rows, :]
            sf[rows, :] = trail
            sb[rows, :] = trail.astype(bf16)

        for_rows(CH, 64, second)
        puts.append(put(y1low, y1S.at[here], 7))
        s2[seg] = dot(spread[...], sb[...]).astype(bf16)
        puts.append(put(s2.at[seg], s2S.at[seg], 8))
        mix_spectra(k2, s2, yspec, 0, seg + 1, lambda j: seg - j, False)
        yb[...] = (dot(back[...], yspec[...]) + par[SKIP + 1 : SKIP + 2, :] * sf[...]).astype(bf16)
        puts.append(put(yb, ybS.at[here], 9))
        cp(wout, woutb, base).wait()
        mb[...] = dot(yb[...], woutb[...])

        def ln2(r):
            rows = pl.ds(r, 64)
            mid = hb[rows, :].astype(f32) + (mb[rows, :] + par[OUTB : OUTB + 1, :])
            mb[rows, :] = mid
            unit, _ = normalize(mid)
            nb[rows, :] = (unit * par[GAIN + 1 : GAIN + 2, :] + par[SHIFT + 1 : SHIFT + 2, :]).astype(bf16)
            ob[rows, :] = mid + par[DOWNB : DOWNB + 1, :]

        for_rows(CH, 64, ln2)
        puts.append(put(mb, mS.at[here], 10))
        puts.append(put(nb, nS.at[here], 11))
        cp(wup, wupb, base + 1).wait()
        cp(wdown, wdownb, base + 2).wait()
        tiles = FF // FT

        def up(k):
            return dot(nb[...], wupb[:, k * FT : (k + 1) * FT])

        def act(k):
            u = ub[k % 2]
            per_row = D // FT if D % FT == 0 else 0
            u = u + bias_up(k)
            e, d = gelu_pair(u)
            eb[:, k * FT : (k + 1) * FT] = e.astype(bf16)
            db[:, k * FT : (k + 1) * FT] = d.astype(bf16)

        def bias_up(k):
            parts, at = [], k * FT
            while at < (k + 1) * FT:
                row, col = at // D, at % D
                wide = min(D - col, (k + 1) * FT - at)
                parts.append(par[UPB + row : UPB + row + 1, col : col + wide])
                at += wide
            return parts[0] if len(parts) == 1 else jnp.concatenate(parts, axis=1)

        def down(k):
            ob[...] += dot(eb[:, k * FT : (k + 1) * FT], wdownb[k * FT : (k + 1) * FT, :])

        ub[0] = up(0)
        for k in range(tiles):
            if k + 1 < tiles:
                ub[(k + 1) % 2] = up(k + 1)
            act(k)
            if k >= 1:
                down(k - 1)
        down(tiles - 1)
        puts.append(put(eb, eS.at[here], 12))
        puts.append(put(db, dS.at[here], 13))
        outb[...] = ob[...].astype(bf16)
        puts.append(put(outb, out_h, 14))
        for c in [back_h_put, a_put, p_put, tail_put] + puts:
            c.wait()


def forward_call(info, par, tokens, arrived, filt, win, wout, wup, wdown, tabs, state):
    T, D = tokens.shape
    FF = wup.shape[1]
    pieces = T // CH
    spec3 = (pieces, 2 * CH, D)
    shapes = [
        ((CH, D), bf16),
        ((T, D), bf16), ((T, D), bf16), ((T, 3 * D), bf16), ((T, D), bf16), ((T, D), bf16), ((T, D), f32),
        ((T, D), bf16), ((T, FF), bf16), ((T, FF), bf16),
        (spec3, bf16), (spec3, bf16), (spec3, bf16), (spec3, bf16),
        ((CARRY, 3 * D), f32),
    ]
    out_shape = [jax.ShapeDtypeStruct(*s) for s in shapes]
    n_state = 0 if state is None else len(shapes) - 1
    V = pltpu.VMEM
    scratch = [
        V((CH, D), bf16), V((CH, D), bf16), V(win.shape, bf16), V(wout.shape, bf16), V(wup.shape, bf16),
        V(wdown.shape, bf16), V((2 * CH, CH), bf16), V((CH, 2 * CH), bf16), V((2 * CH, 2 * CH), bf16),
        V((2 * CH, D), bf16), V((2 * CH, D), bf16), V(spec3, bf16), V(spec3, bf16), V(spec3, bf16), V(spec3, bf16),
        V((CARRY + CH, 3 * D), f32), V((CH, 3 * D), bf16), V((CH, D), f32), V((CH, D), f32), V((CH, D), bf16),
        V((2 * CH, D), bf16), V((CH, D), f32), V((CH, D), bf16), V((CH, D), bf16), V((CH, D), f32), V((CH, D), bf16),
        V((2, CH, FT), f32), V((CH, FF), bf16), V((CH, FF), bf16), V((CH, D), f32), V((CH, D), bf16),
        pltpu.SemaphoreType.DMA((8 + 4 * pieces + 3,)),
        pltpu.SemaphoreType.DMA((15,)),
    ]
    return pl.pallas_call(
        functools.partial(forward_kernel, pieces, n_state),
        out_shape=out_shape,
        in_specs=[SMEM, VM] + [ANY] * (10 + n_state),
        out_specs=[ANY] * len(shapes),
        scratch_shapes=scratch,
        input_output_aliases={12 + i: 1 + i for i in range(n_state)},
        compiler_params=pltpu.CompilerParams(vmem_limit_bytes=VMEM_LIMIT),
        cost_estimate=pl.CostEstimate(flops=2 * CH * (4 * D * D + 2 * D * FF), bytes_accessed=30 << 20, transcendentals=0),
        name="forward_chunk",
    )(info, par, tokens, arrived, filt, win, wout, wup, wdown, *tabs, *(state or ()))


def fold_rows(x):
    return jnp.sum(x.reshape(x.shape[0] // 8, 8, x.shape[1]), axis=0)


def pieces_of(at, wide, D):
    spans, off = [], 0
    while off < wide:
        row, col = (at + off) // D, (at + off) % D
        size = min(D - col, wide - off)
        spans.append((row, col, off, size))
        off += size
    return spans


def backward_kernel(pieces, n_state, info, par, *refs):
    (cots, arrived, win, wout, wup, wdown, spread_h, back_h, hS, pS, y1S, mS, dS, k1S, k2S) = refs[:15]
    refs = refs[15 + n_state :]
    out_h, outf_h, gdS, guS, goS, gpS, g1S, g2S, headS, smallS = refs[:10]
    (
        gdb, winb, woutb, wupb, wdownb, spread, back, k1, k2, g1, g2, db, hb, mb, pb, y1b,
        tb, gub, gnb, gmb, gob, gyb, gylow, gsb, zspec, gy1b, gqb, gpb, outb, outfb, small, sem, osem,
    ) = refs[10:]
    seg, active, last = info[0], info[1], info[2]
    D = hb.shape[1]
    FF = wupb.shape[1]
    here = rows_at(seg, CH)

    def cp(src, dst, k):
        return pltpu.make_async_copy(src, dst, sem.at[k])

    def put(src, dst, k):
        c = pltpu.make_async_copy(src, dst, osem.at[k])
        c.start()
        return c

    def add_small(k, x, cols=slice(None)):
        small[k, :, cols] += fold_rows(x)

    @pl.when(active == 1)
    def _():
        fresh = seg == pieces - 1

        @pl.when(last == 1)
        def _():
            cp(cots.at[here], gdb, 0).start()

        @pl.when(last == 0)
        def _():
            cp(arrived, gdb, 0).start()

        cp(wdown, wdownb, 1).start()
        cp(dS.at[here], db, 2).start()
        cp(wup, wupb, 3).start()
        cp(mS.at[here], mb, 4).start()

        @pl.when(fresh)
        def _():
            small[...] = jnp.zeros(small.shape, f32)
            gqb[pl.ds(CH, CARRY), :] = jnp.zeros((CARRY, 3 * D), f32)

        @pl.when(jnp.logical_not(fresh))
        def _():
            cp(smallS, small, 5).start()
            cp(headS, gqb.at[pl.ds(CH, CARRY)], 6).start()

        cp(arrived, gdb, 0).wait()
        puts = [put(gdb, gdS.at[here], 0)]

        @pl.when(jnp.logical_not(fresh))
        def _():
            cp(smallS, small, 5).wait()
            cp(headS, gqb.at[pl.ds(CH, CARRY)], 6).wait()

        cp(wdown, wdownb, 1).wait()
        cp(dS.at[here], db, 2).wait()
        cp(wout, woutb, 7).start()
        cp(spread_h, spread, 8).start()
        cp(back_h, back, 9).start()
        for j in range(pieces):

            @pl.when(j > seg)
            def _(j=j):
                cp(g2S.at[j], g2.at[j], 16 + 4 * j).start()
                cp(g1S.at[j], g1.at[j], 16 + 4 * j + 1).start()

            @pl.when(j < pieces - seg)
            def _(j=j):
                cp(k2S.at[j], k2.at[j], 16 + 4 * j + 2).start()
                cp(k1S.at[j], k1.at[j], 16 + 4 * j + 3).start()

        @pl.when(seg == 0)
        def _():
            pb[pl.ds(0, 16), :] = jnp.zeros((16, 3 * D), bf16)
            cp(pS.at[pl.ds(0, CH)], pb.at[pl.ds(16, CH)], 10).start()

        @pl.when(seg > 0)
        def _():
            cp(pS.at[pl.ds(pl.multiple_of(seg * CH - 16, 16), CH + 16)], pb, 10).start()

        cp(y1S.at[here], y1b, 11).start()
        cp(win, winb, 12).start()
        cp(hS.at[here], hb, 13).start()
        tiles = FF // FT

        def down(k):
            return dot_nt(gdb[...], wdownb[k * FT : (k + 1) * FT, :])

        def act(k):
            cols = slice(k * FT, (k + 1) * FT)
            gu = (db[:, cols].astype(f32) * tb[k % 2]).astype(bf16)
            gub[:, cols] = gu
            total = fold_rows(gu.astype(f32))
            for row, col, off, size in pieces_of(k * FT, FT, D):
                small[UPB + row, :, col : col + size] += total[:, off : off + size]

        def up(k):
            part = dot_nt(gub[:, k * FT : (k + 1) * FT], wupb[:, k * FT : (k + 1) * FT])
            if k == 0:
                gnb[...] = part
            else:
                gnb[...] += part

        tb[0] = down(0)
        cp(wup, wupb, 3).wait()
        for k in range(tiles):
            if k + 1 < tiles:
                tb[(k + 1) % 2] = down(k + 1)
            act(k)
            if k >= 1:
                up(k - 1)
        up(tiles - 1)
        puts.append(put(gub, guS.at[here], 1))
        cp(mS.at[here], mb, 4).wait()

        def ln2(r):
            rows = pl.ds(r, 32)
            unit, scale = normalize(mb[rows, :])
            z = gnb[rows, :]
            gd = gdb[rows, :].astype(f32)
            gm = gd + norm_back(z, par[GAIN + 1 : GAIN + 2, :], unit, scale)
            gmb[rows, :] = gm
            go = gm.astype(bf16)
            gob[rows, :] = go
            add_small(GAIN + 1, z * unit)
            add_small(SHIFT + 1, z)
            add_small(OUTB, go.astype(f32))
            add_small(DOWNB, gd)

        for_rows(CH, 32, ln2)
        puts.append(put(gob, goS.at[here], 2))
        cp(wout, woutb, 7).wait()
        gy = dot_nt(gob[...], woutb[...])
        gyb[...] = gy
        gylow[...] = gy.astype(bf16)
        cp(spread_h, spread, 8).wait()
        cp(back_h, back, 9).wait()
        g2[seg] = dot(spread[...], gylow[...]).astype(bf16)
        puts.append(put(g2.at[seg], g2S.at[seg], 3))
        for j in range(pieces):

            @pl.when(j > seg)
            def _(j=j):
                cp(g2S.at[j], g2.at[j], 16 + 4 * j).wait()
                cp(g1S.at[j], g1.at[j], 16 + 4 * j + 1).wait()

            @pl.when(j < pieces - seg)
            def _(j=j):
                cp(k2S.at[j], k2.at[j], 16 + 4 * j + 2).wait()
                cp(k1S.at[j], k1.at[j], 16 + 4 * j + 3).wait()

        mix_spectra(k2, g2, zspec, seg, pieces, lambda j: j - seg, True)
        gsb[...] = dot(back[...], zspec[...])

        @pl.when(seg == 0)
        def _():
            cp(pS.at[pl.ds(0, CH)], pb.at[pl.ds(16, CH)], 10).wait()

        @pl.when(seg > 0)
        def _():
            cp(pS.at[pl.ds(0, CH + 16)], pb, 10).wait()

        cp(y1S.at[here], y1b, 11).wait()

        def branch(r, b):
            rows = pb[pl.ds(r, 48), b * D : (b + 1) * D].astype(f32)
            late = [rows[16 - i : 48 - i] for i in range(3)]
            t = [par[TAP + 3 * i + b : TAP + 3 * i + b + 1, :] for i in range(3)]
            return t[0] * late[0] + t[1] * late[1] + t[2] * late[2], late

        def keep(r, b, grad, late):
            gqb[pl.ds(r, 32), b * D : (b + 1) * D] = grad
            for i in range(3):
                add_small(TAP + 3 * i + b, grad * late[i])

        def second(r):
            rows = pl.ds(r, 32)
            gate, late = branch(r, 2)
            y1 = y1b[rows, :].astype(f32)
            gy2 = gyb[rows, :]
            gs2 = gsb[rows, :] + par[SKIP + 1 : SKIP + 2, :] * gy2
            gy1 = gs2 * gate
            gy1b[rows, :] = gy1
            gylow[rows, :] = gy1.astype(bf16)
            add_small(SKIP + 1, gy2 * (y1 * gate))
            keep(r, 2, gs2 * y1, late)

        for_rows(CH, 32, second)
        g1[seg] = dot(spread[...], gylow[...]).astype(bf16)
        puts.append(put(g1.at[seg], g1S.at[seg], 4))
        mix_spectra(k1, g1, zspec, seg, pieces, lambda j: j - seg, True)
        gsb[...] = dot(back[...], zspec[...])

        def first(r):
            rows = pl.ds(r, 32)
            relay, late_relay = branch(r, 0)
            gate, late_gate = branch(r, 1)
            gy1 = gy1b[rows, :]
            gs1 = gsb[rows, :] + par[SKIP : SKIP + 1, :] * gy1
            add_small(SKIP, gy1 * (relay * gate))
            keep(r, 0, gs1 * gate, late_relay)
            keep(r, 1, gs1 * relay, late_gate)

        for_rows(CH, 32, first)
        puts.append(put(gqb.at[pl.ds(0, CARRY)], headS, 5))

        def short(r):
            for b in range(3):
                cols = slice(b * D, (b + 1) * D)
                rows = gqb[pl.ds(r, 32 + CARRY), cols]
                t = [par[TAP + 3 * i + b : TAP + 3 * i + b + 1, :] for i in range(3)]
                gp = (t[0] * rows[:32] + t[1] * rows[1:33] + t[2] * rows[2:34]).astype(bf16)
                gpb[pl.ds(r, 32), cols] = gp
                add_small(INB + b, gp.astype(f32))

        for_rows(CH, 32, short)
        puts.append(put(gpb, gpS.at[here], 6))
        cp(win, winb, 12).wait()
        gnb[...] = dot_nt(gpb[...], winb[...])
        cp(hS.at[here], hb, 13).wait()

        def ln1(r):
            rows = pl.ds(r, 32)
            unit, scale = normalize(hb[rows, :].astype(f32))
            z = gnb[rows, :]
            gh = gmb[rows, :] + norm_back(z, par[GAIN : GAIN + 1, :], unit, scale)
            outfb[rows, :] = gh
            outb[rows, :] = gh.astype(bf16)
            add_small(GAIN, z * unit)
            add_small(SHIFT, z)

        for_rows(CH, 32, ln1)
        puts.append(put(outb, out_h, 7))
        puts.append(put(outfb, outf_h, 8))
        puts.append(put(small, smallS, 9))
        for c in puts:
            c.wait()


def backward_call(info, par, cots, arrived, win, wout, wup, wdown, tabs, kept, state):
    T, D = cots.shape
    FF = wup.shape[1]
    pieces = T // CH
    spec3 = (pieces, 2 * CH, D)
    small = (UPB + FF // D, 8, D)
    shapes = [
        ((CH, D), bf16), ((CH, D), f32),
        ((T, D), bf16), ((T, FF), bf16), ((T, D), bf16), ((T, 3 * D), bf16),
        (spec3, bf16), (spec3, bf16), ((CARRY, 3 * D), f32), (small, f32),
    ]
    out_shape = [jax.ShapeDtypeStruct(*s) for s in shapes]
    n_state = 0 if state is None else len(shapes) - 2
    V = pltpu.VMEM
    scratch = [
        V((CH, D), bf16), V(win.shape, bf16), V(wout.shape, bf16), V(wup.shape, bf16), V(wdown.shape, bf16),
        V((2 * CH, CH), bf16), V((CH, 2 * CH), bf16), V(spec3, bf16), V(spec3, bf16), V(spec3, bf16), V(spec3, bf16),
        V((CH, FF), bf16), V((CH, D), bf16), V((CH, D), f32), V((CH + 16, 3 * D), bf16), V((CH, D), bf16),
        V((2, CH, FT), f32), V((CH, FF), bf16), V((CH, D), f32), V((CH, D), f32), V((CH, D), bf16),
        V((CH, D), f32), V((CH, D), bf16), V((CH, D), f32), V((2 * CH, D), bf16), V((CH, D), f32),
        V((CH + CARRY, 3 * D), f32), V((CH, 3 * D), bf16), V((CH, D), bf16), V((CH, D), f32), V(small, f32),
        pltpu.SemaphoreType.DMA((16 + 4 * pieces,)),
        pltpu.SemaphoreType.DMA((10,)),
    ]
    return pl.pallas_call(
        functools.partial(backward_kernel, pieces, n_state),
        out_shape=out_shape,
        in_specs=[SMEM, VM] + [ANY] * (15 + n_state),
        out_specs=[ANY] * len(shapes),
        scratch_shapes=scratch,
        input_output_aliases={17 + i: 2 + i for i in range(n_state)},
        compiler_params=pltpu.CompilerParams(vmem_limit_bytes=VMEM_LIMIT),
        cost_estimate=pl.CostEstimate(flops=2 * CH * (4 * D * D + 2 * D * FF), bytes_accessed=30 << 20, transcendentals=0),
        name="backward_chunk",
    )(info, par, cots, arrived, win, wout, wup, wdown, tabs[0], tabs[1], *kept, *(state or ()))


def filter_kernel(pieces, s, g, back, turned, out, q):
    width = s.shape[2] // 2

    for d in range(pieces):

        def tile(i, carry, d=d):
            r = pl.multiple_of(i * 16, 16)
            for half in range(2):
                cols = slice(half * width, (half + 1) * width)
                real = jnp.zeros((16, width), f32)
                imag = jnp.zeros((16, width), f32)
                for k in range(d, pieces):
                    ar = s[k - d, pl.ds(r, 16), cols].astype(f32)
                    ai = s[k - d, pl.ds(CH + r, 16), cols].astype(f32)
                    br = g[k, pl.ds(r, 16), cols].astype(f32)
                    bi = g[k, pl.ds(CH + r, 16), cols].astype(f32)
                    real = real + (ar * br + ai * bi)
                    imag = imag + (ar * bi - ai * br)
                q[d, pl.ds(r, 16), cols] = real.astype(bf16)
                q[d, pl.ds(CH + r, 16), cols] = imag.astype(bf16)
            return carry

        lax.fori_loop(0, CH // 16, tile, 0)
    for d in range(pieces):
        rows = dot(back[...], q[d])
        if d + 1 < pieces:
            rows += dot(turned[...], q[d + 1])
        out[pl.ds(d * CH, CH), :] = rows.astype(bf16)


def filter_call(s, g, tabs):
    pieces, _, D = s.shape
    turned = (tabs[2][:, :CH].astype(f32) / CH).astype(bf16).T
    return pl.pallas_call(
        functools.partial(filter_kernel, pieces),
        out_shape=jax.ShapeDtypeStruct((pieces * CH, D), bf16),
        in_specs=[VM] * 4,
        out_specs=VM,
        scratch_shapes=[pltpu.VMEM(s.shape, bf16)],
        compiler_params=pltpu.CompilerParams(vmem_limit_bytes=VMEM_LIMIT),
        name="filter_grad",
    )(s, g, tabs[1], turned)


def dot_rows(x, y):
    return lax.dot_general(x, y, (((0,), (0,)), ((), ())), preferred_element_type=f32).astype(bf16)


def rows_of(chunks, low, high):
    parts, at = [], low
    while at < high:
        k, off = at // CH, at % CH
        size = min(CH - off, high - at)
        parts.append(chunks[k][off : off + size])
        at += size
    return parts[0] if len(parts) == 1 else jnp.concatenate(parts, axis=0)


def spread_rows(chunks, source, total, count, rank):
    share = total // count
    mine = None
    for r in range(count):
        rows = rows_of(chunks, r * share, (r + 1) * share)
        if r != source:
            rows = lax.ppermute(rows.astype(bf16), "section", [(source, r)]).astype(rows.dtype)
        mine = rows if mine is None else jnp.where(rank == r, rows, mine)
    return mine


def body(
    tokens, cotangent, norm_gains, norm_shifts, in_weight, in_bias, short_taps, long_filter, skip_gains,
    out_weight, out_bias, up_weight, up_bias, down_weight, down_bias,
):
    count = lax.axis_size("section")
    ranks = lax.axis_size("dp")
    rank = lax.axis_index("section")
    tok, cot = tokens[0], cotangent[0]
    T, D = tok.shape
    FF = up_weight.shape[2]
    pieces = T // CH
    steps = pieces + 2 * (count - 1)
    tabs = tables()
    as_rows = lambda x: x[0].astype(f32).reshape(-1, D)
    par = jnp.concatenate(
        [as_rows(x) for x in (norm_gains, norm_shifts, in_bias, short_taps, skip_gains, out_bias, down_bias, up_bias)], 0
    )
    win, wout, wup, wdown, filt = in_weight[0], out_weight[0], up_weight[0], down_weight[0], long_filter[0]

    outs, state, sent = [], None, []
    for t in range(steps):
        seg = t - 2 * rank
        active = (seg >= 0) & (seg < pieces)
        info = jnp.stack([jnp.clip(seg, 0, pieces - 1), active.astype(jnp.int32), (rank == 0).astype(jnp.int32)])
        arrived = sent[t - 2] if t >= 2 else tok[:CH]
        got = forward_call(info.astype(jnp.int32), par, tok, arrived, filt, win, wout, wup, wdown, tabs, state)
        outs.append(got[0])
        state = got[1:]
        if t + 2 < steps:
            sent.append(lax.ppermute(got[0], "section", [(i, i + 1) for i in range(count - 1)]))
    aS, hS, pS, y1S, ybS, mS, nS, eS, dS, s1S, s2S, k1S, k2S, _ = state
    kept = (hS, pS, y1S, mS, dS, k1S, k2S)
    stream = spread_rows(outs[2 * (count - 1) :], count - 1, T, count, rank)

    grads, state, sent = [], None, []
    for t in range(steps):
        seg = pieces - 1 - (t - 2 * (count - 1 - rank))
        active = (seg >= 0) & (seg < pieces)
        info = jnp.stack([jnp.clip(seg, 0, pieces - 1), active.astype(jnp.int32), (rank == count - 1).astype(jnp.int32)])
        arrived = sent[t - 2] if t >= 2 else cot[:CH]
        got = backward_call(info.astype(jnp.int32), par, cot, arrived, win, wout, wup, wdown, tabs, kept, state)
        grads.append(got[1])
        state = got[2:]
        if t + 2 < steps:
            sent.append(lax.ppermute(got[0], "section", [(i + 1, i) for i in range(count - 1)]))
    gdS, guS, goS, gpS, g1S, g2S, _, small = state
    token_grad = spread_rows(grads[2 * (count - 1) :][::-1], 0, T, count, rank)

    slab = jnp.concatenate([dot_rows(gdS, eS), dot_rows(nS, guS), dot_rows(ybS, goS), dot_rows(aS, gpS)], axis=1)
    taps = jnp.concatenate([filter_call(s1S, g1S, tabs), filter_call(s2S, g2S, tabs)], axis=1)
    small = jnp.sum(small, axis=1)
    per = D // ranks
    mini = jnp.concatenate(
        [small[:UPB].reshape(UPB, ranks, per).transpose(1, 0, 2).reshape(ranks, -1), small[UPB:].reshape(ranks, -1)], axis=1
    )
    scatter = lambda x: lax.psum_scatter(x, "dp", scatter_dimension=0, tiled=True).astype(f32)
    slab, taps, mini = scatter(slab), scatter(taps), scatter(mini)[0]
    head = mini[: UPB * per].reshape(UPB, per)
    return (
        stream[None],
        token_grad[None],
        head[GAIN : GAIN + 2][None],
        head[SHIFT : SHIFT + 2][None],
        slab[:, 2 * FF + D :][None],
        head[INB : INB + 3][None],
        head[TAP : TAP + 9].reshape(1, 3, 3, per),
        taps.reshape(-1, 2, D).transpose(1, 0, 2)[None],
        head[SKIP : SKIP + 2][None],
        slab[:, 2 * FF : 2 * FF + D][None],
        head[OUTB][None],
        slab[:, FF : 2 * FF][None],
        mini[UPB * per :][None],
        slab[:, :FF].T[None],
        head[DOWNB][None],
    )


def solution(mesh):
    whole = P("dp", None, None)
    split = lambda n: P("section", *([None] * n))
    return jax.shard_map(
        body,
        mesh=mesh,
        in_specs=(
            whole, whole, split(2), split(2), split(2), split(2), split(3), split(3), split(2), split(2), split(1),
            split(2), split(1), split(2), split(1),
        ),
        out_specs=(
            P("dp", "section", None),
            P("dp", "section", None),
            P("section", None, "dp"),
            P("section", None, "dp"),
            P("section", "dp", None),
            P("section", None, "dp"),
            P("section", None, None, "dp"),
            P("section", None, "dp", None),
            P("section", None, "dp"),
            P("section", "dp", None),
            P("section", "dp"),
            P("section", "dp", None),
            P("section", "dp"),
            P("section", None, "dp"),
            P("section", "dp"),
        ),
        check_vma=False,
    )
```

time: 2880 us -> 613 us (0.21)
  local copies, waits for them, and re-layouts: 976 us -> 29 us
  other arithmetic: 774 us -> 31.3 us
  matrix products: 752 us -> 19.1 us
  Pallas kernels: 0 us -> 212 us
  loops' own time: 45.5 us -> 0 us
    dot_general x173 -> x4, matrix products: 752 us -> 19.1 us  [dot_rows(): lax.dot_general(x, y, (((0,), (0,)), ((), ())), preferred_element_type=f32)]
    reduce_sum x85 -> x1, other arithmetic: 379 us -> 1.21 us  [body(): small = jnp.sum(small, axis=1)]
    dynamic_update_slice x50 -> x0, local copies, waits for them, and re-layouts: 364 us -> none  [the longest x10 127 us: place_rows(): lax.dynamic_update_slice_in_dim(buffer, jnp.where(active, rows, previous)...]
    add x50 -> x0, other arithmetic: 324 us -> none  [the longest x5 145 us: add_filter(): lax.dynamic_slice_in_dim(totals[1], segment, pieces, 0) + prod_imag]
    dynamic_slice x40 -> x0, local copies, waits for them, and re-layouts: 252 us -> none  [the longest x20 127 us: add_filter(): lax.dynamic_slice_in_dim(totals[1], segment, pieces, 0) + prod_imag]
    pallas_call x0 -> x14, Pallas kernels: none -> 212 us  [the longest x6 104 us: backward_call(): pl.pallas_call(functools.partial(backward_kernel, pieces, n_state), out_s...]
    while x1365 -> x0, local copies, waits for them, and re-layouts: 181 us -> none
    ppermute x10, waiting for transfers between devices: 0.03 us -> 67.8 us  [the longest x4 47.9 us: body(): lax.ppermute(got[0], 'section', [(i + 1, i) for i in range(count - 1)])]
  transfers between devices with their start and end apart: 16 -> 13, of which waited for: 5 -> 9; matrix products, arithmetic and copies ran while one was open for 36% -> 10% of each run, Pallas kernels for 0% -> 26%
where the time goes in v1:
time: 613 us; the launch traced here: 605 us
  waiting for transfers between devices  282 us (46%)
  Pallas kernels  212 us (35%)
  other arithmetic  31.3 us (5%)
  local copies, waits for them, and re-layouts  29 us (5%)
  matrix products  19.1 us (3%)
  starting transfers between devices  17.9 us (3%)
  between operations  14.8 us (2%)
    reduce_scatter x2, waiting for transfers between devices, body(): lax.psum_scatter(x, 'dp', scatter_dimension=0, tiled=True).astype(f32)  204 us
    pallas_call x6, Pallas kernels, backward_call(): pl.pallas_call(functools.partial(backward_kernel, pieces, n_state), out_s...  104 us
    pallas_call x6, Pallas kernels, forward_call(): pl.pallas_call(functools.partial(forward_kernel, pieces, n_state), out_sh...  89.6 us
    ppermute x4, waiting for transfers between devices, body(): lax.ppermute(got[0], 'section', [(i + 1, i) for i in range(count - 1)])  47.9 us
    dot_general x4, matrix products, dot_rows(): lax.dot_general(x, y, (((0,), (0,)), ((), ())), preferred_element_type=f32)  19.1 us
    pallas_call x2, Pallas kernels, filter_call(): pl.pallas_call(functools.partial(filter_kernel, pieces), out_shape=jax.Sh...  18.3 us
    ppermute x2, waiting for transfers between devices, spread_rows(): lax.ppermute(rows.astype(bf16), 'section', [(source, r)]).astype(rows.dtype)  13 us
  transfers between devices with their start and end apart: 13, of which 9 were waited for; matrix products, arithmetic and copies ran while one was open for 10% of the time, Pallas kernels for 26%

profile of v1, /device:TPU:0, one launch (start us, length us, event | category | flops | bytes accessed | tf_op | source)
XLA Modules:
  0.0 605.2 jit_solution(17003053007137747554)
XLA Ops:
  8.8 1.6 concatenate.27
  11.0 1.8 slice_bitcast_fusion.4.refs_1_
  13.4 17.4 %forward_chunk.6 = (bf16[256,768]{1,0:T(8,128)(2,1)}, bf16[1024,768]{1,0:T(8,128)(2,1)}, bf16[1024,768]{1,0:T(8,128)(2,1)}, bf16[1024,2304]{1,0:T(8,128)(2,1)}, ...) custom-call(s32[3]{0:T(128)} %get-tuple-element.355.info, ...), custom_call_target="tpu_custom_call" | custom-call | flops 3623878656 | bytes 31457280 | tf_op jit(solution)/shard_map/forward_chunk/pallas_call | solution.py:329
  30.8 1.3 collective-permute-start
  32.2 18.7 %forward_chunk.7 = (bf16[256,768]{1,0:T(8,128)(2,1)}, bf16[1024,768]{1,0:T(8,128)(2,1)}, bf16[1024,768]{1,0:T(8,128)(2,1)}, bf16[1024,2304]{1,0:T(8,128)(2,1)}, ...) custom-call(s32[3]{0:T(128)} %get-tuple-element.356.info, ...), custom_call_target="tpu_custom_call", output_to_operand_aliasing={{1}: (12, {}), {2}: (13, {}), {3}: (14, {}), {4}: (15, {}),... | custom-call | flops 3623878656 | bytes 31457280 | tf_op jit(solution)/shard_map/forward_chunk/pallas_call | solution.py:329
  50.9 1.3 collective-permute-start.2
  55.3 1.8 slice_bitcast_fusion.3.refs_1_
  58.4 20.0 %forward_chunk.8 = (bf16[256,768]{1,0:T(8,128)(2,1)}, bf16[1024,768]{1,0:T(8,128)(2,1)}, bf16[1024,768]{1,0:T(8,128)(2,1)}, bf16[1024,2304]{1,0:T(8,128)(2,1)}, ...) custom-call(s32[3]{0:T(128)} %add_add_fusion.1.info, ...), custom_call_target="tpu_custom_call", output_to_operand_aliasing={{1}: (12, {}), {2}: (13, {}), {3}: (14, {}), {4}: (15, {}),... | custom-call | flops 3623878656 | bytes 31457280 | tf_op jit(solution)/shard_map/forward_chunk/pallas_call | solution.py:329
  78.4 1.3 collective-permute-start.1
  80.5 22.4 %forward_chunk.9 = (bf16[256,768]{1,0:T(8,128)(2,1)}, bf16[1024,768]{1,0:T(8,128)(2,1)}, bf16[1024,768]{1,0:T(8,128)(2,1)}, bf16[1024,2304]{1,0:T(8,128)(2,1)}, ...) custom-call(s32[3]{0:T(128)} %add_add_fusion.4.info, ...), custom_call_target="tpu_custom_call", output_to_operand_aliasing={{1}: (12, {}), {2}: (13, {}), {3}: (14, {}), {4}: (15, {}),... | custom-call | flops 3623878656 | bytes 31457280 | tf_op jit(solution)/shard_map/forward_chunk/pallas_call | solution.py:329
  102.9 1.3 collective-permute-start.3
  106.9 6.9 %collective-permute-done.3.refs_1_ = bf16[256,768]{1,0:T(8,128)(2,1)S(1)} collective-permute-done((bf16[256,768]{1,0:T(8,128)(2,1)}, bf16[256,768]{1,0:T(8,128)(2,1)S(1)}, u32[]{:S(2)}, u32[]{:S(2)}) %collective-permute-start.3) | collective-permute-done | bytes 393248 | tf_op jit(solution)/shard_map/ppermute | solution.py:735
  114.5 9.8 %forward_chunk.11 = (bf16[256,768]{1,0:T(8,128)(2,1)}, bf16[1024,768]{1,0:T(8,128)(2,1)}, bf16[1024,768]{1,0:T(8,128)(2,1)}, bf16[1024,2304]{1,0:T(8,128)(2,1)},...) custom-call(s32[3]{0:T(128)} %add_add_fusion.5.info, ...), custom_call_target="tpu_custom_call", output_to_operand_aliasing={{1}: (12, {}), {2}: (13, {}), {3}: (14, {}), {4}: (15, {}),... | custom-call | flops 3623878656 | bytes 31457280 | tf_op jit(solution)/shard_map/forward_chunk/pallas_call | solution.py:329
  124.3 1.3 backward_chunk.6
  125.7 1.3 collective-permute-start.6
  127.0 1.3 backward_chunk.7
  128.3 1.3 collective-permute-start.5
  130.2 43.1 %collective-permute-done.6.refs_1_ = bf16[256,768]{1,0:T(8,128)(2,1)S(1)} collective-permute-done((bf16[256,768]{1,0:T(8,128)(2,1)}, bf16[256,768]{1,0:T(8,128)(2,1)S(1)}, u32[]{:S(2)}, u32[]{:S(2)}) %collective-permute-start.6) | collective-permute-done | bytes 393248 | tf_op jit(solution)/shard_map/ppermute | solution.py:750
  174.0 23.3 %backward_chunk.8 = (bf16[256,768]{1,0:T(8,128)(2,1)}, f32[256,768]{1,0:T(8,128)}, bf16[1024,768]{1,0:T(8,128)(2,1)}, bf16[1024,3072]{1,0:T(8,128)(2,1)}, bf16[1...) custom-call(s32[3]{0:T(128)} %add_add_fusion.9.info, ...), custom_call_target="tpu_custom_call", output_to_operand_aliasing={{2}: (17, {}), {3}: (18, {}), {4}: (19, {}), {5}: (20, {}),... | custom-call | flops 3623878656 | bytes 31457280 | tf_op jit(solution)/shard_map/backward_chunk/pallas_call | solution.py:624
  197.3 1.3 collective-permute-start.9
  200.2 24.8 %backward_chunk.9 = (bf16[256,768]{1,0:T(8,128)(2,1)}, f32[256,768]{1,0:T(8,128)}, bf16[1024,768]{1,0:T(8,128)(2,1)}, bf16[1024,3072]{1,0:T(8,128)(2,1)}, bf16[1...) custom-call(s32[3]{0:T(128)} %add_add_fusion.6.info, ...), custom_call_target="tpu_custom_call", output_to_operand_aliasing={{2}: (17, {}), {3}: (18, {}), {4}: (19, {}), {5}: (20, {}),... | custom-call | flops 3623878656 | bytes 31457280 | tf_op jit(solution)/shard_map/backward_chunk/pallas_call | solution.py:624
  225.0 1.3 collective-permute-start.8
  226.9 1.6 collective-permute-done.9.refs_1_
  229.2 25.8 %backward_chunk.10 = (bf16[256,768]{1,0:T(8,128)(2,1)}, f32[256,768]{1,0:T(8,128)}, bf16[1024,768]{1,0:T(8,128)(2,1)}, bf16[1024,3072]{1,0:T(8,128)(2,1)}, bf16[...) custom-call(s32[3]{0:T(128)} %add_add_fusion.11.info, ...), custom_call_target="tpu_custom_call", output_to_operand_aliasing={{2}: (17, {}), {3}: (18, {}), {4}: (19, {}), {5}: (20, {}),... | custom-call | flops 3623878656 | bytes 31457280 | tf_op jit(solution)/shard_map/backward_chunk/pallas_call | solution.py:624
  255.0 2.3 collective-permute-done.8.refs_1_
  258.1 27.2 %backward_chunk.11 = (bf16[256,768]{1,0:T(8,128)(2,1)}, f32[256,768]{1,0:T(8,128)}, bf16[1024,768]{1,0:T(8,128)(2,1)}, bf16[1024,3072]{1,0:T(8,128)(2,1)}, bf16[...) custom-call(s32[3]{0:T(128)} %add_add_fusion.10.info, ...), custom_call_target="tpu_custom_call", output_to_operand_aliasing={{2}: (17, {}), {3}: (18, {}), {4}: (19, {}), {5}: (20, {}),... | custom-call | flops 3623878656 | bytes 31457280 | tf_op jit(solution)/shard_map/backward_chunk/pallas_call | solution.py:624
  287.7 9.1 %filter_grad.3 = bf16[1024,768]{1,0:T(8,128)(2,1)} custom-call(bf16[4,512,768]{2,1,0:T(8,128)(2,1)} %get-tuple-element.301.s, bf16[4,512,768]{2,1,0:T(8,128)(2,1)} %get-tuple-element.302.g, bf16[256,512]{1,0:T(8,128)(2,1)} %constant.28.clone.refs_8_.refs_7_.back, bf16[256,512]{1,0:T(8,128)(2,1)} %constant.49.turned), custom_call_target="tpu_custom_call" | custom-call | tf_op jit(solution)/shard_map/filter_grad/pallas_call | solution.py:670
  296.8 9.2 %filter_grad.2 = bf16[1024,768]{1,0:T(8,128)(2,1)} custom-call(bf16[4,512,768]{2,1,0:T(8,128)(2,1)} %get-tuple-element.299.s, bf16[4,512,768]{2,1,0:T(8,128)(2,1)} %get-tuple-element.300.g, bf16[256,512]{1,0:T(8,128)(2,1)} %constant.28.clone.refs_8_.refs_7_.back, bf16[256,512]{1,0:T(8,128)(2,1)} %constant.49.turned), custom_call_target="tpu_custom_call" | custom-call | tf_op jit(solution)/shard_map/filter_grad/pallas_call | solution.py:670
  306.0 4.0 pad_maximum_fusion.1
  310.4 6.9 %convolution_convert_fusion.2 = bf16[768,2304]{1,0:T(8,128)(2,1)S(1)} fusion(bf16[1024,768]{1,0:T(8,128)(2,1)} %get-tuple-element.297, bf16[1024,2304]{1,0:T(8,128)(2,1)} %get-tuple-element.298), kind=kOutput, calls=%fused_computation.3 | convolution fusion | flops 3625648128 | bytes 9830400 | tf_op jit(solution)/shard_map/dot_general | solution.py:682
  317.3 1.4 convolution_convert_fusion.3
  318.8 5.4 convolution_convert_fusion.1
  324.2 5.4 convolution_convert_fusion
  329.6 10.7 %pad_maximum_fusion = bf16[768,9216]{1,0:T(8,128)(2,1)} fusion(bf16[768,2304]{1,0:T(8,128)(2,1)S(1)} %convolution_convert_fusion.2, bf16[768,768]{1,0:T(8,128)(2,1)S(1)} %convolution_convert_fusion.3, bf16[768,3072]{1,0:T(8,128)(2,1)S(1)} %convolution_convert_fusion, bf16[768,3072]{1,0:T(8,128)(2,1)S(1)} %convolution_convert_fusion.1), kind=kLoop, calls=%fused_computation | loop fusion | flops 56623104 | bytes 28311552 | tf_op jit(solution)/shard_map/concatenate | solution.py:754
  341.6 1.4 collective-permute-start.4
  343.2 5.6 collective-permute-start.7
  349.4 13.0 %collective-permute-done.4 = bf16[512,768]{1,0:T(8,128)(2,1)S(1)} collective-permute-done((bf16[512,768]{1,0:T(8,128)(2,1)S(1)}, bf16[512,768]{1,0:T(8,128)(2,1)S(1)}, u32[]{:S(2)}, u32[]{:S(2)}) %collective-permute-start.4) | collective-permute-done | bytes 786464 | tf_op jit(solution)/shard_map/ppermute | solution.py:701
  362.3 2.1 fusion.1
  364.4 9.3 %all-reduce.3.cloned.1.call-done = f32[16,1152]{1,0:T(8,128)} async-done(((f32[16,1152]{1,0:T(8,128)}), f32[16,1152]{1,0:T(8,128)}) %all-reduce.3.cloned.1.call-update) | async-done | bytes 73744
  373.7 1.4 dynamic-slice_reduce_fusion.1
  375.8 1.5 dynamic-slice_reduce_fusion.2
  379.2 1.5 dynamic-slice_reduce_fusion
  381.3 2.0 dynamic-slice.8
  383.3 2.0 fusion.2
  385.3 2.8 fusion
  388.1 56.9 %reduce-scatter.5.cloned.1.call-done = bf16[64,1536]{1,0:T(8,128)(2,1)} async-done(((bf16[1024,1536]{1,0:T(8,128)(2,1)}), bf16[64,1536]{1,0:T(8,128)(2,1)}) %reduce-scatter.5.cloned.1.call-update) | async-done | bytes 196624 | tf_op jit(solution)/shard_map/reduce_scatter | solution.py:761
  446.7 147.6 %reduce-scatter.3.cloned.1.call-done = bf16[48,9216]{1,0:T(8,128)(2,1)} async-done(((bf16[768,9216]{1,0:T(8,128)(2,1)}), bf16[48,9216]{1,0:T(8,128)(2,1)}) %reduce-scatter.3.cloned.1.call-update) | async-done | bytes 884752 | tf_op jit(solution)/shard_map/reduce_scatter | solution.py:761
  594.3 1.3 convert_element_type.93
  (96 shorter events, 28.5 us)
Async XLA Ops:
  7.2 366.5 %all-reduce.3.cloned.1.call-start = ((), (), s32[]{:S(2)}) async-start(), calls=%async_computation.4 | async-start | bytes 147456
  30.8 26.8 %collective-permute-start = (bf16[256,768]{1,0:T(8,128)(2,1)}, bf16[256,768]{1,0:T(8,128)(2,1)S(1)}, u32[]{:S(2)}, u32[]{:S(2)}) collective-permute-start(bf16[256,768]{1,0:T(8,128)(2,1)} %get-tuple-element.159), channel_id=1, source_target_pairs={{0,1},{2,3},{4,5},{6,7},{8,9},{10,11},{12,13},{14,15},{16,17},{18,... | collective-permute-start | bytes 1179656 | tf_op jit(solution)/shard_map/ppermute | solution.py:735
  50.9 28.9 %collective-permute-start.2 = (bf16[256,768]{1,0:T(8,128)(2,1)}, bf16[256,768]{1,0:T(8,128)(2,1)S(1)}, u32[]{:S(2)}, u32[]{:S(2)}) collective-permute-start(bf16[256,768]{1,0:T(8,128)(2,1)} %get-tuple-element.189), channel_id=1, source_target_pairs={{0,1},{2,3},{4,5},{6,7},{8,9},{10,11},{12,13},{14,15},{16,17},{18,... | collective-permute-start | bytes 1179656 | tf_op jit(solution)/shard_map/ppermute | solution.py:735
  57.7 0.7 copy-start.8
  78.4 26.4 %collective-permute-start.1 = (bf16[256,768]{1,0:T(8,128)(2,1)}, bf16[256,768]{1,0:T(8,128)(2,1)S(1)}, u32[]{:S(2)}, u32[]{:S(2)}) collective-permute-start(bf16[256,768]{1,0:T(8,128)(2,1)} %get-tuple-element.188), channel_id=1, source_target_pairs={{0,1},{2,3},{4,5},{6,7},{8,9},{10,11},{12,13},{14,15},{16,17},{18,... | collective-permute-start | bytes 1179656 | tf_op jit(solution)/shard_map/ppermute | solution.py:735
  79.7 0.7 copy-start.7
  102.9 10.9 %collective-permute-start.3 = (bf16[256,768]{1,0:T(8,128)(2,1)}, bf16[256,768]{1,0:T(8,128)(2,1)S(1)}, u32[]{:S(2)}, u32[]{:S(2)}) collective-permute-start(bf16[256,768]{1,0:T(8,128)(2,1)} %get-tuple-element.219), channel_id=1, source_target_pairs={{0,1},{2,3},{4,5},{6,7},{8,9},{10,11},{12,13},{14,15},{16,17},{18,... | collective-permute-start | bytes 1179656 | tf_op jit(solution)/shard_map/ppermute | solution.py:735
  104.8 0.7 copy-start.9
  113.8 0.7 copy-start.10
  125.7 47.6 %collective-permute-start.6 = (bf16[256,768]{1,0:T(8,128)(2,1)}, bf16[256,768]{1,0:T(8,128)(2,1)S(1)}, u32[]{:S(2)}, u32[]{:S(2)}) collective-permute-start(bf16[256,768]{1,0:T(8,128)(2,1)} %get-tuple-element.251), channel_id=1, source_target_pairs={{1,0},{3,2},{5,4},{7,6},{9,8},{11,10},{13,12},{15,14},{17,16},{19,... | collective-permute-start | bytes 1179656 | tf_op jit(solution)/shard_map/ppermute | solution.py:750
  128.3 71.1 %collective-permute-start.5 = (bf16[256,768]{1,0:T(8,128)(2,1)}, bf16[256,768]{1,0:T(8,128)(2,1)S(1)}, u32[]{:S(2)}, u32[]{:S(2)}) collective-permute-start(bf16[256,768]{1,0:T(8,128)(2,1)} %get-tuple-element.250), channel_id=1, source_target_pairs={{1,0},{3,2},{5,4},{7,6},{9,8},{11,10},{13,12},{15,14},{17,16},{19,... | collective-permute-start | bytes 1179656 | tf_op jit(solution)/shard_map/ppermute | solution.py:750
  173.3 0.7 copy-start.11
  197.3 31.2 %collective-permute-start.9 = (bf16[256,768]{1,0:T(8,128)(2,1)}, bf16[256,768]{1,0:T(8,128)(2,1)S(1)}, u32[]{:S(2)}, u32[]{:S(2)}) collective-permute-start(bf16[256,768]{1,0:T(8,128)(2,1)} %get-tuple-element.271), channel_id=1, source_target_pairs={{1,0},{3,2},{5,4},{7,6},{9,8},{11,10},{13,12},{15,14},{17,16},{19,... | collective-permute-start | bytes 1179656 | tf_op jit(solution)/shard_map/ppermute | solution.py:750
  199.4 0.7 copy-start.12
  225.0 32.4 %collective-permute-start.8 = (bf16[256,768]{1,0:T(8,128)(2,1)}, bf16[256,768]{1,0:T(8,128)(2,1)S(1)}, u32[]{:S(2)}, u32[]{:S(2)}) collective-permute-start(bf16[256,768]{1,0:T(8,128)(2,1)} %get-tuple-element.270), channel_id=1, source_target_pairs={{1,0},{3,2},{5,4},{7,6},{9,8},{11,10},{13,12},{15,14},{17,16},{19,... | collective-permute-start | bytes 1179656 | tf_op jit(solution)/shard_map/ppermute | solution.py:750
  228.5 0.7 copy-start.14
  257.4 0.7 copy-start.13
  287.7 157.3 %reduce-scatter.5.cloned.1.call-start = ((), (), s32[]{:S(2)}) async-start(), calls=%async_computation.3 | async-start | bytes 3342336 | tf_op jit(solution)/shard_map/reduce_scatter | solution.py:761
  306.0 12.7 %slice-start = ((s8[6291456]{0:T(1024)(128)(4,1)}), s8[2097152]{0:T(1024)(128)(4,1)S(1)}, s32[]{:S(2)}) async-start(s8[6291456]{0:T(1024)(128)(4,1)} %bitcast.123), calls=%async_computation.5 | async-start | bytes 4194304
  310.0 284.3 %reduce-scatter.3.cloned.1.call-start = ((), (), s32[]{:S(2)}) async-start(), calls=%async_computation.2 | async-start | bytes 15040512 | tf_op jit(solution)/shard_map/reduce_scatter | solution.py:761
  310.4 6.9 %copy-start.1 = (bf16[1024,768]{1,0:T(8,128)(2,1)S(1)}, bf16[1024,768]{1,0:T(8,128)(2,1)}, u32[]{:S(2)}) copy-start(bf16[1024,768]{1,0:T(8,128)(2,1)} %get-tuple-element.296) | copy-start | bytes 4718596
  310.4 6.9 %copy-start.2 = (bf16[1024,768]{1,0:T(8,128)(2,1)S(1)}, bf16[1024,768]{1,0:T(8,128)(2,1)}, u32[]{:S(2)}) copy-start(bf16[1024,768]{1,0:T(8,128)(2,1)} %get-tuple-element.295) | copy-start | bytes 4718596
  310.4 8.4 %slice-start.1 = ((s8[6291456]{0:T(1024)(128)(4,1)}), s8[4194304]{0:T(1024)(128)(4,1)S(1)}, s32[]{:S(2)}) async-start(s8[6291456]{0:T(1024)(128)(4,1)} %bitcast.123), calls=%async_computation.6 | async-start | bytes 8388608
  317.3 1.5 copy-start
  317.3 6.9 %slice-start.2 = ((s8[6291456]{0:T(1024)(128)(4,1)}), s8[4194304]{0:T(1024)(128)(4,1)S(1)}, s32[]{:S(2)}) async-start(s8[6291456]{0:T(1024)(128)(4,1)} %bitcast.125), calls=%async_computation.7 | async-start | bytes 8388608
  318.8 5.4 slice-start.3
  318.8 5.4 copy-start.3
  340.4 1.0 copy-start.16
  340.4 1.1 copy-start.17
  340.4 2.6 copy-start.4
  341.5 1.6 copy-start.5
  341.5 7.3 %copy-start.18 = (u32[32]{0:T(128)S(1)}, u32[32]{0:T(128)}, u32[]{:S(2)}) copy-start(u32[32]{0:T(128)} %constant.52) | copy-start | bytes 388
  341.5 20.8 %copy-start.15 = (bf16[256,768]{1,0:T(8,128)(2,1)S(1)}, bf16[256,768]{1,0:T(8,128)(2,1)}, u32[]{:S(2)}) copy-start(bf16[256,768]{1,0:T(8,128)(2,1)} %get-tuple-element.218) | copy-start | bytes 1179652
  341.6 20.8 %collective-permute-start.4 = (bf16[512,768]{1,0:T(8,128)(2,1)S(1)}, bf16[512,768]{1,0:T(8,128)(2,1)S(1)}, u32[]{:S(2)}, u32[]{:S(2)}) collective-permute-start(bf16[512,768]{1,0:T(8,128)(2,1)S(1)} %pad_maximum_fusion.2), channel_id=1, source_target_pairs={{1,0},{3,2},{5,4},{7,6},{9,8},{11,10},{13,12},{15,14},{17,16},{19,... | collective-permute-start | bytes 2359304 | tf_op jit(solution)/shard_map/ppermute | solution.py:701
  343.0 42.3 %copy-start.6 = (f32[256,768]{1,0:T(8,128)S(1)}, f32[256,768]{1,0:T(8,128)}, u32[]{:S(2)}) copy-start(f32[256,768]{1,0:T(8,128)} %get-tuple-element.289) | copy-start | bytes 2359300
  343.2 42.2 %collective-permute-start.7 = (bf16[512,768]{1,0:T(8,128)(2,1)S(1)}, bf16[512,768]{1,0:T(8,128)(2,1)}, u32[]{:S(2)}, u32[]{:S(2)}) collective-permute-start(bf16[512,768]{1,0:T(8,128)(2,1)S(1)} %pad_maximum_fusion.3), channel_id=1, source_target_pairs={{0,1},{2,3},{4,5},{6,7},{8,9},{10,11},{12,13},{14,15},{16,17},{18,... | collective-permute-start | bytes 2359304 | tf_op jit(solution)/shard_map/ppermute | solution.py:701
Sparse Core Ops, SparseCore 0:
  287.8 85.8 all-reduce.2
  377.9 67.0 reduce-scatter.4
  449.7 144.5 reduce-scatter.2

commit v2 on v1

--- a/solution.py
+++ b/solution.py
@@ -678,6 +678,308 @@
     )(s, g, tabs[1], turned)
 
 
+def exchange_kernel(
+    pieces, small_in, back_h, turned_h, gdS, eS, nS, guS, ybS, goS, aS, gpS, s1S, g1S, s2S, g2S,
+    downT, upO, outO, inO, filtO, smallO,
+    x, r1, r2, rr, rl, gb, lb, lt, sb, qb, back, turned, ob, mine, got, lsem, osem, csem, ysem, rsem, fsem, msem,
+):
+    D = lb.shape[2]
+    me = lax.axis_index("dp")
+    c, y, z = me % 2, (me // 2) % 2, me // 4
+    Z = r2.shape[1]
+    groups = lt.shape[2]
+    n_blocks = 3 * groups + 2
+    at = lambda i: {"dp": i}
+    core_id, y_id = me + 1 - 2 * c, me + 2 - 4 * y
+    mates = (core_id, y_id, me + 4 - 8 * (z % 2), me + 8 - 16 * (z // 2))
+    inner = (z == 1) | (z == 2)
+
+    barrier = pltpu.get_barrier_semaphore()
+    for mate in mates:
+        pl.semaphore_signal(barrier, inc=1, device_id=at(mate), device_id_type=pl.DeviceIdType.MESH)
+
+    @pl.when(inner)
+    def _():
+        other = me + 12 - 8 * z
+        pl.semaphore_signal(barrier, inc=1, device_id=at(other), device_id_type=pl.DeviceIdType.MESH)
+
+    @pl.when(inner)
+    def _():
+        pl.semaphore_wait(barrier, len(mates) + 1)
+
+    @pl.when(jnp.logical_not(inner))
+    def _():
+        pl.semaphore_wait(barrier, len(mates))
+
+    def remote(src, dst, send, recv, mate):
+        return pltpu.make_async_remote_copy(
+            src_ref=src, dst_ref=dst, send_sem=send, recv_sem=recv, device_id=at(mate),
+            device_id_type=pl.DeviceIdType.MESH,
+        )
+
+    def load(src, dst, k):
+        return pltpu.make_async_copy(src, dst, lsem.at[k])
+
+    rights = ((eS,), (guS,), (goS, gpS))
+    lefts = ((gdS,), (nS,), (ybS, aS))
+
+    def loads(m):
+        found, off = [], 0
+        for k, src in enumerate(rights[m]):
+            wide = src.shape[1]
+            found.append(load(src, gb.at[m % 2, :, pl.ds(off, wide)], 4 * m + k))
+            off += wide
+        for k, src in enumerate(lefts[m]):
+            found.append(load(src, lb.at[k], 4 * m + 2 + k))
+        return found
+
+    def spectra(f):
+        src = ((s1S, g1S), (s2S, g2S))[f]
+        return [load(src[k], sb.at[k], 12 + 2 * f + k) for k in range(2)]
+
+    def turn(m):
+        for k in range(len(lefts[m])):
+
+            def part(i, carry, k=k):
+                rows = pl.multiple_of(i * 128, 128)
+                piece = jnp.transpose(lb[k, pl.ds(rows, 128), :])
+                lt[k, :, :, :, pl.ds(rows, 128)] = piece.reshape(lt.shape[1:4] + (128,))
+                return carry
+
+            lax.fori_loop(0, lb.shape[1] // 128, part, 0)
+
+    def product(m, g, slot):
+        def part(i, carry):
+            k = jnp.minimum(i, 1) if m == 2 else 0
+            left = lt[k, :, g].reshape(16 * lt.shape[1], lt.shape[4])
+            cols = pl.ds(pl.multiple_of(i * D, D), D)
+            value = dot(left, gb[m % 2, :, cols]).astype(bf16)
+            x[slot, :, :, :, pl.ds(pl.multiple_of(i * 16, 16), 16), :] = value.reshape(x.shape[1:4] + (16, D))
+            return carry
+
+        lax.fori_loop(0, 4, part, 0)
+
+    def filters(f, slot):
+        def mix(d, carry):
+            mix_spectra(sb.at[0], sb.at[1], qb.at[d], d, pieces, lambda j: j - d, True)
+            return carry
+
+        lax.fori_loop(0, pieces, mix, 0)
+        qb[pieces] = jnp.zeros(qb.shape[1:], bf16)
+
+        def part(d, carry):
+            rows = dot(back[...], qb[d]) + dot(turned[...], qb[d + 1])
+            x[slot, d] = rows.astype(bf16).reshape(x.shape[2:])
+            return carry
+
+        lax.fori_loop(0, pieces, part, 0)
+
+    def core_copy(b, slot):
+        return remote(x.at[slot, :, :, 1 - c], r1.at[b], csem.at[0, b], csem.at[1, b], core_id)
+
+    def y_copy(b):
+        return remote(r1.at[b, :, 1 - y], r2.at[b], ysem.at[0, b], ysem.at[1, b], y_id)
+
+    def right_copy(b, d, src):
+        return remote(src, rr.at[b, d - 1], rsem.at[0, b, d - 1], rsem.at[1, b, d - 1], me + 4)
+
+    def left_copy(b, d, src):
+        return remote(src, rl.at[b, d], fsem.at[0, b, d], fsem.at[1, b, d], me - 4)
+
+    def add(p, q):
+        return (p.astype(f32) + q.astype(f32)).astype(bf16)
+
+    def after_core(b):
+        slot = b % x.shape[0]
+        core_copy(b, slot).wait()
+
+        def part(i, carry):
+            for j in range(2):
+                r1[b, i, j] = add(r1[b, i, j], x[slot, i, j, c])
+            return carry
+
+        lax.fori_loop(0, Z, part, 0)
+        y_copy(b).start()
+
+    def after_y(b):
+        y_copy(b).wait()
+
+        def part(i, carry):
+            r2[b, i] = add(r2[b, i], r1[b, i, y])
+            return carry
+
+        lax.fori_loop(0, Z, part, 0)
+
+    def hop(b, h):
+        @pl.when(z == h)
+        def _():
+            for d in range(Z - 1, h, -1):
+                if h > 0:
+                    right_copy(b, d, r2.at[b, d]).wait_recv()
+                    rr[b, d - 1] = add(rr[b, d - 1], r2[b, d])
+                right_copy(b, d, r2.at[b, d] if h == 0 else rr.at[b, d - 1]).start()
+
+        @pl.when(z == Z - 1 - h)
+        def _():
+            for d in range(Z - 1 - h):
+                if h > 0:
+                    left_copy(b, d, r2.at[b, d]).wait_recv()
+                    rl[b, d] = add(rl[b, d], r2[b, d])
+                left_copy(b, d, r2.at[b, d] if h == 0 else rl.at[b, d]).start()
+
+    def out_copies(b, slot):
+        kind, a, g = order[b]
+        src = ob.at[slot]
+        if kind == "filter":
+            return [pltpu.make_async_copy(src, filtO.at[a], osem.at[4 * slot])]
+        found = []
+        rows = pl.ds(g * 16, 16)
+        for k in range(4):
+            if a < 2:
+                dst = (downT, upO)[a].at[rows, pl.ds(k * D, D)]
+            elif k == 0:
+                dst = outO.at[rows]
+            else:
+                dst = inO.at[rows, pl.ds((k - 1) * D, D)]
+            found.append(pltpu.make_async_copy(src.at[pl.ds(16 * k, 16)], dst, osem.at[4 * slot + k]))
+        return found
+
+    def finish(b):
+        slot = b % 2
+        if b >= 2:
+            for copy in out_copies(b - 2, slot):
+                copy.wait()
+        for p in range(Z):
+
+            @pl.when(z == p)
+            def _(p=p):
+                total = r2[b, p].astype(f32)
+                if p > 0:
+                    right_copy(b, p, r2.at[b, p]).wait_recv()
+                    total += rr[b, p - 1].astype(f32)
+                if p < Z - 1:
+                    left_copy(b, p, r2.at[b, p]).wait_recv()
+                    total += rl[b, p].astype(f32)
+                ob[slot] = total
+                for d in range(p + 1, Z):
+                    right_copy(b, d, r2.at[b, d]).wait_send()
+                for d in range(p):
+                    left_copy(b, d, r2.at[b, d]).wait_send()
+
+        for copy in out_copies(b, slot):
+            copy.start()
+
+    def mini_copy(k):
+        return remote(mine.at[k], got.at[k], msem.at[0, k], msem.at[1, k], mates[k])
+
+    order = [("product", 0, g) for g in range(groups)] + [("filter", 0, 0)]
+    order += [("product", 1, g) for g in range(groups)] + [("filter", 1, 0)]
+    order += [("product", 2, g) for g in range(groups)]
+
+    for copy in loads(0):
+        copy.start()
+    tables_in = [load(back_h, back, 16), load(turned_h, turned, 17)]
+    tables_in[0].start()
+    tables_in[1].start()
+    for copy in spectra(0):
+        copy.start()
+    mine[0] = jnp.sum(small_in[...], axis=1)
+    mini_copy(0).start()
+
+    for i in range(n_blocks + 6):
+        if 0 <= i - 1 < n_blocks:
+            after_core(i - 1)
+        if 0 <= i - 2 < n_blocks:
+            after_y(i - 2)
+            hop(i - 2, 0)
+        if 0 <= i - 3 < n_blocks:
+            hop(i - 3, 1)
+        if 0 <= i - 4 < n_blocks:
+            hop(i - 4, 2)
+        if 0 <= i - 5 < n_blocks:
+            finish(i - 5)
+        if i < n_blocks:
+            kind, a, g = order[i]
+            slot = i % x.shape[0]
+            if kind == "product":
+                if g == 0:
+                    for copy in loads(a):
+                        copy.wait()
+                    turn(a)
+                    if a + 1 < 3:
+                        for copy in loads(a + 1):
+                            copy.start()
+                product(a, g, slot)
+            else:
+                if a == 0:
+                    tables_in[0].wait()
+                    tables_in[1].wait()
+                for copy in spectra(a):
+                    copy.wait()
+                filters(a, slot)
+                if a == 0:
+                    for copy in spectra(1):
+                        copy.start()
+            core_copy(i, slot).start()
+        if 2 <= i < 6:
+            k = i - 2
+            mini_copy(k).wait()
+            total = mine[k] + got[k]
+            if k < 3:
+                mine[k + 1] = total
+                mini_copy(k + 1).start()
+            else:
+                smallO[...] = total
+    for b in (n_blocks - 2, n_blocks - 1):
+        for copy in out_copies(b, b % 2):
+            copy.wait()
+
+
+def exchange_call(small, tabs, gdS, eS, nS, guS, ybS, goS, aS, gpS, s1S, g1S, s2S, g2S, ranks):
+    T, D = aS.shape
+    FF = eS.shape[1]
+    pieces = T // CH
+    per = D // ranks
+    groups = per // 16
+    blocks = 3 * groups + 2
+    Z, Y, rows = 4, 2, T // ranks
+    turned = (tabs[2][:, :CH].astype(f32) / CH).astype(bf16).T
+    V, S = pltpu.VMEM, pltpu.SemaphoreType.DMA
+    shard = (rows, D)
+    scratch = [
+        V((3, Z, Y, 2) + shard, bf16),
+        V((blocks, Z, Y) + shard, bf16),
+        V((blocks, Z) + shard, bf16),
+        V((blocks, Z - 1) + shard, bf16),
+        V((blocks, Z - 1) + shard, bf16),
+        V((2, T, FF), bf16),
+        V((2, T, D), bf16),
+        V((2, ranks, groups, 16, T), bf16),
+        V((2,) + s1S.shape, bf16),
+        V((pieces + 1, 2 * CH, D), bf16),
+        V((CH, 2 * CH), bf16),
+        V((CH, 2 * CH), bf16),
+        V((2,) + shard, f32),
+        V((4, small.shape[0], D), f32),
+        V((4, small.shape[0], D), f32),
+        S((18,)), S((8,)), S((2, blocks)), S((2, blocks)), S((2, blocks, Z - 1)), S((2, blocks, Z - 1)), S((2, 4)),
+    ]
+    out_shape = [
+        jax.ShapeDtypeStruct(s, f32)
+        for s in ((per, FF), (per, FF), (per, D), (per, 3 * D), (2, rows, D), (small.shape[0], D))
+    ]
+    return pl.pallas_call(
+        functools.partial(exchange_kernel, pieces),
+        out_shape=out_shape,
+        in_specs=[VM] + [ANY] * 14,
+        out_specs=[ANY] * 5 + [VM],
+        scratch_shapes=scratch,
+        compiler_params=pltpu.CompilerParams(vmem_limit_bytes=VMEM_LIMIT, collective_id=0, has_side_effects=True),
+        cost_estimate=pl.CostEstimate(flops=2 * T * 12 * D * D, bytes_accessed=40 << 20, transcendentals=0),
+        name="exchange",
+    )(small, tabs[1], turned, gdS, eS, nS, guS, ybS, goS, aS, gpS, s1S, g1S, s2S, g2S)
+
+
 def dot_rows(x, y):
     return lax.dot_general(x, y, (((0,), (0,)), ((), ())), preferred_element_type=f32).astype(bf16)
 
@@ -751,31 +1053,43 @@
     gdS, guS, goS, gpS, g1S, g2S, _, small = state
     token_grad = spread_rows(grads[2 * (count - 1) :][::-1], 0, T, count, rank)
 
-    slab = jnp.concatenate([dot_rows(gdS, eS), dot_rows(nS, guS), dot_rows(ybS, goS), dot_rows(aS, gpS)], axis=1)
-    taps = jnp.concatenate([filter_call(s1S, g1S, tabs), filter_call(s2S, g2S, tabs)], axis=1)
-    small = jnp.sum(small, axis=1)
-    per = D // ranks
-    mini = jnp.concatenate(
-        [small[:UPB].reshape(UPB, ranks, per).transpose(1, 0, 2).reshape(ranks, -1), small[UPB:].reshape(ranks, -1)], axis=1
-    )
-    scatter = lambda x: lax.psum_scatter(x, "dp", scatter_dimension=0, tiled=True).astype(f32)
-    slab, taps, mini = scatter(slab), scatter(taps), scatter(mini)[0]
-    head = mini[: UPB * per].reshape(UPB, per)
+    if ranks == 16 and D % (16 * ranks) == 0 and T == 64 * ranks and FF == 4 * D and pieces == 4:
+        downT, up, out, inn, taps, small = exchange_call(
+            small, tabs, gdS, eS, nS, guS, ybS, goS, aS, gpS, s1S, g1S, s2S, g2S, ranks
+        )
+        spot = lax.axis_index("dp")
+        per = D // ranks
+        head = lax.dynamic_slice_in_dim(small[:UPB], spot * per, per, 1)
+        up_bias_grad = lax.dynamic_slice_in_dim(small[UPB:].reshape(-1), spot * (FF // ranks), FF // ranks, 0)
+    else:
+        slab = jnp.concatenate([dot_rows(gdS, eS), dot_rows(nS, guS), dot_rows(ybS, goS), dot_rows(aS, gpS)], axis=1)
+        taps = jnp.concatenate([filter_call(s1S, g1S, tabs), filter_call(s2S, g2S, tabs)], axis=1)
+        small = jnp.sum(small, axis=1)
+        per = D // ranks
+        mini = jnp.concatenate(
+            [small[:UPB].reshape(UPB, ranks, per).transpose(1, 0, 2).reshape(ranks, -1), small[UPB:].reshape(ranks, -1)], axis=1
+        )
+        scatter = lambda x: lax.psum_scatter(x, "dp", scatter_dimension=0, tiled=True).astype(f32)
+        slab, taps, mini = scatter(slab), scatter(taps), scatter(mini)[0]
+        head = mini[: UPB * per].reshape(UPB, per)
+        up_bias_grad = mini[UPB * per :]
+        taps = taps.reshape(-1, 2, D).transpose(1, 0, 2)
+        downT, up, out, inn = (slab[:, i:j] for i, j in ((0, FF), (FF, 2 * FF), (2 * FF, 2 * FF + D), (2 * FF + D, None)))
     return (
         stream[None],
         token_grad[None],
         head[GAIN : GAIN + 2][None],
         head[SHIFT : SHIFT + 2][None],
-        slab[:, 2 * FF + D :][None],
+        inn[None],
         head[INB : INB + 3][None],
         head[TAP : TAP + 9].reshape(1, 3, 3, per),
-        taps.reshape(-1, 2, D).transpose(1, 0, 2)[None],
+        taps[None],
         head[SKIP : SKIP + 2][None],
-        slab[:, 2 * FF : 2 * FF + D][None],
+        out[None],
         head[OUTB][None],
-        slab[:, FF : 2 * FF][None],
-        mini[UPB * per :][None],
-        slab[:, :FF].T[None],
+        up[None],
+        up_bias_grad[None],
+        downT.T[None],
         head[DOWNB][None],
     )
 

time: 613 us -> 462 us (0.75)
  waiting for transfers between devices: 282 us -> 49.7 us
  Pallas kernels: 212 us -> 328 us
  matrix products: 19.1 us -> 0 us
  starting transfers between devices: 17.9 us -> 37 us
  other arithmetic: 31.3 us -> 13.3 us
  between operations: 14.8 us -> 1.57 us
    reduce_scatter x2 -> x0, waiting for transfers between devices: 204 us -> none  [body(): lax.psum_scatter(x, 'dp', scatter_dimension=0, tiled=True).astype(f32)]
    pallas_call x2 -> x1, Pallas kernels: 18.3 us -> 134 us  [exchange_call(): pl.pallas_call(functools.partial(exchange_kernel, pieces), out_shape=out_...]
    ppermute x2, starting transfers between devices: 7.04 us -> 26.6 us  [spread_rows(): lax.ppermute(rows.astype(bf16), 'section', [(source, r)]).astype(rows.dtype)]
    dot_general x4 -> x0, matrix products: 19.1 us -> none  [dot_rows(): lax.dot_general(x, y, (((0,), (0,)), ((), ())), preferred_element_type=f32)]
    concatenate x3 -> x0, other arithmetic: 15.4 us -> none  [the longest x1 10.7 us: body(): jnp.concatenate([dot_rows(gdS, eS), dot_rows(nS, guS), dot_rows(ybS, goS)...]
    ppermute x2, waiting for transfers between devices: 13 us -> 0.01 us  [spread_rows(): lax.ppermute(rows.astype(bf16), 'section', [(source, r)]).astype(rows.dtype)]
    unnamed x4 -> x0, waiting for transfers between devices: 9.3 us -> none
  transfers between devices with their start and end apart: 13 -> 10, of which waited for: 9 -> 3; matrix products, arithmetic and copies ran while one was open for 10% -> 5% of each run, Pallas kernels for 26% -> 66%
where the time goes in v2:
time: 462 us; the launch traced here: 454 us
  Pallas kernels  328 us (71%)
  waiting for transfers between devices  49.7 us (11%)
  starting transfers between devices  37 us (8%)
  local copies, waits for them, and re-layouts  24.6 us (5%)
  other arithmetic  13.3 us (3%)
    pallas_call x1, Pallas kernels, exchange_call(): pl.pallas_call(functools.partial(exchange_kernel, pieces), out_shape=out_...  134 us
    pallas_call x6, Pallas kernels, backward_call(): pl.pallas_call(functools.partial(backward_kernel, pieces, n_state), out_s...  104 us
    pallas_call x6, Pallas kernels, forward_call(): pl.pallas_call(functools.partial(forward_kernel, pieces, n_state), out_sh...  89.7 us
    ppermute x4, waiting for transfers between devices, body(): lax.ppermute(got[0], 'section', [(i + 1, i) for i in range(count - 1)])  42.7 us
    ppermute x2, starting transfers between devices, spread_rows(): lax.ppermute(rows.astype(bf16), 'section', [(source, r)]).astype(rows.dtype)  26.6 us
    unnamed x40, local copies, waits for them, and re-layouts  9.62 us
  transfers between devices with their start and end apart: 10, of which 3 were waited for; matrix products, arithmetic and copies ran while one was open for 5% of the time, Pallas kernels for 66%

profile of v2, /device:TPU:0, one launch (start us, length us, event | category | flops | bytes accessed | tf_op | source)
XLA Modules:
  0.0 454.1 jit_solution(8583220353603857819)
XLA Ops:
  0.7 0.7 reduce
  1.4 0.7 convert_element_type.31
  2.2 1.6 concatenate.18
  4.5 1.8 slice_bitcast_fusion.1.refs_1_
  6.8 17.4 %forward_chunk.6 = (bf16[256,768]{1,0:T(8,128)(2,1)}, bf16[1024,768]{1,0:T(8,128)(2,1)}, bf16[1024,768]{1,0:T(8,128)(2,1)}, bf16[1024,2304]{1,0:T(8,128)(2,1)}, ...) custom-call(s32[3]{0:T(128)} %get-tuple-element.350.info, ...), custom_call_target="tpu_custom_call" | custom-call | flops 3623878656 | bytes 31457280 | tf_op jit(solution)/shard_map/forward_chunk/pallas_call | solution.py:329
  24.3 1.3 collective-permute-start
  25.6 18.7 %forward_chunk.7 = (bf16[256,768]{1,0:T(8,128)(2,1)}, bf16[1024,768]{1,0:T(8,128)(2,1)}, bf16[1024,768]{1,0:T(8,128)(2,1)}, bf16[1024,2304]{1,0:T(8,128)(2,1)}, ...) custom-call(s32[3]{0:T(128)} %get-tuple-element.351.info, ...), custom_call_target="tpu_custom_call", output_to_operand_aliasing={{1}: (12, {}), {2}: (13, {}), {3}: (14, {}), {4}: (15, {}),... | custom-call | flops 3623878656 | bytes 31457280 | tf_op jit(solution)/shard_map/forward_chunk/pallas_call | solution.py:329
  44.3 1.3 collective-permute-start.2
  50.0 1.8 slice_bitcast_fusion.refs_1_
  52.4 0.7 copy-done.6
  53.1 20.0 %forward_chunk.8 = (bf16[256,768]{1,0:T(8,128)(2,1)}, bf16[1024,768]{1,0:T(8,128)(2,1)}, bf16[1024,768]{1,0:T(8,128)(2,1)}, bf16[1024,2304]{1,0:T(8,128)(2,1)}, ...) custom-call(s32[3]{0:T(128)} %add_add_fusion.1.info, ...), custom_call_target="tpu_custom_call", output_to_operand_aliasing={{1}: (12, {}), {2}: (13, {}), {3}: (14, {}), {4}: (15, {}),... | custom-call | flops 3623878656 | bytes 31457280 | tf_op jit(solution)/shard_map/forward_chunk/pallas_call | solution.py:329
  73.1 1.3 collective-permute-start.1
  75.1 22.4 %forward_chunk.9 = (bf16[256,768]{1,0:T(8,128)(2,1)}, bf16[1024,768]{1,0:T(8,128)(2,1)}, bf16[1024,768]{1,0:T(8,128)(2,1)}, bf16[1024,2304]{1,0:T(8,128)(2,1)}, ...) custom-call(s32[3]{0:T(128)} %add_add_fusion.4.info, ...), custom_call_target="tpu_custom_call", output_to_operand_aliasing={{1}: (12, {}), {2}: (13, {}), {3}: (14, {}), {4}: (15, {}),... | custom-call | flops 3623878656 | bytes 31457280 | tf_op jit(solution)/shard_map/forward_chunk/pallas_call | solution.py:329
  97.6 1.3 collective-permute-start.3
  99.5 0.7 copy-done.7
  100.2 1.3 forward_chunk.10
  101.5 6.9 %collective-permute-done.3.refs_1_ = bf16[256,768]{1,0:T(8,128)(2,1)S(1)} collective-permute-done((bf16[256,768]{1,0:T(8,128)(2,1)}, bf16[256,768]{1,0:T(8,128)(2,1)S(1)}, u32[]{:S(2)}, u32[]{:S(2)}) %collective-permute-start.3) | collective-permute-done | bytes 393248 | tf_op jit(solution)/shard_map/ppermute | solution.py:1037
  109.2 9.9 %forward_chunk.11 = (bf16[256,768]{1,0:T(8,128)(2,1)}, bf16[1024,768]{1,0:T(8,128)(2,1)}, bf16[1024,768]{1,0:T(8,128)(2,1)}, bf16[1024,2304]{1,0:T(8,128)(2,1)},...) custom-call(s32[3]{0:T(128)} %add_add_fusion.5.info, ...), custom_call_target="tpu_custom_call", output_to_operand_aliasing={{1}: (12, {}), {2}: (13, {}), {3}: (14, {}), {4}: (15, {}),... | custom-call | flops 3623878656 | bytes 31457280 | tf_op jit(solution)/shard_map/forward_chunk/pallas_call | solution.py:329
  119.1 1.3 backward_chunk.6
  120.4 1.3 collective-permute-start.6
  121.7 1.4 backward_chunk.7
  123.1 1.3 collective-permute-start.5
  124.5 1.3 collective-permute-start.4
  125.8 42.2 %collective-permute-done.6.refs_1_ = bf16[256,768]{1,0:T(8,128)(2,1)S(1)} collective-permute-done((bf16[256,768]{1,0:T(8,128)(2,1)}, bf16[256,768]{1,0:T(8,128)(2,1)S(1)}, u32[]{:S(2)}, u32[]{:S(2)}) %collective-permute-start.6) | collective-permute-done | bytes 393248 | tf_op jit(solution)/shard_map/ppermute | solution.py:1052
  168.0 0.7 copy-done.11
  168.8 23.3 %backward_chunk.8 = (bf16[256,768]{1,0:T(8,128)(2,1)}, f32[256,768]{1,0:T(8,128)}, bf16[1024,768]{1,0:T(8,128)(2,1)}, bf16[1024,3072]{1,0:T(8,128)(2,1)}, bf16[1...) custom-call(s32[3]{0:T(128)} %add_add_fusion.9.info, ...), custom_call_target="tpu_custom_call", output_to_operand_aliasing={{2}: (17, {}), {3}: (18, {}), {4}: (19, {}), {5}: (20, {}),... | custom-call | flops 3623878656 | bytes 31457280 | tf_op jit(solution)/shard_map/backward_chunk/pallas_call | solution.py:624
  192.0 1.2 convert.28
  193.2 1.3 collective-permute-start.9
  195.8 24.8 %backward_chunk.9 = (bf16[256,768]{1,0:T(8,128)(2,1)}, f32[256,768]{1,0:T(8,128)}, bf16[1024,768]{1,0:T(8,128)(2,1)}, bf16[1024,3072]{1,0:T(8,128)(2,1)}, bf16[1...) custom-call(s32[3]{0:T(128)} %add_add_fusion.6.info, ...), custom_call_target="tpu_custom_call", output_to_operand_aliasing={{2}: (17, {}), {3}: (18, {}), {4}: (19, {}), {5}: (20, {}),... | custom-call | flops 3623878656 | bytes 31457280 | tf_op jit(solution)/shard_map/backward_chunk/pallas_call | solution.py:624
  220.6 1.2 convert.27
  221.8 1.3 collective-permute-start.8
  223.2 25.3 %collective-permute-start.7 = (bf16[512,768]{1,0:T(8,128)(2,1)S(1)}, bf16[512,768]{1,0:T(8,128)(2,1)S(1)}, u32[]{:S(2)}, u32[]{:S(2)}) collective-permute-start(bf16[512,768]{1,0:T(8,128)(2,1)S(1)} %pad_maximum_fusion.1), channel_id=1, source_target_pairs={{0,1},{2,3},{4,5},{6,7},{8,9},{10,11},{12,13},{14,15},{16,17},{18,... | collective-permute-start | bytes 2359304 | tf_op jit(solution)/shard_map/ppermute | solution.py:1003
  248.5 2.1 fusion.1
  250.6 26.2 %backward_chunk.10 = (bf16[256,768]{1,0:T(8,128)(2,1)}, f32[256,768]{1,0:T(8,128)}, bf16[1024,768]{1,0:T(8,128)(2,1)}, bf16[1024,3072]{1,0:T(8,128)(2,1)}, bf16[...) custom-call(s32[3]{0:T(128)} %add_add_fusion.11.info, ...), custom_call_target="tpu_custom_call", output_to_operand_aliasing={{2}: (17, {}), {3}: (18, {}), {4}: (19, {}), {5}: (20, {}),... | custom-call | flops 3623878656 | bytes 31457280 | tf_op jit(solution)/shard_map/backward_chunk/pallas_call | solution.py:624
  277.5 26.8 %backward_chunk.11 = (bf16[256,768]{1,0:T(8,128)(2,1)}, f32[256,768]{1,0:T(8,128)}, bf16[1024,768]{1,0:T(8,128)(2,1)}, bf16[1024,3072]{1,0:T(8,128)(2,1)}, bf16[...) custom-call(s32[3]{0:T(128)} %add_add_fusion.10.info, ...), custom_call_target="tpu_custom_call", output_to_operand_aliasing={{2}: (17, {}), {3}: (18, {}), {4}: (19, {}), {5}: (20, {}),... | custom-call | flops 3623878656 | bytes 31457280 | tf_op jit(solution)/shard_map/backward_chunk/pallas_call | solution.py:624
  304.3 134.4 %exchange.1 = (f32[48,3072]{1,0:T(8,128)}, f32[48,3072]{1,0:T(8,128)}, f32[48,768]{1,0:T(8,128)}, f32[48,2304]{1,0:T(8,128)}, f32[2,64,768]{2,1,0:T(8,128)}, /*index=5*/f32[24,768]{1,0:T(8,128)}) custom-call(f32[24,8,768]{2,1,0:T(8,128)} %get-tuple-element.296.small_in, bf16[256,512]{1,0:T(8,128)(2,1)} %constant.38.clone.refs_8_.refs_7_.back_h, ...), custom_call_target="tpu_custom_call" | custom-call | flops 14495514624 | bytes 41943040 | tf_op jit(solution)/shard_map/exchange/pallas_call | solution.py:971
  438.8 0.8 slice.56
  439.6 0.8 dynamic-slice_bitcast_fusion
  440.9 1.4 dynamic-slice.3
  442.3 1.3 reshape.72
  444.2 1.4 dynamic_slice.7
  445.6 1.4 fusion.2
  447.0 1.4 dynamic-slice_bitcast_fusion.1
  448.4 1.3 fusion
  449.7 0.8 copy.262
  450.5 0.7 copy.263
  451.9 0.8 copy.265
  452.7 0.8 copy.266
  (56 shorter events, 12.3 us)
Async XLA Ops:
  24.3 28.1 %collective-permute-start = (bf16[256,768]{1,0:T(8,128)(2,1)}, bf16[256,768]{1,0:T(8,128)(2,1)S(1)}, u32[]{:S(2)}, u32[]{:S(2)}) collective-permute-start(bf16[256,768]{1,0:T(8,128)(2,1)} %get-tuple-element.165), channel_id=1, source_target_pairs={{0,1},{2,3},{4,5},{6,7},{8,9},{10,11},{12,13},{14,15},{16,17},{18,... | collective-permute-start | bytes 1179656 | tf_op jit(solution)/shard_map/ppermute | solution.py:1037
  44.3 30.1 %collective-permute-start.2 = (bf16[256,768]{1,0:T(8,128)(2,1)}, bf16[256,768]{1,0:T(8,128)(2,1)S(1)}, u32[]{:S(2)}, u32[]{:S(2)}) collective-permute-start(bf16[256,768]{1,0:T(8,128)(2,1)} %get-tuple-element.195), channel_id=1, source_target_pairs={{0,1},{2,3},{4,5},{6,7},{8,9},{10,11},{12,13},{14,15},{16,17},{18,... | collective-permute-start | bytes 1179656 | tf_op jit(solution)/shard_map/ppermute | solution.py:1037
  52.4 0.7 copy-start.6
  73.1 26.4 %collective-permute-start.1 = (bf16[256,768]{1,0:T(8,128)(2,1)}, bf16[256,768]{1,0:T(8,128)(2,1)S(1)}, u32[]{:S(2)}, u32[]{:S(2)}) collective-permute-start(bf16[256,768]{1,0:T(8,128)(2,1)} %get-tuple-element.194), channel_id=1, source_target_pairs={{0,1},{2,3},{4,5},{6,7},{8,9},{10,11},{12,13},{14,15},{16,17},{18,... | collective-permute-start | bytes 1179656 | tf_op jit(solution)/shard_map/ppermute | solution.py:1037
  74.4 0.7 copy-start.5
  97.6 10.9 %collective-permute-start.3 = (bf16[256,768]{1,0:T(8,128)(2,1)}, bf16[256,768]{1,0:T(8,128)(2,1)S(1)}, u32[]{:S(2)}, u32[]{:S(2)}) collective-permute-start(bf16[256,768]{1,0:T(8,128)(2,1)} %get-tuple-element.225), channel_id=1, source_target_pairs={{0,1},{2,3},{4,5},{6,7},{8,9},{10,11},{12,13},{14,15},{16,17},{18,... | collective-permute-start | bytes 1179656 | tf_op jit(solution)/shard_map/ppermute | solution.py:1037
  99.5 0.7 copy-start.7
  108.5 0.7 copy-start.8
  120.4 47.6 %collective-permute-start.6 = (bf16[256,768]{1,0:T(8,128)(2,1)}, bf16[256,768]{1,0:T(8,128)(2,1)S(1)}, u32[]{:S(2)}, u32[]{:S(2)}) collective-permute-start(bf16[256,768]{1,0:T(8,128)(2,1)} %get-tuple-element.257), channel_id=1, source_target_pairs={{1,0},{3,2},{5,4},{7,6},{9,8},{11,10},{13,12},{15,14},{17,16},{19,... | collective-permute-start | bytes 1179656 | tf_op jit(solution)/shard_map/ppermute | solution.py:1052
  121.7 2.7 copy-start.14
  121.7 2.7 copy-start.15
  123.1 71.9 %collective-permute-start.5 = (bf16[256,768]{1,0:T(8,128)(2,1)}, bf16[256,768]{1,0:T(8,128)(2,1)S(1)}, u32[]{:S(2)}, u32[]{:S(2)}) collective-permute-start(bf16[256,768]{1,0:T(8,128)(2,1)} %get-tuple-element.256), channel_id=1, source_target_pairs={{1,0},{3,2},{5,4},{7,6},{9,8},{11,10},{13,12},{15,14},{17,16},{19,... | collective-permute-start | bytes 1179656 | tf_op jit(solution)/shard_map/ppermute | solution.py:1052
  124.5 124.0 %collective-permute-start.4 = (bf16[512,768]{1,0:T(8,128)(2,1)S(1)}, bf16[512,768]{1,0:T(8,128)(2,1)S(1)}, u32[]{:S(2)}, u32[]{:S(2)}) collective-permute-start(bf16[512,768]{1,0:T(8,128)(2,1)S(1)} %pad_maximum_fusion), channel_id=1, source_target_pairs={{1,0},{3,2},{5,4},{7,6},{9,8},{11,10},{13,12},{15,14},{17,16},{19,... | collective-permute-start | bytes 2359304 | tf_op jit(solution)/shard_map/ppermute | solution.py:1003
  168.0 0.7 copy-start.11
  193.2 57.3 %collective-permute-start.9 = (bf16[256,768]{1,0:T(8,128)(2,1)}, bf16[256,768]{1,0:T(8,128)(2,1)}, u32[]{:S(2)}, u32[]{:S(2)}) collective-permute-start(bf16[256,768]{1,0:T(8,128)(2,1)} %get-tuple-element.277), channel_id=1, source_target_pairs={{1,0},{3,2},{5,4},{7,6},{9,8},{11,10},{13,12},{15,14},{17,16},{19,... | collective-permute-start | bytes 1179656 | tf_op jit(solution)/shard_map/ppermute | solution.py:1052
  195.0 0.7 copy-start.10
  195.8 52.7 %copy-start.12 = (bf16[256,768]{1,0:T(8,128)(2,1)S(1)}, bf16[256,768]{1,0:T(8,128)(2,1)}, u32[]{:S(2)}) copy-start(bf16[256,768]{1,0:T(8,128)(2,1)} %get-tuple-element.224) | copy-start | bytes 1179652
  221.8 55.0 %collective-permute-start.8 = (bf16[256,768]{1,0:T(8,128)(2,1)}, bf16[256,768]{1,0:T(8,128)(2,1)S(1)}, u32[]{:S(2)}, u32[]{:S(2)}) collective-permute-start(bf16[256,768]{1,0:T(8,128)(2,1)} %get-tuple-element.276), channel_id=1, source_target_pairs={{1,0},{3,2},{5,4},{7,6},{9,8},{11,10},{13,12},{15,14},{17,16},{19,... | collective-permute-start | bytes 1179656 | tf_op jit(solution)/shard_map/ppermute | solution.py:1052
  223.2 225.2 %collective-permute-start.7 = (bf16[512,768]{1,0:T(8,128)(2,1)S(1)}, bf16[512,768]{1,0:T(8,128)(2,1)S(1)}, u32[]{:S(2)}, u32[]{:S(2)}) collective-permute-start(bf16[512,768]{1,0:T(8,128)(2,1)S(1)} %pad_maximum_fusion.1), channel_id=1, source_target_pairs={{0,1},{2,3},{4,5},{6,7},{8,9},{10,11},{12,13},{14,15},{16,17},{18,... | collective-permute-start | bytes 2359304 | tf_op jit(solution)/shard_map/ppermute | solution.py:1003
  276.8 0.7 copy-start.9
  304.3 144.1 %copy-start = (f32[256,768]{1,0:T(8,128)S(1)}, f32[256,768]{1,0:T(8,128)}, u32[]{:S(2)}) copy-start(f32[256,768]{1,0:T(8,128)} %get-tuple-element.295) | copy-start | bytes 2359300
  304.3 144.1 %copy-start.1 = (f32[256,768]{1,0:T(8,128)S(1)}, f32[256,768]{1,0:T(8,128)}, u32[]{:S(2)}) copy-start(f32[256,768]{1,0:T(8,128)} %get-tuple-element.294) | copy-start | bytes 2359300
  438.8 11.8 %copy-start.13 = (f32[2,64,768]{2,1,0:T(8,128)S(1)}, f32[2,64,768]{2,1,0:T(8,128)}, u32[]{:S(2)}) copy-start(f32[2,64,768]{2,1,0:T(8,128)} %get-tuple-element.311) | copy-start | bytes 1179652
  444.2 5.5 %copy-start.4 = (f32[48,2304]{1,0:T(8,128)S(1)}, f32[48,2304]{1,0:T(8,128)}, u32[]{:S(2)}) copy-start(f32[48,2304]{1,0:T(8,128)} %get-tuple-element.310) | copy-start | bytes 1327108
  444.2 7.0 %copy-start.16 = (f32[48,768]{1,0:T(8,128)S(1)}, f32[48,768]{1,0:T(8,128)}, u32[]{:S(2)}) copy-start(f32[48,768]{1,0:T(8,128)} %get-tuple-element.312) | copy-start | bytes 442372
  444.2 7.7 %copy-start.3 = (f32[48,3072]{1,0:T(8,128)S(1)}, f32[48,3072]{1,0:T(8,128)}, u32[]{:S(2)}) copy-start(f32[48,3072]{1,0:T(8,128)} %get-tuple-element.313) | copy-start | bytes 1769476
  448.4 4.3 copy-start.2

commit v3 on v2

v3 whole, which is shorter than its diff:
```python
import functools
import math

import jax
import jax.numpy as jnp
import ml_dtypes
import numpy as np
from jax import lax
from jax.experimental import pallas as pl
from jax.experimental.pallas import tpu as pltpu
from jax.sharding import PartitionSpec as P

CH = 256
FT = 512
CARRY = 8
f32, bf16 = jnp.float32, jnp.bfloat16
VMEM_LIMIT = 60 * 1024 * 1024
ANY = pl.BlockSpec(memory_space=pl.ANY)
SMEM = pl.BlockSpec(memory_space=pltpu.SMEM)
VM = pl.BlockSpec(memory_space=pltpu.VMEM)

GAIN, SHIFT, INB, TAP, SKIP, OUTB, DOWNB, UPB = 0, 2, 4, 7, 16, 18, 19, 20


def tables():
    order = np.concatenate([np.arange(0, CH, 2), np.arange(1, CH, 2)])
    angle = np.pi * ((2 * order[:, None] + 1) * np.arange(CH)[None] % (4 * CH)) / (2 * CH)
    cos, sin = np.cos(angle), np.sin(angle)
    sign = np.where(order % 2 == 0, 1.0, -1.0)[:, None]
    spread = np.concatenate([cos, -sin], 0)
    turned = np.concatenate([sign * sin, sign * cos], 0)
    as_low = lambda t: jnp.asarray(t.astype(ml_dtypes.bfloat16))
    return as_low(spread), as_low(spread.T / CH), as_low(np.concatenate([turned, spread], 1))


def dot(x, y):
    return jnp.dot(x, y, preferred_element_type=f32)


def dot_nt(x, y):
    return lax.dot_general(x, y, (((1,), (1,)), ((), ())), preferred_element_type=f32)


def rows_at(index, size):
    return pl.ds(pl.multiple_of(index * size, size), size)


def for_rows(total, size, step):
    def run(i, carry):
        step(pl.multiple_of(i * size, size))
        return carry

    lax.fori_loop(0, total // size, run, 0)


def normalize(rows):
    average = jnp.mean(rows, axis=-1, keepdims=True)
    centered = rows - average
    scale = lax.rsqrt(jnp.mean(centered * centered, axis=-1, keepdims=True) + 1e-05)
    return centered * scale, scale


def norm_back(z, gain, unit, scale):
    w = z * gain
    return (
        w - jnp.mean(w, axis=-1, keepdims=True) - unit * jnp.mean(w * unit, axis=-1, keepdims=True)
    ) * scale


def gelu_pair(u):
    t = 1.0 / (1.0 + (0.3275911 * math.sqrt(0.5)) * jnp.abs(u))
    series = t * (
        0.5 * 0.254829592
        + t * (0.5 * -0.284496736 + t * (0.5 * 1.421413741 + t * (0.5 * -1.453152027 + t * (0.5 * 1.061405429))))
    )
    bell = jnp.exp(-0.5 * (u * u))
    tail = series * bell
    phi_sum = jnp.where(u >= 0, 1.0 - tail, tail)
    return u * phi_sum, phi_sum + u * (bell * (1.0 / math.sqrt(2.0 * math.pi)))


def mix_spectra(left, right, out, low, high, left_of, conj):
    width = out.shape[1] // 2

    def tile(i, carry):
        r = pl.multiple_of(i * 16, 16)
        for half in range(2):
            cols = slice(half * width, (half + 1) * width)

            def term(j, acc):
                k = left_of(j)
                ar = left[k, pl.ds(r, 16), cols].astype(f32)
                ai = left[k, pl.ds(CH + r, 16), cols].astype(f32)
                br = right[j, pl.ds(r, 16), cols].astype(f32)
                bi = right[j, pl.ds(CH + r, 16), cols].astype(f32)
                if conj:
                    return acc[0] + (ar * br + ai * bi), acc[1] + (ar * bi - ai * br)
                return acc[0] + (ar * br - ai * bi), acc[1] + (ar * bi + ai * br)

            zero = jnp.zeros((16, width), f32)
            real, imag = lax.fori_loop(low, high, term, (zero, zero))
            out[pl.ds(r, 16), cols] = real.astype(out.dtype)
            out[pl.ds(CH + r, 16), cols] = imag.astype(out.dtype)
        return carry

    lax.fori_loop(0, CH // 16, tile, 0)


def fold_rows(x):
    return jnp.sum(x.reshape(x.shape[0] // 8, 8, x.shape[1]), axis=0)


def pieces_of(at, wide, D):
    spans, off = [], 0
    while off < wide:
        row, col = (at + off) // D, (at + off) % D
        size = min(D - col, wide - off)
        spans.append((row, col, off, size))
        off += size
    return spans


def pass_kernel(
    sections, pieces, par, tokens, cots, filt, win, wout, wup, wdown, spread_h, back_h, pair_h,
    stream, gtok, aS, ybS, nS, eS, s1S, s2S, gdS, guS, goS, gpS, g1S, g2S, smallO,
    inf, inb, gin, winb, woutb, wupb, wdownb, spread, back, pair, k1, k2, sp1, sp2, pall, y1all, mall, dall,
    ab, lead, leadlow, spec, wide, gate2, mid, nb, tile2, hid, outb, outfb, gnb, gqb, gpb, small,
    wsem, osem, fsem, bsem, ssem, gsem,
):
    rank = lax.axis_index("section")
    first, final = rank == 0, rank == sections - 1
    D, FF = woutb.shape[0], wupb.shape[1]
    tiles = FF // FT
    T = pieces * CH
    share = T // sections
    sub = min(CH, share)
    at = lambda r: {"section": r}

    def when(condition):
        return pl.when(condition)

    def remote(src, dst, send, recv, r):
        return pltpu.make_async_remote_copy(
            src_ref=src, dst_ref=dst, send_sem=send, recv_sem=recv, device_id=at(r), device_id_type=pl.DeviceIdType.MESH
        )

    def local(src, dst, sem):
        return pltpu.make_async_copy(src, dst, sem)

    loads = [
        local(win, winb, wsem.at[0]),
        local(wout, woutb, wsem.at[1]),
        local(wup, wupb, wsem.at[2]),
        local(wdown, wdownb, wsem.at[3]),
        local(spread_h, spread, wsem.at[4]),
        local(back_h, back, wsem.at[5]),
        local(pair_h, pair, wsem.at[6]),
    ]
    fill = [local(filt.at[f, pl.ds(0, CH)], sp.at[0, pl.ds(CH, CH)], wsem.at[7 + f]) for f, sp in enumerate((sp1, sp2))]
    for seg in range(1, pieces):
        window = pl.ds((seg - 1) * CH, 2 * CH)
        fill += [local(filt.at[f, window], sp.at[seg], wsem.at[7 + 2 * seg + f]) for f, sp in enumerate((sp1, sp2))]

    def own_chunk(src, dst, seg, sems):
        return local(src.at[rows_at(seg, CH)], dst.at[seg], sems.at[1, seg])

    def relay(src, dst, seg, sems, r):
        return remote(src, dst.at[seg], sems.at[0, seg], sems.at[1, seg], r)

    @when(first)
    def _():
        for seg in range(pieces):
            own_chunk(tokens, inf, seg, fsem).start()

    loads[0].start()
    for copy in fill:
        copy.start()
    for k in (6, 4, 5, 1, 2, 3):
        loads[k].start()

    @when(final)
    def _():
        for seg in range(pieces):
            own_chunk(cots, inb, seg, bsem).start()

    barrier = pltpu.get_barrier_semaphore()
    for r in range(sections):

        @when(rank != r)
        def _(r=r):
            pl.semaphore_signal(barrier, inc=1, device_id=at(r), device_id_type=pl.DeviceIdType.MESH)

    pl.semaphore_wait(barrier, sections - 1)

    pall[pl.ds(0, 16), :] = jnp.zeros((16, 3 * D), bf16)
    for sp in (sp1, sp2):
        sp[0, pl.ds(0, CH), :] = jnp.zeros((CH, D), bf16)
    small[...] = jnp.zeros(small.shape, f32)
    gqb[pl.ds(CH, CARRY), :] = jnp.zeros((CARRY, 3 * D), f32)

    def filter_spectra(seg):
        k1[seg] = dot(pair[...], sp1[seg]).astype(bf16)
        k2[seg] = dot(pair[...], sp2[seg]).astype(bf16)

    @when(jnp.logical_not(first))
    def _():
        for copy in fill:
            copy.wait()
        loads[6].wait()

        def run(seg, carry):
            filter_spectra(seg)
            return carry

        lax.fori_loop(0, pieces, run, 0)

    def out_parts(seg, src, dst, sems, to_self):
        found = []
        for j in range(CH // sub):
            row = seg * CH + j * sub
            r, off = row // share, row % share
            found.append((r, off, src.at[pl.ds(j * sub, sub)], sems.at[0, seg * (CH // sub) + j], off // sub))
        return found

    def put(src, dst, k):
        return local(src, dst, osem.at[k])

    def forward_chunk(seg, carry):
        here = rows_at(seg, CH)
        base = pl.multiple_of(seg * CH, CH)
        hb = inf.at[seg]
        slot = 0
        later = seg > 0

        def before(copy):
            @when(later)
            def _():
                copy.wait()

        puts = [
            put(ab, aS.at[here], 0), put(sp1.at[seg], s1S.at[seg], 1), put(sp2.at[seg], s2S.at[seg], 2),
            put(leadlow, ybS.at[here], 3), put(nb, nS.at[here], 4), put(hid, eS.at[here], 5),
        ]

        @when(first)
        def _():
            own_chunk(tokens, inf, seg, fsem).wait()

        @when(jnp.logical_not(first))
        def _():
            relay(outb.at[slot], inf, seg, fsem, rank).wait_recv()

        before(puts[0])

        def ln1(r):
            unit, _ = normalize(hb[pl.ds(r, 64), :].astype(f32))
            ab[pl.ds(r, 64), :] = (unit * par[GAIN : GAIN + 1, :] + par[SHIFT : SHIFT + 1, :]).astype(bf16)

        for_rows(CH, 64, ln1)
        puts[0].start()

        @when(seg == 0)
        def _():
            loads[0].wait()

        for b in range(3):
            cols = slice(b * D, (b + 1) * D)
            value = dot(ab[...], winb[:, cols]) + par[INB + b : INB + b + 1, :]
            pall[pl.ds(pl.multiple_of(base + 16, 16), CH), cols] = value.astype(bf16)

        before(puts[3])

        def short(r):
            got = [branch(base + r, b)[0] for b in range(3)]
            gate2[pl.ds(r, 32), :] = got[2]
            s = got[0] * got[1]
            lead[pl.ds(r, 32), :] = s
            leadlow[pl.ds(r, 32), :] = s.astype(bf16)

        for_rows(CH, 32, short)

        @when(first)
        def _():
            @when(seg == 0)
            def _():
                for copy in fill:
                    copy.wait()
                loads[6].wait()

            filter_spectra(seg)

        @when(seg == 0)
        def _():
            loads[4].wait()
            loads[5].wait()

        sp1[seg] = dot(spread[...], leadlow[...]).astype(bf16)
        puts[1].start()
        mix_spectra(k1, sp1, spec, 0, seg + 1, lambda j: seg - j, False)
        wide[...] = dot(back[...], spec[...])

        def second(r):
            rows = pl.ds(r, 64)
            y = wide[rows, :] + par[SKIP : SKIP + 1, :] * lead[rows, :]
            y1all[seg, rows, :] = y.astype(bf16)
            trail = y * gate2[rows, :]
            lead[rows, :] = trail
            leadlow[rows, :] = trail.astype(bf16)

        for_rows(CH, 64, second)
        sp2[seg] = dot(spread[...], leadlow[...]).astype(bf16)
        puts[2].start()
        mix_spectra(k2, sp2, spec, 0, seg + 1, lambda j: seg - j, False)
        leadlow[...] = (dot(back[...], spec[...]) + par[SKIP + 1 : SKIP + 2, :] * lead[...]).astype(bf16)
        puts[3].start()

        @when(seg == 0)
        def _():
            loads[1].wait()

        wide[...] = dot(leadlow[...], woutb[...])
        before(puts[4])

        def ln2(r):
            rows = pl.ds(r, 64)
            m = hb[rows, :].astype(f32) + (wide[rows, :] + par[OUTB : OUTB + 1, :])
            mall[seg, rows, :] = m.astype(bf16)
            unit, _ = normalize(m)
            nb[rows, :] = (unit * par[GAIN + 1 : GAIN + 2, :] + par[SHIFT + 1 : SHIFT + 2, :]).astype(bf16)
            mid[rows, :] = m + par[DOWNB : DOWNB + 1, :]

        for_rows(CH, 64, ln2)
        puts[4].start()

        @when(seg == 0)
        def _():
            loads[2].wait()
            loads[3].wait()

        before(puts[5])

        def up(k):
            return dot(nb[...], wupb[:, k * FT : (k + 1) * FT])

        def act(k):
            spans = pieces_of(k * FT, FT, D)
            bias = [par[UPB + row : UPB + row + 1, col : col + size] for row, col, _, size in spans]
            bias = bias[0] if len(bias) == 1 else jnp.concatenate(bias, axis=1)
            e, d = gelu_pair(tile2[k % 2] + bias)
            hid[:, k * FT : (k + 1) * FT] = e.astype(bf16)
            dall[seg, :, k * FT : (k + 1) * FT] = d.astype(bf16)

        def down(k):
            mid[...] += dot(hid[:, k * FT : (k + 1) * FT], wdownb[k * FT : (k + 1) * FT, :])

        tile2[0] = up(0)
        for k in range(tiles):
            if k + 1 < tiles:
                tile2[(k + 1) % 2] = up(k + 1)
            act(k)
            if k >= 1:
                down(k - 1)
        down(tiles - 1)
        puts[5].start()

        @when(later)
        def _():
            finish_out(seg - 1, slot)

        outb[slot] = mid[...].astype(bf16)

        @when(jnp.logical_not(final))
        def _():
            relay(outb.at[slot], inf, seg, fsem, rank + 1).start()

        @when(final)
        def _():
            for r, off, src, sem, k in out_parts(seg, outb.at[slot], stream, ssem, None):

                @when(r != rank)
                def _():
                    remote(src, stream.at[pl.ds(pl.multiple_of(off, sub), sub)], sem, ssem.at[1, k], r).start()

                @when(r == rank)
                def _():
                    local(src, stream.at[pl.ds(pl.multiple_of(off, sub), sub)], sem).start()

        return carry

    def finish_out(seg, slot):
        @when(jnp.logical_not(final))
        def _():
            relay(outb.at[slot], inf, seg, fsem, rank + 1).wait_send()

        @when(final)
        def _():
            for r, off, src, sem, k in out_parts(seg, outb.at[slot], stream, ssem, None):

                @when(r != rank)
                def _():
                    remote(src, stream.at[pl.ds(pl.multiple_of(off, sub), sub)], sem, ssem.at[1, k], r).wait_send()

                @when(r == rank)
                def _():
                    local(src, stream.at[pl.ds(pl.multiple_of(off, sub), sub)], sem).wait()

    def branch(start, b):
        rows = pall[pl.ds(pl.multiple_of(start, 16), 48), b * D : (b + 1) * D].astype(f32)
        late = [rows[16 - i : 48 - i] for i in range(3)]
        t = [par[TAP + 3 * i + b : TAP + 3 * i + b + 1, :] for i in range(3)]
        return t[0] * late[0] + t[1] * late[1] + t[2] * late[2], late

    lax.fori_loop(0, pieces, forward_chunk, 0)
    last = pieces - 1
    here = rows_at(last, CH)
    for copy in (
        put(ab, aS.at[here], 0), put(sp1.at[last], s1S.at[last], 1), put(sp2.at[last], s2S.at[last], 2),
        put(leadlow, ybS.at[here], 3), put(nb, nS.at[here], 4), put(hid, eS.at[here], 5),
    ):
        copy.wait()
    for k in range(last):
        put(sp1.at[k], s1S.at[k], 1).wait()
        put(sp2.at[k], s2S.at[k], 2).wait()
    finish_out(last, 0)

    def add_small(k, x, cols=slice(None)):
        small[k, :, cols] += fold_rows(x)

    def backward_chunk(i, carry):
        seg = pieces - 1 - i
        here = rows_at(seg, CH)
        base = pl.multiple_of(seg * CH, CH)
        gdb, hb = inb.at[seg], inf.at[seg]
        slot = 0

        def before(copy):
            @when(i > 0)
            def _():
                copy.wait()

        puts = [
            put(gdb, gdS.at[here], 6), put(hid, guS.at[here], 7), put(nb, goS.at[here], 8), put(gpb, gpS.at[here], 9),
            put(sp2.at[seg], g2S.at[seg], 10), put(sp1.at[seg], g1S.at[seg], 11),
        ]

        @when(final)
        def _():
            own_chunk(cots, inb, seg, bsem).wait()

        @when(jnp.logical_not(final))
        def _():
            relay(outb.at[slot], inb, seg, bsem, rank).wait_recv()

        before(puts[0])
        puts[0].start()
        before(puts[1])

        def down(k):
            return dot_nt(gdb[...], wdownb[k * FT : (k + 1) * FT, :])

        def act(k):
            cols = slice(k * FT, (k + 1) * FT)
            gu = (dall[seg, :, cols].astype(f32) * tile2[k % 2]).astype(bf16)
            hid[:, cols] = gu
            total = fold_rows(gu.astype(f32))
            for row, col, off, size in pieces_of(k * FT, FT, D):
                small[UPB + row, :, col : col + size] += total[:, off : off + size]

        def up(k):
            part = dot_nt(hid[:, k * FT : (k + 1) * FT], wupb[:, k * FT : (k + 1) * FT])
            if k == 0:
                gnb[...] = part
            else:
                gnb[...] += part

        tile2[0] = down(0)
        for k in range(tiles):
            if k + 1 < tiles:
                tile2[(k + 1) % 2] = down(k + 1)
            act(k)
            if k >= 1:
                up(k - 1)
        up(tiles - 1)
        puts[1].start()
        before(puts[2])

        def ln2(r):
            rows = pl.ds(r, 32)
            unit, scale = normalize(mall[seg, rows, :].astype(f32))
            z = gnb[rows, :]
            gd = gdb[rows, :].astype(f32)
            gm = gd + norm_back(z, par[GAIN + 1 : GAIN + 2, :], unit, scale)
            mid[rows, :] = gm
            go = gm.astype(bf16)
            nb[rows, :] = go
            add_small(GAIN + 1, z * unit)
            add_small(SHIFT + 1, z)
            add_small(OUTB, go.astype(f32))
            add_small(DOWNB, gd)

        for_rows(CH, 32, ln2)
        puts[2].start()
        gy = dot_nt(nb[...], woutb[...])
        lead[...] = gy
        leadlow[...] = gy.astype(bf16)
        sp2[seg] = dot(spread[...], leadlow[...]).astype(bf16)
        puts[4].start()
        mix_spectra(k2, sp2, spec, seg, pieces, lambda j: j - seg, True)
        wide[...] = dot(back[...], spec[...])

        def keep(r, b, grad, late):
            gqb[pl.ds(r, 32), b * D : (b + 1) * D] = grad
            for tap in range(3):
                add_small(TAP + 3 * tap + b, grad * late[tap])

        def second(r):
            rows = pl.ds(r, 32)
            gate, late = branch(base + r, 2)
            y1 = y1all[seg, rows, :].astype(f32)
            gy2 = lead[rows, :]
            gs2 = wide[rows, :] + par[SKIP + 1 : SKIP + 2, :] * gy2
            gy1 = gs2 * gate
            gate2[rows, :] = gy1
            leadlow[rows, :] = gy1.astype(bf16)
            add_small(SKIP + 1, gy2 * (y1 * gate))
            keep(r, 2, gs2 * y1, late)

        for_rows(CH, 32, second)
        sp1[seg] = dot(spread[...], leadlow[...]).astype(bf16)
        puts[5].start()
        mix_spectra(k1, sp1, spec, seg, pieces, lambda j: j - seg, True)
        wide[...] = dot(back[...], spec[...])

        def lower(r):
            rows = pl.ds(r, 32)
            carrier, late_carrier = branch(base + r, 0)
            gate, late_gate = branch(base + r, 1)
            gy1 = gate2[rows, :]
            gs1 = wide[rows, :] + par[SKIP : SKIP + 1, :] * gy1
            add_small(SKIP, gy1 * (carrier * gate))
            keep(r, 0, gs1 * gate, late_carrier)
            keep(r, 1, gs1 * carrier, late_gate)

        for_rows(CH, 32, lower)
        before(puts[3])

        def short(r):
            for b in range(3):
                cols = slice(b * D, (b + 1) * D)
                rows = gqb[pl.ds(r, 32 + CARRY), cols]
                t = [par[TAP + 3 * tap + b : TAP + 3 * tap + b + 1, :] for tap in range(3)]
                gp = (t[0] * rows[:32] + t[1] * rows[1:33] + t[2] * rows[2:34]).astype(bf16)
                gpb[pl.ds(r, 32), cols] = gp
                add_small(INB + b, gp.astype(f32))

        for_rows(CH, 32, short)
        puts[3].start()
        gqb[pl.ds(CH, CARRY), :] = gqb[pl.ds(0, CARRY), :]
        gnb[...] = dot_nt(gpb[...], winb[...])

        @when(i > 0)
        def _():
            finish_grad(i - 1, slot)

        def ln1(r):
            rows = pl.ds(r, 32)
            unit, scale = normalize(hb[rows, :].astype(f32))
            z = gnb[rows, :]
            gh = mid[rows, :] + norm_back(z, par[GAIN : GAIN + 1, :], unit, scale)
            outfb[slot, rows, :] = gh
            outb[slot, rows, :] = gh.astype(bf16)
            add_small(GAIN, z * unit)
            add_small(SHIFT, z)

        for_rows(CH, 32, ln1)

        @when(jnp.logical_not(first))
        def _():
            relay(outb.at[slot], inb, seg, bsem, rank - 1).start()

        @when(first)
        def _():
            for r, off, src, sem, k in out_parts(seg, outb.at[slot], gtok, gsem, None):
                whole = outfb.at[slot, pl.ds(lax.rem(seg * CH + off, CH) if sub < CH else 0, sub)]

                @when(r != rank)
                def _():
                    remote(src, gin.at[k], sem, gsem.at[1, k], r).start()

                @when(r == rank)
                def _():
                    local(whole, gtok.at[pl.ds(pl.multiple_of(off, sub), sub)], sem).start()

        return carry

    def finish_grad(i, slot):
        seg = pieces - 1 - i

        @when(jnp.logical_not(first))
        def _():
            relay(outb.at[slot], inb, seg, bsem, rank - 1).wait_send()

        @when(first)
        def _():
            for r, off, src, sem, k in out_parts(seg, outb.at[slot], gtok, gsem, None):
                whole = outfb.at[slot, pl.ds(0, sub)]

                @when(r != rank)
                def _():
                    remote(src, gin.at[k], sem, gsem.at[1, k], r).wait_send()

                @when(r == rank)
                def _():
                    local(whole, gtok.at[pl.ds(pl.multiple_of(off, sub), sub)], sem).wait()

    lax.fori_loop(0, pieces, backward_chunk, 0)
    here = rows_at(0, CH)
    ends = [
        put(inb.at[0], gdS.at[here], 6), put(hid, guS.at[here], 7), put(nb, goS.at[here], 8), put(gpb, gpS.at[here], 9),
        put(sp2.at[0], g2S.at[0], 10), put(sp1.at[0], g1S.at[0], 11),
    ]
    for copy in ends:
        copy.wait()
    for k in range(last):
        ends[4].wait()
        ends[5].wait()
    total = put(small, smallO, 12)
    total.start()
    finish_grad(last, 0)
    parts = share // sub

    @when(jnp.logical_not(final))
    def _():
        for k in range(parts):
            remote(outb.at[0, pl.ds(0, sub)], stream.at[pl.ds(k * sub, sub)], ssem.at[0, 0], ssem.at[1, k], rank).wait_recv()

    @when(jnp.logical_not(first))
    def _():
        for k in range(parts):
            remote(outb.at[0, pl.ds(0, sub)], gin.at[k], gsem.at[0, 0], gsem.at[1, k], rank).wait_recv()
            outfb[0, pl.ds(0, sub), :] = gin[k].astype(f32)
            copy = local(outfb.at[0, pl.ds(0, sub)], gtok.at[pl.ds(k * sub, sub)], gsem.at[0, k])
            copy.start()
            copy.wait()

    total.wait()


def pass_call(par, tokens, cots, filt, win, wout, wup, wdown, tabs, sections):
    T, D = tokens.shape
    FF = wup.shape[1]
    pieces = T // CH
    share = T // sections
    sub = min(CH, share)
    spec3 = (pieces, 2 * CH, D)
    small = (UPB + FF // D, 8, D)
    shapes = [
        ((share, D), bf16), ((share, D), f32),
        ((T, D), bf16), ((T, D), bf16), ((T, D), bf16), ((T, FF), bf16), (spec3, bf16), (spec3, bf16),
        ((T, D), bf16), ((T, FF), bf16), ((T, D), bf16), ((T, 3 * D), bf16), (spec3, bf16), (spec3, bf16),
        (small, f32),
    ]
    V, S = pltpu.VMEM, pltpu.SemaphoreType.DMA
    chunk, chunks = (CH, D), (pieces, CH, D)
    scratch = [
        V(chunks, bf16), V(chunks, bf16), V((share // sub, sub, D), bf16),
        V(win.shape, bf16), V(wout.shape, bf16), V(wup.shape, bf16), V(wdown.shape, bf16),
        V((2 * CH, CH), bf16), V((CH, 2 * CH), bf16), V((2 * CH, 2 * CH), bf16),
        V(spec3, bf16), V(spec3, bf16), V(spec3, bf16), V(spec3, bf16),
        V((16 + T, 3 * D), bf16), V(chunks, bf16), V(chunks, bf16), V((pieces, CH, FF), bf16),
        V(chunk, bf16), V(chunk, f32), V(chunk, bf16), V((2 * CH, D), bf16), V(chunk, f32), V(chunk, f32), V(chunk, f32),
        V(chunk, bf16), V((2, CH, FT), f32), V((CH, FF), bf16), V((1,) + chunk, bf16), V((1,) + chunk, f32),
        V(chunk, f32), V((CH + CARRY, 3 * D), f32), V((CH, 3 * D), bf16), V(small, f32),
        S((7 + 2 * pieces,)), S((13,)), S((2, pieces)), S((2, pieces)), S((2, T // sub)), S((2, T // sub)),
    ]
    return pl.pallas_call(
        functools.partial(pass_kernel, sections, pieces),
        out_shape=[jax.ShapeDtypeStruct(*s) for s in shapes],
        in_specs=[VM] + [ANY] * 10,
        out_specs=[ANY] * len(shapes),
        scratch_shapes=scratch,
        compiler_params=pltpu.CompilerParams(vmem_limit_bytes=63 * 1024 * 1024, collective_id=1, has_side_effects=True),
        name="layer_pass",
    )(par, tokens, cots, filt, win, wout, wup, wdown, *tabs)


def filter_kernel(pieces, s, g, back, turned, out, q):
    width = s.shape[2] // 2

    for d in range(pieces):

        def tile(i, carry, d=d):
            r = pl.multiple_of(i * 16, 16)
            for half in range(2):
                cols = slice(half * width, (half + 1) * width)
                real = jnp.zeros((16, width), f32)
                imag = jnp.zeros((16, width), f32)
                for k in range(d, pieces):
                    ar = s[k - d, pl.ds(r, 16), cols].astype(f32)
                    ai = s[k - d, pl.ds(CH + r, 16), cols].astype(f32)
                    br = g[k, pl.ds(r, 16), cols].astype(f32)
                    bi = g[k, pl.ds(CH + r, 16), cols].astype(f32)
                    real = real + (ar * br + ai * bi)
                    imag = imag + (ar * bi - ai * br)
                q[d, pl.ds(r, 16), cols] = real.astype(bf16)
                q[d, pl.ds(CH + r, 16), cols] = imag.astype(bf16)
            return carry

        lax.fori_loop(0, CH // 16, tile, 0)
    for d in range(pieces):
        rows = dot(back[...], q[d])
        if d + 1 < pieces:
            rows += dot(turned[...], q[d + 1])
        out[pl.ds(d * CH, CH), :] = rows.astype(bf16)


def filter_call(s, g, tabs):
    pieces, _, D = s.shape
    turned = (tabs[2][:, :CH].astype(f32) / CH).astype(bf16).T
    return pl.pallas_call(
        functools.partial(filter_kernel, pieces),
        out_shape=jax.ShapeDtypeStruct((pieces * CH, D), bf16),
        in_specs=[VM] * 4,
        out_specs=VM,
        scratch_shapes=[pltpu.VMEM(s.shape, bf16)],
        compiler_params=pltpu.CompilerParams(vmem_limit_bytes=VMEM_LIMIT),
        name="filter_grad",
    )(s, g, tabs[1], turned)


def exchange_kernel(
    pieces, small_in, back_h, turned_h, gdS, eS, nS, guS, ybS, goS, aS, gpS, s1S, g1S, s2S, g2S,
    downT, upO, outO, inO, filtO, smallO,
    x, r1, r2, rr, rl, gb, lb, lt, sb, qb, back, turned, ob, mine, got, lsem, osem, csem, ysem, rsem, fsem, msem,
):
    D = lb.shape[2]
    me = lax.axis_index("dp")
    c, y, z = me % 2, (me // 2) % 2, me // 4
    Z = r2.shape[1]
    groups = lt.shape[2]
    n_blocks = 3 * groups + 2
    at = lambda i: {"dp": i}
    core_id, y_id = me + 1 - 2 * c, me + 2 - 4 * y
    mates = (core_id, y_id, me + 4 - 8 * (z % 2), me + 8 - 16 * (z // 2))
    inner = (z == 1) | (z == 2)

    barrier = pltpu.get_barrier_semaphore()
    for mate in mates:
        pl.semaphore_signal(barrier, inc=1, device_id=at(mate), device_id_type=pl.DeviceIdType.MESH)

    @pl.when(inner)
    def _():
        other = me + 12 - 8 * z
        pl.semaphore_signal(barrier, inc=1, device_id=at(other), device_id_type=pl.DeviceIdType.MESH)

    @pl.when(inner)
    def _():
        pl.semaphore_wait(barrier, len(mates) + 1)

    @pl.when(jnp.logical_not(inner))
    def _():
        pl.semaphore_wait(barrier, len(mates))

    def remote(src, dst, send, recv, mate):
        return pltpu.make_async_remote_copy(
            src_ref=src, dst_ref=dst, send_sem=send, recv_sem=recv, device_id=at(mate),
            device_id_type=pl.DeviceIdType.MESH,
        )

    def load(src, dst, k):
        return pltpu.make_async_copy(src, dst, lsem.at[k])

    rights = ((eS,), (guS,), (goS, gpS))
    lefts = ((gdS,), (nS,), (ybS, aS))

    def loads(m):
        found, off = [], 0
        for k, src in enumerate(rights[m]):
            wide = src.shape[1]
            found.append(load(src, gb.at[m % 2, :, pl.ds(off, wide)], 4 * m + k))
            off += wide
        for k, src in enumerate(lefts[m]):
            found.append(load(src, lb.at[k], 4 * m + 2 + k))
        return found

    def spectra(f):
        src = ((s1S, g1S), (s2S, g2S))[f]
        return [load(src[k], sb.at[k], 12 + 2 * f + k) for k in range(2)]

    def turn(m):
        for k in range(len(lefts[m])):

            def part(i, carry, k=k):
                rows = pl.multiple_of(i * 128, 128)
                piece = jnp.transpose(lb[k, pl.ds(rows, 128), :])
                lt[k, :, :, :, pl.ds(rows, 128)] = piece.reshape(lt.shape[1:4] + (128,))
                return carry

            lax.fori_loop(0, lb.shape[1] // 128, part, 0)

    def product(m, g, slot):
        def part(i, carry):
            k = jnp.minimum(i, 1) if m == 2 else 0
            left = lt[k, :, g].reshape(16 * lt.shape[1], lt.shape[4])
            cols = pl.ds(pl.multiple_of(i * D, D), D)
            value = dot(left, gb[m % 2, :, cols]).astype(bf16)
            x[slot, :, :, :, pl.ds(pl.multiple_of(i * 16, 16), 16), :] = value.reshape(x.shape[1:4] + (16, D))
            return carry

        lax.fori_loop(0, 4, part, 0)

    def filters(f, slot):
        def mix(d, carry):
            mix_spectra(sb.at[0], sb.at[1], qb.at[d], d, pieces, lambda j: j - d, True)
            return carry

        lax.fori_loop(0, pieces, mix, 0)
        qb[pieces] = jnp.zeros(qb.shape[1:], bf16)

        def part(d, carry):
            rows = dot(back[...], qb[d]) + dot(turned[...], qb[d + 1])
            x[slot, d] = rows.astype(bf16).reshape(x.shape[2:])
            return carry

        lax.fori_loop(0, pieces, part, 0)

    def core_copy(b, slot):
        return remote(x.at[slot, :, :, 1 - c], r1.at[b], csem.at[0, b], csem.at[1, b], core_id)

    def y_copy(b):
        return remote(r1.at[b, :, 1 - y], r2.at[b], ysem.at[0, b], ysem.at[1, b], y_id)

    def right_copy(b, d, src):
        return remote(src, rr.at[b, d - 1], rsem.at[0, b, d - 1], rsem.at[1, b, d - 1], me + 4)

    def left_copy(b, d, src):
        return remote(src, rl.at[b, d], fsem.at[0, b, d], fsem.at[1, b, d], me - 4)

    def add(p, q):
        return (p.astype(f32) + q.astype(f32)).astype(bf16)

    def after_core(b):
        slot = b % x.shape[0]
        core_copy(b, slot).wait()

        def part(i, carry):
            for j in range(2):
                r1[b, i, j] = add(r1[b, i, j], x[slot, i, j, c])
            return carry

        lax.fori_loop(0, Z, part, 0)
        y_copy(b).start()

    def after_y(b):
        y_copy(b).wait()

        def part(i, carry):
            r2[b, i] = add(r2[b, i], r1[b, i, y])
            return carry

        lax.fori_loop(0, Z, part, 0)

    def hop(b, h):
        @pl.when(z == h)
        def _():
            for d in range(Z - 1, h, -1):
                if h > 0:
                    right_copy(b, d, r2.at[b, d]).wait_recv()
                    rr[b, d - 1] = add(rr[b, d - 1], r2[b, d])
                right_copy(b, d, r2.at[b, d] if h == 0 else rr.at[b, d - 1]).start()

        @pl.when(z == Z - 1 - h)
        def _():
            for d in range(Z - 1 - h):
                if h > 0:
                    left_copy(b, d, r2.at[b, d]).wait_recv()
                    rl[b, d] = add(rl[b, d], r2[b, d])
                left_copy(b, d, r2.at[b, d] if h == 0 else rl.at[b, d]).start()

    def out_copies(b, slot):
        kind, a, g = order[b]
        src = ob.at[slot]
        if kind == "filter":
            return [pltpu.make_async_copy(src, filtO.at[a], osem.at[4 * slot])]
        found = []
        rows = pl.ds(g * 16, 16)
        for k in range(4):
            if a < 2:
                dst = (downT, upO)[a].at[rows, pl.ds(k * D, D)]
            elif k == 0:
                dst = outO.at[rows]
            else:
                dst = inO.at[rows, pl.ds((k - 1) * D, D)]
            found.append(pltpu.make_async_copy(src.at[pl.ds(16 * k, 16)], dst, osem.at[4 * slot + k]))
        return found

    def finish(b):
        slot = b % 2
        if b >= 2:
            for copy in out_copies(b - 2, slot):
                copy.wait()
        for p in range(Z):

            @pl.when(z == p)
            def _(p=p):
                total = r2[b, p].astype(f32)
                if p > 0:
                    right_copy(b, p, r2.at[b, p]).wait_recv()
                    total += rr[b, p - 1].astype(f32)
                if p < Z - 1:
                    left_copy(b, p, r2.at[b, p]).wait_recv()
                    total += rl[b, p].astype(f32)
                ob[slot] = total
                for d in range(p + 1, Z):
                    right_copy(b, d, r2.at[b, d]).wait_send()
                for d in range(p):
                    left_copy(b, d, r2.at[b, d]).wait_send()

        for copy in out_copies(b, slot):
            copy.start()

    def mini_copy(k):
        return remote(mine.at[k], got.at[k], msem.at[0, k], msem.at[1, k], mates[k])

    order = [("product", 0, g) for g in range(groups)] + [("filter", 0, 0)]
    order += [("product", 1, g) for g in range(groups)] + [("filter", 1, 0)]
    order += [("product", 2, g) for g in range(groups)]

    for copy in loads(0):
        copy.start()
    tables_in = [load(back_h, back, 16), load(turned_h, turned, 17)]
    tables_in[0].start()
    tables_in[1].start()
    for copy in spectra(0):
        copy.start()
    mine[0] = jnp.sum(small_in[...], axis=1)
    mini_copy(0).start()

    for i in range(n_blocks + 6):
        if 0 <= i - 1 < n_blocks:
            after_core(i - 1)
        if 0 <= i - 2 < n_blocks:
            after_y(i - 2)
            hop(i - 2, 0)
        if 0 <= i - 3 < n_blocks:
            hop(i - 3, 1)
        if 0 <= i - 4 < n_blocks:
            hop(i - 4, 2)
        if 0 <= i - 5 < n_blocks:
            finish(i - 5)
        if i < n_blocks:
            kind, a, g = order[i]
            slot = i % x.shape[0]
            if kind == "product":
                if g == 0:
                    for copy in loads(a):
                        copy.wait()
                    turn(a)
                    if a + 1 < 3:
                        for copy in loads(a + 1):
                            copy.start()
                product(a, g, slot)
            else:
                if a == 0:
                    tables_in[0].wait()
                    tables_in[1].wait()
                for copy in spectra(a):
                    copy.wait()
                filters(a, slot)
                if a == 0:
                    for copy in spectra(1):
                        copy.start()
            core_copy(i, slot).start()
        if 2 <= i < 6:
            k = i - 2
            mini_copy(k).wait()
            total = mine[k] + got[k]
            if k < 3:
                mine[k + 1] = total
                mini_copy(k + 1).start()
            else:
                smallO[...] = total
    for b in (n_blocks - 2, n_blocks - 1):
        for copy in out_copies(b, b % 2):
            copy.wait()


def exchange_call(small, tabs, gdS, eS, nS, guS, ybS, goS, aS, gpS, s1S, g1S, s2S, g2S, ranks):
    T, D = aS.shape
    FF = eS.shape[1]
    pieces = T // CH
    per = D // ranks
    groups = per // 16
    blocks = 3 * groups + 2
    Z, Y, rows = 4, 2, T // ranks
    turned = (tabs[2][:, :CH].astype(f32) / CH).astype(bf16).T
    V, S = pltpu.VMEM, pltpu.SemaphoreType.DMA
    shard = (rows, D)
    scratch = [
        V((3, Z, Y, 2) + shard, bf16),
        V((blocks, Z, Y) + shard, bf16),
        V((blocks, Z) + shard, bf16),
        V((blocks, Z - 1) + shard, bf16),
        V((blocks, Z - 1) + shard, bf16),
        V((2, T, FF), bf16),
        V((2, T, D), bf16),
        V((2, ranks, groups, 16, T), bf16),
        V((2,) + s1S.shape, bf16),
        V((pieces + 1, 2 * CH, D), bf16),
        V((CH, 2 * CH), bf16),
        V((CH, 2 * CH), bf16),
        V((2,) + shard, f32),
        V((4, small.shape[0], D), f32),
        V((4, small.shape[0], D), f32),
        S((18,)), S((8,)), S((2, blocks)), S((2, blocks)), S((2, blocks, Z - 1)), S((2, blocks, Z - 1)), S((2, 4)),
    ]
    out_shape = [
        jax.ShapeDtypeStruct(s, f32)
        for s in ((per, FF), (per, FF), (per, D), (per, 3 * D), (2, rows, D), (small.shape[0], D))
    ]
    return pl.pallas_call(
        functools.partial(exchange_kernel, pieces),
        out_shape=out_shape,
        in_specs=[VM] + [ANY] * 14,
        out_specs=[ANY] * 5 + [VM],
        scratch_shapes=scratch,
        compiler_params=pltpu.CompilerParams(vmem_limit_bytes=VMEM_LIMIT, collective_id=0, has_side_effects=True),
        cost_estimate=pl.CostEstimate(flops=2 * T * 12 * D * D, bytes_accessed=40 << 20, transcendentals=0),
        name="exchange",
    )(small, tabs[1], turned, gdS, eS, nS, guS, ybS, goS, aS, gpS, s1S, g1S, s2S, g2S)


def dot_rows(x, y):
    return lax.dot_general(x, y, (((0,), (0,)), ((), ())), preferred_element_type=f32).astype(bf16)


def body(
    tokens, cotangent, norm_gains, norm_shifts, in_weight, in_bias, short_taps, long_filter, skip_gains,
    out_weight, out_bias, up_weight, up_bias, down_weight, down_bias,
):
    count = lax.axis_size("section")
    ranks = lax.axis_size("dp")
    tok, cot = tokens[0], cotangent[0]
    T, D = tok.shape
    FF = up_weight.shape[2]
    pieces = T // CH
    tabs = tables()
    as_rows = lambda x: x[0].astype(f32).reshape(-1, D)
    par = jnp.concatenate(
        [as_rows(x) for x in (norm_gains, norm_shifts, in_bias, short_taps, skip_gains, out_bias, down_bias, up_bias)], 0
    )
    win, wout, wup, wdown, filt = in_weight[0], out_weight[0], up_weight[0], down_weight[0], long_filter[0]

    (stream, token_grad, aS, ybS, nS, eS, s1S, s2S, gdS, guS, goS, gpS, g1S, g2S, small) = pass_call(
        par, tok, cot, filt, win, wout, wup, wdown, tabs, count
    )
    if ranks == 16 and D % (16 * ranks) == 0 and T == 64 * ranks and FF == 4 * D and pieces == 4:
        downT, up, out, inn, taps, small = exchange_call(
            small, tabs, gdS, eS, nS, guS, ybS, goS, aS, gpS, s1S, g1S, s2S, g2S, ranks
        )
        spot = lax.axis_index("dp")
        per = D // ranks
        head = lax.dynamic_slice_in_dim(small[:UPB], spot * per, per, 1)
        up_bias_grad = lax.dynamic_slice_in_dim(small[UPB:].reshape(-1), spot * (FF // ranks), FF // ranks, 0)
    else:
        slab = jnp.concatenate([dot_rows(gdS, eS), dot_rows(nS, guS), dot_rows(ybS, goS), dot_rows(aS, gpS)], axis=1)
        taps = jnp.concatenate([filter_call(s1S, g1S, tabs), filter_call(s2S, g2S, tabs)], axis=1)
        small = jnp.sum(small, axis=1)
        per = D // ranks
        mini = jnp.concatenate(
            [small[:UPB].reshape(UPB, ranks, per).transpose(1, 0, 2).reshape(ranks, -1), small[UPB:].reshape(ranks, -1)], axis=1
        )
        scatter = lambda x: lax.psum_scatter(x, "dp", scatter_dimension=0, tiled=True).astype(f32)
        slab, taps, mini = scatter(slab), scatter(taps), scatter(mini)[0]
        head = mini[: UPB * per].reshape(UPB, per)
        up_bias_grad = mini[UPB * per :]
        taps = taps.reshape(-1, 2, D).transpose(1, 0, 2)
        downT, up, out, inn = (slab[:, i:j] for i, j in ((0, FF), (FF, 2 * FF), (2 * FF, 2 * FF + D), (2 * FF + D, None)))
    return (
        stream[None],
        token_grad[None],
        head[GAIN : GAIN + 2][None],
        head[SHIFT : SHIFT + 2][None],
        inn[None],
        head[INB : INB + 3][None],
        head[TAP : TAP + 9].reshape(1, 3, 3, per),
        taps[None],
        head[SKIP : SKIP + 2][None],
        out[None],
        head[OUTB][None],
        up[None],
        up_bias_grad[None],
        downT.T[None],
        head[DOWNB][None],
    )


def solution(mesh):
    whole = P("dp", None, None)
    split = lambda n: P("section", *([None] * n))
    return jax.shard_map(
        body,
        mesh=mesh,
        in_specs=(
            whole, whole, split(2), split(2), split(2), split(2), split(3), split(3), split(2), split(2), split(1),
            split(2), split(1), split(2), split(1),
        ),
        out_specs=(
            P("dp", "section", None),
            P("dp", "section", None),
            P("section", None, "dp"),
            P("section", None, "dp"),
            P("section", "dp", None),
            P("section", None, "dp"),
            P("section", None, None, "dp"),
            P("section", None, "dp", None),
            P("section", None, "dp"),
            P("section", "dp", None),
            P("section", "dp"),
            P("section", "dp", None),
            P("section", "dp"),
            P("section", None, "dp"),
            P("section", "dp"),
        ),
        check_vma=False,
    )
```

time: 462 us -> 344 us (0.74); the launches traced: 454 us -> 343 us
  waiting for transfers between devices: 49.7 us -> 0 us
  starting transfers between devices: 37 us -> 0 us
  other arithmetic: 13.3 us -> 1.39 us
  local copies, waits for them, and re-layouts: 24.6 us -> 15.2 us
    ppermute x10 -> x0, waiting for transfers between devices: 49.7 us -> none  [the longest x4 42.7 us: body(): lax.ppermute(got[0], 'section', [(i + 1, i) for i in range(count - 1)])]
    ppermute x10 -> x0, starting transfers between devices: 37 us -> none  [the longest x2 26.6 us: spread_rows(): lax.ppermute(rows.astype(bf16), 'section', [(source, r)]).astype(rows.dtype)]
    another operation x12 -> x0, other arithmetic: 8.45 us -> none  [the longest x10 6.1 us: body(): jnp.stack([jnp.clip(seg, 0, pieces - 1), active.astype(jnp.int32), (rank...]
    unnamed x40 -> x22, local copies, waits for them, and re-layouts: 9.62 us -> 6.41 us
    pallas_call x12 -> x1, Pallas kernels: 193 us -> 192 us  [pass_call(): pl.pallas_call(functools.partial(pass_kernel, sections, pieces), out_shap...]
  transfers between devices with their start and end apart: 10 -> 0, of which waited for: 3 -> 0; matrix products, arithmetic and copies ran while one was open for 5% -> 0% of each run, Pallas kernels for 66% -> 0%
where the time goes in v3:
time: 344 us; the launch traced here: 343 us
  Pallas kernels  326 us (95%)
  local copies, waits for them, and re-layouts  15.2 us (4%)
    pallas_call x1, Pallas kernels, pass_call(): pl.pallas_call(functools.partial(pass_kernel, sections, pieces), out_shap...  192 us
    pallas_call x1, Pallas kernels, exchange_call(): pl.pallas_call(functools.partial(exchange_kernel, pieces), out_shape=out_...  134 us

profile of v3, /device:TPU:0, one launch (start us, length us, event | category | flops | bytes accessed | tf_op | source)
XLA Modules:
  0.0 343.3 jit_solution(4527371215252079077)
XLA Ops:
  0.6 0.7 convert_element_type.39
  1.4 0.7 reduce
  2.2 1.6 concatenate.5
  3.8 0.6 concatenate.6.par
  4.4 192.2 %layer_pass.1 = (bf16[512,768]{1,0:T(8,128)(2,1)}, f32[512,768]{1,0:T(8,128)}, bf16[1024,768]{1,0:T(8,128)(2,1)}, bf16[1024,768]{1,0:T(8,128)(2,1)}, bf16[1024,7...) custom-call(f32[24,768]{1,0:T(8,128)} %concatenate.6.par, ...), custom_call_target="tpu_custom_call" | custom-call | tf_op jit(solution)/shard_map/layer_pass/pallas_call | solution.py:676
  196.6 0.0 copy-start.1
  196.6 0.0 copy-start
  196.7 133.8 %exchange.1 = (f32[48,3072]{1,0:T(8,128)}, f32[48,3072]{1,0:T(8,128)}, f32[48,768]{1,0:T(8,128)}, f32[48,2304]{1,0:T(8,128)}, f32[2,64,768]{2,1,0:T(8,128)}, /*index=5*/f32[24,768]{1,0:T(8,128)}) custom-call(f32[24,8,768]{2,1,0:T(8,128)} %get-tuple-element.38.small_in, bf16[256,512]{1,0:T(8,128)(2,1)} %constant.26.clone.back_h, ...), custom_call_target="tpu_custom_call" | custom-call | flops 14495514624 | bytes 41943040 | tf_op jit(solution)/shard_map/exchange/pallas_call | solution.py:1021
  330.5 0.0 copy-start.4
  330.5 0.0 copy-start.5
  330.5 1.5 dynamic-slice_bitcast_fusion.1
  332.0 0.8 dynamic-slice_bitcast_fusion
  332.7 0.6 copy.35
  333.3 0.8 dynamic-slice.3
  334.1 0.6 reshape.56
  334.7 1.4 fusion
  336.1 0.7 slice.38
  336.8 0.6 dynamic_slice.7
  337.5 0.0 copy-done.1
  337.5 0.0 copy-start.6
  337.5 0.0 copy-start.3
  337.5 0.9 copy.44
  338.4 0.0 copy-done
  338.4 0.0 copy-start.2
  338.4 1.1 copy.45
  339.5 0.0 copy-done.4
  339.5 0.8 copy.46
  340.3 0.0 copy-done.5
  340.3 0.7 copy.47
  341.0 0.0 copy-done.6
  341.0 0.7 copy.48
  341.7 0.0 copy-done.3
  341.7 0.8 copy.49
  342.5 0.0 copy-done.2
  342.5 0.8 copy.50
  (2 shorter events, 0.0 us)
Async XLA Ops:
  196.6 140.8 %copy-start.1 = (bf16[512,768]{1,0:T(8,128)(2,1)S(1)}, bf16[512,768]{1,0:T(8,128)(2,1)}, u32[]{:S(2)}) copy-start(bf16[512,768]{1,0:T(8,128)(2,1)} %get-tuple-element.36) | copy-start | bytes 2359300
  196.6 141.7 %copy-start = (f32[512,768]{1,0:T(8,128)S(1)}, f32[512,768]{1,0:T(8,128)}, u32[]{:S(2)}) copy-start(f32[512,768]{1,0:T(8,128)} %get-tuple-element.37) | copy-start | bytes 4718596
  330.5 9.0 %copy-start.4 = (f32[48,2304]{1,0:T(8,128)S(1)}, f32[48,2304]{1,0:T(8,128)}, u32[]{:S(2)}) copy-start(f32[48,2304]{1,0:T(8,128)} %get-tuple-element.52) | copy-start | bytes 1327108
  330.5 9.8 %copy-start.5 = (f32[2,64,768]{2,1,0:T(8,128)S(1)}, f32[2,64,768]{2,1,0:T(8,128)}, u32[]{:S(2)}) copy-start(f32[2,64,768]{2,1,0:T(8,128)} %get-tuple-element.53) | copy-start | bytes 1179652
  337.5 3.5 %copy-start.6 = (f32[48,768]{1,0:T(8,128)S(1)}, f32[48,768]{1,0:T(8,128)}, u32[]{:S(2)}) copy-start(f32[48,768]{1,0:T(8,128)} %get-tuple-element.54) | copy-start | bytes 442372
  337.5 4.2 %copy-start.3 = (f32[48,3072]{1,0:T(8,128)S(1)}, f32[48,3072]{1,0:T(8,128)}, u32[]{:S(2)}) copy-start(f32[48,3072]{1,0:T(8,128)} %get-tuple-element.55) | copy-start | bytes 1769476
  338.4 4.1 %copy-start.2 = (f32[48,3072]{1,0:T(8,128)S(1)}, f32[48,3072]{1,0:T(8,128)}, u32[]{:S(2)}) copy-start(f32[48,3072]{1,0:T(8,128)} %get-tuple-element.56) | copy-start | bytes 1769476
